TPU v7x, 32 devices: a whole 2x2x4 slice. The times are simulated.
32 devices in a mesh: ctx: 16 (over z, x, core), fsdp: 2 (over y).
Axes of the slice: x: 2, y: 2, z: 4, core: 2. Of those that a mesh axis runs over, the one named last changes fastest.
Arguments:
- streams: bfloat16 [3, 8192, 8192], P(None, ('ctx', 'fsdp')), may hold values from -6 to 6
- segments: int32 [8192], replicated, may hold values from 0 to 31, never falling along the last dimension, each value on 1 to 4096 neighbouring positions
- short_taps: float32 [3, 3, 8192], P(None, None, 'fsdp'), may hold values from -3 to 3
- decay_rates: float32 [512, 16], P('fsdp'), may hold values from 1.2207031e-05 to 0.1
- residues: float32 [512, 16], P('fsdp'), may hold values from -2 to 2
- skip_gain: float32 [8192], P('fsdp'), may hold values from -4 to 4
Outputs:
- output: bfloat16 [8192, 8192], P(('ctx', 'fsdp'))
Inputs may be any that keep to these rules, and one draw needn't show every extreme that they name: `segments`: never falling along the window; every document has 1 to 4096 tokens and one has exactly 4096.
All inputs are finite; a program needn't handle non-finite values.
Results may differ from a plain program's by a relative error of at most 0.0064.
Values may be sent and summed in bfloat16 or wider, within the bound.
No kernel may reach another device: no remote copies, remote signals or barrier semaphores. Data moves between devices by JAX's collectives and lax.ppermute only.
A program may use at most 192 MiB of HBM per device.

v0:
```python
import jax
import jax.numpy as jnp
from jax import lax
from jax.sharding import PartitionSpec as P

GROUP = 16
MODES = 16
SHORT = 3
SPAN = 8


def shifted_2(block, axis, distance):
    devices = range(lax.axis_size(axis))
    route = [(i - distance, i) for i in devices if i - distance in devices]
    return lax.ppermute(block, axis, route)


def contract(pattern, left_side, right_side):
    return jnp.einsum(pattern, left_side, right_side, precision=lax.Precision.HIGHEST)


def featurize(block_rows, before_rows, tap_rows, row_marks, before_marks):
    margin = before_rows.shape[1]
    row_count = block_rows.shape[1]
    joined = jnp.concatenate([before_rows, block_rows], axis=1)
    all_marks = jnp.concatenate([before_marks, row_marks])
    summed = block_rows.astype(jnp.float32) * tap_rows[:, 0][:, None, :]
    for offset in range(1, margin + 1):
        shifted = joined[:, margin - offset : margin - offset + row_count].astype(jnp.float32)
        agreeing = all_marks[margin - offset : margin - offset + row_count] == row_marks
        summed = (
            summed
            + jnp.where(agreeing[None, :, None], shifted, 0.0) * tap_rows[:, offset][:, None, :]
        )
    queries = summed[0].astype(jnp.bfloat16)
    gated_prod = (summed[1] * summed[2]).astype(jnp.bfloat16)
    return lax.optimization_barrier((queries, gated_prod))


def tile_filter(gated_prod, tile_marks, decay_rates, mode_gain, rising):
    tile_rows, channels = gated_prod.shape
    groups = channels // GROUP
    block_len = min(128, tile_rows)
    offsets = jnp.arange(block_len, dtype=jnp.float32)
    forward = mode_gain[:, :, None] * jnp.exp(-decay_rates[:, :, None] * offsets)
    backward = jnp.exp(decay_rates[:, :, None] * offsets)
    causal = (offsets[:, None] >= offsets[None, :]).astype(jnp.float32)
    kernel = contract("gmt,gms->gts", forward, backward) * causal
    mode_rates = decay_rates.T[:, :, None]
    closing = jnp.exp(-mode_rates * (block_len - 1.0 - offsets))
    through = jnp.exp(-mode_rates * block_len)
    head_rising = rising[:, :, :block_len]
    values = gated_prod.astype(jnp.float32).reshape(tile_rows, groups, GROUP)
    carried = jnp.zeros((MODES, groups, GROUP), jnp.float32)
    last_seen = jnp.int32(-1)
    pieces = []
    for number in range(tile_rows // block_len):
        block_vals = values[number * block_len : (number + 1) * block_len]
        block_marks = tile_marks[number * block_len : (number + 1) * block_len]
        agreeing = (block_marks[:, None] == block_marks[None, :]).astype(jnp.float32)
        inside = contract("gts,sgc->tgc", kernel * agreeing, block_vals)
        follow = (block_marks == last_seen).astype(jnp.float32)
        inside = inside + follow[:, None, None] * contract("mgt,mgc->tgc", head_rising, carried)
        ending = (block_marks == block_marks[block_len - 1]).astype(jnp.float32)
        fresh_state = contract("mgs,sgc->mgc", closing * ending, block_vals)
        passing = (block_marks[block_len - 1] == last_seen).astype(jnp.float32)
        carried = fresh_state + passing * through * carried
        last_seen = block_marks[block_len - 1]
        pieces.append(inside)
    return (jnp.concatenate(pieces, axis=0), carried)


def local(streams, segments, short_taps, decay_rates, residues, skip_gain):
    fsdp_count = lax.axis_size("fsdp")
    ctx_count = lax.axis_size("ctx")
    tile_index = lax.axis_index("ctx")
    own_rows = streams.shape[1]
    tile_rows = own_rows * fsdp_count
    margin = SHORT - 1
    padded_marks = jnp.concatenate([jnp.full((margin,), -1, jnp.int32), segments])
    tile_start = tile_index * tile_rows
    tile_marks = lax.dynamic_slice_in_dim(segments, tile_start, tile_rows)
    local_streams = lax.all_to_all(streams, "fsdp", split_axis=2, concat_axis=1, tiled=True)
    before_rows = shifted_2(local_streams[:, tile_rows - margin :, :], "ctx", 1)
    before_marks = lax.dynamic_slice_in_dim(padded_marks, tile_start, margin)
    queries, gated_prod = featurize(
        local_streams, before_rows, short_taps, tile_marks, before_marks
    )
    channels = gated_prod.shape[1]
    groups = channels // GROUP
    mode_gain = residues * jnp.sqrt(-jnp.expm1(-2.0 * decay_rates))
    positions = jnp.arange(tile_rows, dtype=jnp.float32)
    mode_rates = decay_rates.T[:, :, None]
    rising = mode_gain.T[:, :, None] * jnp.exp(-mode_rates * (positions + 1.0))
    local_part, end_state = tile_filter(gated_prod, tile_marks, decay_rates, mode_gain, rising)
    first_mark = tile_marks[0]
    falling = jnp.exp(-mode_rates * (tile_rows - 1.0 - positions))

    def source_state(operand):
        source_vals, source_marks = operand
        chosen = (source_marks == first_mark).astype(jnp.float32)
        return contract(
            "mgs,sgc->mgc",
            falling * chosen,
            source_vals.astype(jnp.float32).reshape(tile_rows, groups, GROUP),
        )

    def empty_state(operand):
        return jnp.zeros((MODES, groups, GROUP), jnp.float32)

    prior_state = jnp.zeros((MODES, groups, GROUP), jnp.float32)
    for distance in range(1, min(SPAN, ctx_count - 1) + 1):
        source_tile = shifted_2(gated_prod, "ctx", distance)
        source_index = tile_index - distance
        source_marks = lax.dynamic_slice_in_dim(
            segments, jnp.maximum(source_index, 0) * tile_rows, tile_rows
        )
        paired = (source_index >= 0) & (source_marks[tile_rows - 1] == first_mark)
        received = lax.cond(paired, source_state, empty_state, (source_tile, source_marks))
        prior_state = prior_state + jnp.exp(-mode_rates * ((distance - 1) * tile_rows)) * received
    prior_mark = first_mark.astype(jnp.float32)
    follow_tile = (tile_marks.astype(jnp.float32) == prior_mark).astype(jnp.float32)
    filtered = local_part + follow_tile[:, None, None] * contract(
        "mgt,mgc->tgc", rising, prior_state
    )
    mixed_out = (
        filtered.reshape(tile_rows, channels) + skip_gain * gated_prod.astype(jnp.float32)
    ).astype(jnp.bfloat16)
    mixed_out = lax.optimization_barrier(mixed_out)
    payload = (queries.astype(jnp.float32) * mixed_out.astype(jnp.float32)).astype(jnp.bfloat16)
    returned = lax.all_to_all(payload, "fsdp", split_axis=0, concat_axis=1, tiled=True)
    return returned


def solution(mesh):
    placed = (
        P(None, ("ctx", "fsdp"), None),
        P(),
        P(None, None, "fsdp"),
        P("fsdp", None),
        P("fsdp", None),
        P("fsdp"),
    )
    return jax.shard_map(
        local, mesh=mesh, in_specs=placed, out_specs=P(("ctx", "fsdp"), None), check_vma=False
    )
```

profile of v0, /device:TPU:16, one launch (start us, length us, event | category | flops | bytes accessed | tf_op | source)
XLA Modules:
  0.0 1401.9 jit_solution(10802754011798964845)
XLA Ops:
  0.0 25.0 %copy.80 = bf16[3,256,8192]{1,0,2:T(4,128)(2,1)} copy(bf16[3,256,8192]{2,1,0:T(8,128)(2,1)} %param.22) | data formatting | bytes 25165824 | tf_op args[0]
  25.0 10.0 all-to-all-start
  40.0 2.5 compare_convert_fusion.18
  44.6 6.9 multiply_exponential_fusion
  51.7 165.8 %all-to-all-done = bf16[3,256,8192]{1,0,2:T(4,128)(2,1)} async-done(((bf16[3,256,8192]{1,0,2:T(4,128)(2,1)}), bf16[3,256,8192]{1,0,2:T(4,128)(2,1)}, u32[]{:S(2)}, u32[]{:S(2)}) %all-to-all-start) | async-done | bytes 12582944 | tf_op jit(solution)/shard_map/all_to_all | solution.py:83
  217.5 24.9 %copy.81 = bf16[3,2,256,4096]{3,2,1,0:T(8,128)(2,1)} copy(bf16[3,2,256,4096]{2,0,3,1:T(4,128)(2,1)} %bitcast.17) | data formatting | bytes 25165824 | tf_op jit(solution)/shard_map/all_to_all | solution.py:83
  243.4 1.9 collective-permute-start
  268.4 28.0 %multiply_add_fusion = f32[3,512,4096]{2,1,0:T(8,128)} fusion(bf16[3,512,4096]{2,1,0:T(8,128)(2,1)} %bitcast.113, bf16[3,2,4096]{2,1,0:T(2,128)(2,1)S(1)} %collective-permute-done, f32[3,4096]{1,0:T(4,128)S(1)} %get-tuple-element.243, f32[3,4096]{1,0:T(4,128)S(1)} %get-tuple-element.244, f32[3,4096]{1,0:T(4,128)S(1)} %bitcast.132, ...), kind=kLoop, calls=%fused_computation.40 | loop fusion | flops 100663296 | bytes 37946368 | tf_op jit(solution)/shard_map/add | solution.py:32
  296.3 6.1 fusion.70
  302.4 8.4 fusion.71
  312.2 2.4 collective-permute-start.7
  314.5 3.8 collective-permute-start.6
  318.9 30.4 %fusion.95 = f32[256,128,128]{2,1,0:T(8,128)} fusion(f32[256,16]{1,0:T(8,128)S(1)} %copy.85, f32[256,16]{1,0:T(8,128)S(1)} %copy.84, f32[256,16]{1,0:T(8,128)S(1)} %copy.83), kind=kOutput, calls=%fused_computation.106 | convolution fusion | flops 806879232 | bytes 16826368 | tf_op jit(solution)/shard_map/gmt,gms->gts/dot_general | solution.py:19
  349.4 1.9 collective-permute-start.5
  351.3 2.1 collective-permute-start.4
  353.4 3.9 fusion.148
  360.2 2.3 copy.93
  362.5 2.7 fusion.93
  365.2 3.0 bitcast_add_fusion.2
  368.3 17.5 %fusion.54 = f32[256,16,128]{2,1,0:T(8,128)S(1)} fusion(bf16[128,256,16]{0,2,1:T(8,128)(2,1)S(1)} %bitcast.127, f32[256,128,128]{2,1,0:T(8,128)} %fusion.95, f32[128,128]{1,0:T(8,128)S(1)} %copy-done.14, f32[128,128]{1,0:T(8,128)S(1)} %fusion.143), kind=kOutput, calls=%fused_computation.47 | convolution fusion | flops 813694976 | bytes 20054016 | tf_op jit(solution)/shard_map/gts,sgc->tgc/dot_general | solution.py:19
  385.8 4.9 add_bitcast_fusion.3
  390.7 5.3 fusion.103
  396.0 10.9 collective-permute-done.8
  407.0 4.0 collective-permute-start.3
  411.0 86.9 %collective-permute-done.7 = bf16[512,4096]{1,0:T(8,128)(2,1)} collective-permute-done((bf16[512,4096]{1,0:T(8,128)(2,1)}, bf16[512,4096]{1,0:T(8,128)(2,1)}, u32[]{:S(2)}, u32[]{:S(2)}) %collective-permute-start.7) | collective-permute-done | bytes 4194336 | tf_op jit(solution)/shard_map/ppermute | solution.py:15
  497.9 50.8 %collective-permute-start.2 = (bf16[512,4096]{1,0:T(8,128)(2,1)}, bf16[512,4096]{1,0:T(8,128)(2,1)}, u32[]{:S(2)}, u32[]{:S(2)}) collective-permute-start(bf16[512,4096]{1,0:T(8,128)(2,1)} %fusion.71), channel_id=1, source_target_pairs={{0,4},{2,6},{4,8},{6,10},{8,12},{10,14},{12,16},{14,18},{16,20},{1... | collective-permute-start | bytes 12582920 | tf_op jit(solution)/shard_map/ppermute | solution.py:15
  548.7 77.1 %collective-permute-done.6 = bf16[512,4096]{1,0:T(8,128)(2,1)} collective-permute-done((bf16[512,4096]{1,0:T(8,128)(2,1)}, bf16[512,4096]{1,0:T(8,128)(2,1)}, u32[]{:S(2)}, u32[]{:S(2)}) %collective-permute-start.6) | collective-permute-done | bytes 4194336 | tf_op jit(solution)/shard_map/ppermute | solution.py:15
  625.8 105.3 %collective-permute-start.1 = (bf16[512,4096]{1,0:T(8,128)(2,1)}, bf16[512,4096]{1,0:T(8,128)(2,1)}, u32[]{:S(2)}, u32[]{:S(2)}) collective-permute-start(bf16[512,4096]{1,0:T(8,128)(2,1)} %fusion.71), channel_id=1, source_target_pairs={{0,2},{2,4},{4,6},{6,8},{8,10},{10,12},{12,14},{14,16},{16,18},{18... | collective-permute-start | bytes 12582920 | tf_op jit(solution)/shard_map/ppermute | solution.py:15
  731.2 2.0 fusion.89
  733.2 14.7 %fusion.50 = f32[256,16,128]{2,1,0:T(8,128)} fusion(bf16[128,256,16]{0,2,1:T(8,128)(2,1)S(1)} %bitcast.125, f32[256,128,128]{2,1,0:T(8,128)S(1)} %bitcast.111, f32[128,128]{1,0:T(8,128)S(1)} %copy-done.13, f32[128,128]{1,0:T(8,128)S(1)} %fusion.143), kind=kOutput, calls=%fused_computation.43 | convolution fusion | flops 813694976 | bytes 20054016 | tf_op jit(solution)/shard_map/gts,sgc->tgc/dot_general | solution.py:19
  748.0 5.8 add_bitcast_fusion.1
  753.8 5.4 fusion.72
  759.2 14.8 %add_bitcast_fusion.2 = f32[128,256,16]{0,2,1:T(8,128)} fusion(f32[256,16,128]{2,1,0:T(8,128)S(1)} %copy-done.1, bf16[128,256,16]{0,2,1:T(8,128)(2,1)S(1)} %bitcast.129, f32[256,128,128]{2,1,0:T(8,128)S(1)} %bitcast.111, f32[128,128]{1,0:T(8,128)S(1)} %copy-done.12, f32[128,128]{1,0:T(8,128)S(1)} %fusion.143, f32[128]{0:T(128)S(1)} %copy-done.40), kind=kOutput, calls=%fused_computation.101 | convolution fusion | flops 814743552 | bytes 22151680 | tf_op jit(solution)/shard_map/gts,sgc->tgc/dot_general | solution.py:19
  774.0 15.0 %add_bitcast_fusion = f32[128,256,16]{0,2,1:T(8,128)} fusion(f32[256,16,128]{2,1,0:T(8,128)S(1)} %copy-done.2, bf16[128,256,16]{0,2,1:T(8,128)(2,1)S(1)} %bitcast.131, f32[256,128,128]{2,1,0:T(8,128)S(1)} %bitcast.111, f32[128,128]{1,0:T(8,128)S(1)} %get-tuple-element.245, f32[128,128]{1,0:T(8,128)S(1)} %fusion.143, f32[128]{0:T(128)S(1)} %copy-done.39), kind=kOutput, calls=%fused_computation.94 | convolution fusion | flops 814743552 | bytes 22151680 | tf_op jit(solution)/shard_map/gts,sgc->tgc/dot_general | solution.py:19
  793.7 5.4 conditional.12
  799.1 102.7 %collective-permute-done.4 = bf16[512,4096]{1,0:T(8,128)(2,1)} collective-permute-done((bf16[512,4096]{1,0:T(8,128)(2,1)}, bf16[512,4096]{1,0:T(8,128)(2,1)}, u32[]{:S(2)}, u32[]{:S(2)}) %collective-permute-start.4) | collective-permute-done | bytes 4194336 | tf_op jit(solution)/shard_map/ppermute | solution.py:15
  902.0 44.8 %collective-permute-done.3 = bf16[512,4096]{1,0:T(8,128)(2,1)} collective-permute-done((bf16[512,4096]{1,0:T(8,128)(2,1)}, bf16[512,4096]{1,0:T(8,128)(2,1)}, u32[]{:S(2)}, u32[]{:S(2)}) %collective-permute-start.3) | collective-permute-done | bytes 4194336 | tf_op jit(solution)/shard_map/ppermute | solution.py:15
  948.7 313.8 %collective-permute-done.2 = bf16[512,4096]{1,0:T(8,128)(2,1)} collective-permute-done((bf16[512,4096]{1,0:T(8,128)(2,1)}, bf16[512,4096]{1,0:T(8,128)(2,1)}, u32[]{:S(2)}, u32[]{:S(2)}) %collective-permute-start.2) | collective-permute-done | bytes 4194336 | tf_op jit(solution)/shard_map/ppermute | solution.py:15
  1262.6 42.5 %collective-permute-done.1 = bf16[512,4096]{1,0:T(8,128)(2,1)} collective-permute-done((bf16[512,4096]{1,0:T(8,128)(2,1)}, bf16[512,4096]{1,0:T(8,128)(2,1)}, u32[]{:S(2)}, u32[]{:S(2)}) %collective-permute-start.1) | collective-permute-done | bytes 4194336 | tf_op jit(solution)/shard_map/ppermute | solution.py:15
  1305.2 18.2 %conditional.8 = (f32[16,256,16]{2,0,1:T(8,128)}) conditional(s32[]{:T(128)} %convert_element_type.190, () %tuple.55, (s32[]{:T(128)}, s32[512]{0:T(512)S(1)}, f32[16,256,512]{2,0,1:T(8,128)}, bf16[512,4096]{1,0:T(8,128)(2,1)}) %tuple.56), branch_computations={%region_0.1_spmd, %region_1.2_spmd} | conditional | flops 404751360 | bytes 21239820 | solution.py:119
  1305.4 6.7 copy.96
  1312.7 10.6 fusion.3
  1323.4 19.0 %maximum_add_fusion = f32[512,256,16]{0,2,1:T(8,128)} fusion(f32[128,256,16]{0,2,1:T(8,128)} %add_bitcast_fusion, f32[128,256,16]{0,2,1:T(8,128)} %add_bitcast_fusion.1, f32[128,256,16]{0,2,1:T(8,128)} %add_bitcast_fusion.2, f32[128,256,16]{0,2,1:T(8,128)S(1)} %copy-done.4, f32[512]{0:T(512)S(1)} %copy-done.44, f32[16,256,16]{2,0,1:T(8,128)} %copy-done.5, ...), kind=kOutput, calls=%fused_computation.60 | convolution fusion | flops 418316288 | bytes 19042304 | tf_op jit(solution)/shard_map/mgt,mgc->tgc/dot_general | solution.py:19
  1342.5 9.0 copy.112
  1351.5 6.1 add_convert_fusion
  1359.1 30.0 %all_to_all.37 = bf16[2,256,4096]{2,1,0:T(8,128)(2,1)} all-to-all(bf16[2,256,4096]{2,1,0:T(8,128)(2,1)S(1)} %bitcast.114), channel_id=1, replica_groups=mesh['ctx'=16,'fsdp'=2] {'fsdp'}, dimensions={0} | all-to-all | bytes 8388608 | tf_op jit(solution)/shard_map/all_to_all | solution.py:131
  1389.1 6.3 copy.113
  1395.4 6.3 copy.114
  (162 shorter events, 36.0 us)
Async XLA Ops:
  25.0 10.0 copy-start.25
  25.0 11.5 copy-start.15
  25.0 11.5 copy-start.27
  25.0 192.5 %all-to-all-start = ((bf16[3,256,8192]{1,0,2:T(4,128)(2,1)}), bf16[3,256,8192]{1,0,2:T(4,128)(2,1)}, u32[]{:S(2)}, u32[]{:S(2)}) async-start(bf16[3,256,8192]{1,0,2:T(4,128)(2,1)} %copy.80), calls=%async_computation | async-start | bytes 33554432 | tf_op jit(solution)/shard_map/all_to_all | solution.py:83
  35.1 212.2 %copy-start.36 = (s32[512]{0:T(512)}, s32[512]{0:T(512)S(1)}, u32[]{:S(2)}) copy-start(s32[512]{0:T(512)S(1)} %get-tuple-element.209) | copy-start | bytes 6148
  35.1 214.1 %copy-start.34 = (s32[512]{0:T(512)}, s32[512]{0:T(512)S(1)}, u32[]{:S(2)}) copy-start(s32[512]{0:T(512)S(1)} %get-tuple-element.210) | copy-start | bytes 6148
  35.1 216.0 %copy-start.32 = (s32[512]{0:T(512)}, s32[512]{0:T(512)S(1)}, u32[]{:S(2)}) copy-start(s32[512]{0:T(512)S(1)} %get-tuple-element.203) | copy-start | bytes 6148
  35.1 217.8 %copy-start.30 = (s32[512]{0:T(512)}, s32[512]{0:T(512)S(1)}, u32[]{:S(2)}) copy-start(s32[512]{0:T(512)S(1)} %get-tuple-element.204) | copy-start | bytes 6148
  35.1 219.7 %copy-start.28 = (s32[512]{0:T(512)}, s32[512]{0:T(512)S(1)}, u32[]{:S(2)}) copy-start(s32[512]{0:T(512)S(1)} %get-tuple-element.205) | copy-start | bytes 6148
  39.8 11.7 copy-start.9
  44.6 7.0 copy-start.24
  243.4 25.0 %collective-permute-start = (bf16[3,2,4096]{2,1,0:T(2,128)(2,1)S(1)}, bf16[3,2,4096]{2,1,0:T(2,128)(2,1)S(1)}, u32[]{:S(2)}, u32[]{:S(2)}) collective-permute-start(bf16[3,2,4096]{2,1,0:T(2,128)(2,1)S(1)} %slice.154), channel_id=1, source_target_pairs={{0,2},{2,4},{4,6},{6,8},{8,10},{10,12},{12,14},{14,16},{16,18},{18... | collective-permute-start | bytes 147464 | tf_op jit(solution)/shard_map/ppermute | solution.py:15
  310.9 96.1 %collective-permute-start.8 = (bf16[512,4096]{1,0:T(8,128)(2,1)}, bf16[512,4096]{1,0:T(8,128)(2,1)}, u32[]{:S(2)}, u32[]{:S(2)}) collective-permute-start(bf16[512,4096]{1,0:T(8,128)(2,1)} %fusion.71), channel_id=1, source_target_pairs={{0,16},{2,18},{4,20},{6,22},{8,24},{10,26},{12,28},{14,30},{1,17},... | collective-permute-start | bytes 12582920 | tf_op jit(solution)/shard_map/ppermute | solution.py:15
  312.2 185.7 %collective-permute-start.7 = (bf16[512,4096]{1,0:T(8,128)(2,1)}, bf16[512,4096]{1,0:T(8,128)(2,1)}, u32[]{:S(2)}, u32[]{:S(2)}) collective-permute-start(bf16[512,4096]{1,0:T(8,128)(2,1)} %fusion.71), channel_id=1, source_target_pairs={{0,14},{2,16},{4,18},{6,20},{8,22},{10,24},{12,26},{14,28},{16,30}... | collective-permute-start | bytes 12582920 | tf_op jit(solution)/shard_map/ppermute | solution.py:15
  314.5 311.3 %collective-permute-start.6 = (bf16[512,4096]{1,0:T(8,128)(2,1)}, bf16[512,4096]{1,0:T(8,128)(2,1)}, u32[]{:S(2)}, u32[]{:S(2)}) collective-permute-start(bf16[512,4096]{1,0:T(8,128)(2,1)} %fusion.71), channel_id=1, source_target_pairs={{0,12},{2,14},{4,16},{6,18},{8,20},{10,22},{12,24},{14,26},{16,28}... | collective-permute-start | bytes 12582920 | tf_op jit(solution)/shard_map/ppermute | solution.py:15
  349.4 443.0 %collective-permute-start.5 = (bf16[512,4096]{1,0:T(8,128)(2,1)}, bf16[512,4096]{1,0:T(8,128)(2,1)}, u32[]{:S(2)}, u32[]{:S(2)}) collective-permute-start(bf16[512,4096]{1,0:T(8,128)(2,1)} %fusion.71), channel_id=1, source_target_pairs={{0,10},{2,12},{4,14},{6,16},{8,18},{10,20},{12,22},{14,24},{16,26}... | collective-permute-start | bytes 12582920 | tf_op jit(solution)/shard_map/ppermute | solution.py:15
  351.3 550.5 %collective-permute-start.4 = (bf16[512,4096]{1,0:T(8,128)(2,1)}, bf16[512,4096]{1,0:T(8,128)(2,1)}, u32[]{:S(2)}, u32[]{:S(2)}) collective-permute-start(bf16[512,4096]{1,0:T(8,128)(2,1)} %fusion.71), channel_id=1, source_target_pairs={{0,8},{2,10},{4,12},{6,14},{8,16},{10,18},{12,20},{14,22},{16,24},... | collective-permute-start | bytes 12582920 | tf_op jit(solution)/shard_map/ppermute | solution.py:15
  368.2 17.5 %copy-start.43 = (f32[128]{0:T(128)S(1)}, f32[128]{0:T(128)}, u32[]{:S(2)}) copy-start(f32[128]{0:T(128)} %get-tuple-element.232) | copy-start | bytes 1540
  368.3 364.9 %slice-start = ((s8[16777216]{0:T(1024)(128)(4,1)}), s8[4194304]{0:T(1024)(128)(4,1)S(1)}, s32[]{:S(2)}) async-start(s8[16777216]{0:T(1024)(128)(4,1)} %bitcast.110), calls=%async_computation.2 | async-start | bytes 8388608
  368.3 364.9 %slice-start.1 = ((s8[16777216]{0:T(1024)(128)(4,1)}), s8[4194304]{0:T(1024)(128)(4,1)S(1)}, s32[]{:S(2)}) async-start(s8[16777216]{0:T(1024)(128)(4,1)} %bitcast.110), calls=%async_computation.3 | async-start | bytes 8388608
  368.3 364.9 %slice-start.2 = ((s8[16777216]{0:T(1024)(128)(4,1)}), s8[4194304]{0:T(1024)(128)(4,1)S(1)}, s32[]{:S(2)}) async-start(s8[16777216]{0:T(1024)(128)(4,1)} %bitcast.110), calls=%async_computation.4 | async-start | bytes 8388608
  390.7 340.5 %copy-start.38 = (f32[128]{0:T(128)S(1)}, f32[128]{0:T(128)}, u32[]{:S(2)}) copy-start(f32[128]{0:T(128)} %iota_subtract_fusion.1) | copy-start | bytes 1540
  390.7 340.5 %copy-start.42 = (f32[128]{0:T(128)S(1)}, f32[128]{0:T(128)}, u32[]{:S(2)}) copy-start(f32[128]{0:T(128)} %get-tuple-element.236) | copy-start | bytes 1540
  390.7 342.5 %slice-start.3 = ((s8[16777216]{0:T(1024)(128)(4,1)}), s8[4194304]{0:T(1024)(128)(4,1)S(1)}, s32[]{:S(2)}) async-start(s8[16777216]{0:T(1024)(128)(4,1)} %bitcast.110), calls=%async_computation.5 | async-start | bytes 8388608
  390.7 342.5 %copy-start.13 = (f32[128,128]{1,0:T(8,128)S(1)}, f32[128,128]{1,0:T(8,128)}, u32[]{:S(2)}) copy-start(f32[128,128]{1,0:T(8,128)} %get-tuple-element.247) | copy-start | bytes 196612
  407.0 539.9 %collective-permute-start.3 = (bf16[512,4096]{1,0:T(8,128)(2,1)}, bf16[512,4096]{1,0:T(8,128)(2,1)}, u32[]{:S(2)}, u32[]{:S(2)}) collective-permute-start(bf16[512,4096]{1,0:T(8,128)(2,1)} %fusion.71), channel_id=1, source_target_pairs={{0,6},{2,8},{4,10},{6,12},{8,14},{10,16},{12,18},{14,20},{16,22},{... | collective-permute-start | bytes 12582920 | tf_op jit(solution)/shard_map/ppermute | solution.py:15
  497.9 764.5 %collective-permute-start.2 = (bf16[512,4096]{1,0:T(8,128)(2,1)}, bf16[512,4096]{1,0:T(8,128)(2,1)}, u32[]{:S(2)}, u32[]{:S(2)}) collective-permute-start(bf16[512,4096]{1,0:T(8,128)(2,1)} %fusion.71), channel_id=1, source_target_pairs={{0,4},{2,6},{4,8},{6,10},{8,12},{10,14},{12,16},{14,18},{16,20},{1... | collective-permute-start | bytes 12582920 | tf_op jit(solution)/shard_map/ppermute | solution.py:15
  625.8 679.3 %collective-permute-start.1 = (bf16[512,4096]{1,0:T(8,128)(2,1)}, bf16[512,4096]{1,0:T(8,128)(2,1)}, u32[]{:S(2)}, u32[]{:S(2)}) collective-permute-start(bf16[512,4096]{1,0:T(8,128)(2,1)} %fusion.71), channel_id=1, source_target_pairs={{0,2},{2,4},{4,6},{6,8},{8,10},{10,12},{12,14},{14,16},{16,18},{18... | collective-permute-start | bytes 12582920 | tf_op jit(solution)/shard_map/ppermute | solution.py:15
  733.2 14.7 %copy-start.41 = (f32[128]{0:T(128)S(1)}, f32[128]{0:T(128)}, u32[]{:S(2)}) copy-start(f32[128]{0:T(128)} %get-tuple-element.237) | copy-start | bytes 1540
  759.2 14.8 %copy-start.2 = (f32[256,16,128]{2,1,0:T(8,128)S(1)}, f32[256,16,128]{2,1,0:T(8,128)}, u32[]{:S(2)}) copy-start(f32[256,16,128]{2,1,0:T(8,128)} %fusion.72) | copy-start | bytes 6291460
  759.2 14.8 %copy-start.3 = (bf16[128,4096]{0,1:T(8,128)(2,1)S(1)}, bf16[128,4096]{0,1:T(8,128)(2,1)}, u32[]{:S(2)}) copy-start(bf16[128,4096]{0,1:T(8,128)(2,1)} %copy.93) | copy-start | bytes 3145732
  759.2 14.8 %copy-start.39 = (f32[128]{0:T(128)S(1)}, f32[128]{0:T(128)}, u32[]{:S(2)}) copy-start(f32[128]{0:T(128)} %get-tuple-element.238) | copy-start | bytes 1540
  774.0 15.0 %copy-start.37 = (s32[512]{0:T(512)S(1)}, s32[512]{0:T(512)}, u32[]{:S(2)}) copy-start(s32[512]{0:T(512)} %copy-done.36) | copy-start | bytes 6148
  792.8 109.1 %copy-start.29 = (s32[512]{0:T(512)S(1)}, s32[512]{0:T(512)}, u32[]{:S(2)}) copy-start(s32[512]{0:T(512)} %copy-done.28) | copy-start | bytes 6148
  902.0 44.9 %copy-start.7 = (f32[16,256,16]{2,0,1:T(8,128)}, f32[16,256,16]{2,0,1:T(8,128)S(1)}, u32[]{:S(2)}) copy-start(f32[16,256,16]{2,0,1:T(8,128)S(1)} %get-tuple-element.252) | copy-start | bytes 786436
  1262.6 42.5 %copy-start.8 = (f32[16,256,16]{2,0,1:T(8,128)}, f32[16,256,16]{2,0,1:T(8,128)S(1)}, u32[]{:S(2)}) copy-start(f32[16,256,16]{2,0,1:T(8,128)S(1)} %get-tuple-element.250) | copy-start | bytes 786436
  1305.1 18.3 %copy-start.4 = (f32[128,256,16]{0,2,1:T(8,128)S(1)}, f32[128,256,16]{0,2,1:T(8,128)}, u32[]{:S(2)}) copy-start(f32[128,256,16]{0,2,1:T(8,128)} %add_bitcast_fusion.3) | copy-start | bytes 6291460
  1305.1 18.3 %copy-start.10 = (f32[16,256]{0,1:T(8,128)S(1)}, f32[16,256]{0,1:T(8,128)}, u32[]{:S(2)}) copy-start(f32[16,256]{0,1:T(8,128)} %copy-done.9) | copy-start | bytes 49156
  1305.1 18.3 %copy-start.16 = (f32[16,256]{0,1:T(8,128)S(1)}, f32[16,256]{0,1:T(8,128)}, u32[]{:S(2)}) copy-start(f32[16,256]{0,1:T(8,128)} %copy.109) | copy-start | bytes 49156
  1305.1 18.3 %copy-start.17 = (f32[16,256]{0,1:T(8,128)S(1)}, f32[16,256]{0,1:T(8,128)}, u32[]{:S(2)}) copy-start(f32[16,256]{0,1:T(8,128)} %copy.107) | copy-start | bytes 49156
  1305.1 18.3 %copy-start.18 = (f32[16,256]{0,1:T(8,128)S(1)}, f32[16,256]{0,1:T(8,128)}, u32[]{:S(2)}) copy-start(f32[16,256]{0,1:T(8,128)} %copy.105) | copy-start | bytes 49156
  1305.1 18.3 %copy-start.19 = (f32[16,256]{0,1:T(8,128)S(1)}, f32[16,256]{0,1:T(8,128)}, u32[]{:S(2)}) copy-start(f32[16,256]{0,1:T(8,128)} %copy.103) | copy-start | bytes 49156
  1305.1 18.3 %copy-start.20 = (f32[16,256]{0,1:T(8,128)S(1)}, f32[16,256]{0,1:T(8,128)}, u32[]{:S(2)}) copy-start(f32[16,256]{0,1:T(8,128)} %copy.101) | copy-start | bytes 49156
  1305.2 18.3 %copy-start.21 = (f32[16,256]{0,1:T(8,128)S(1)}, f32[16,256]{0,1:T(8,128)}, u32[]{:S(2)}) copy-start(f32[16,256]{0,1:T(8,128)} %copy.99) | copy-start | bytes 49156
  1305.2 18.3 %copy-start.22 = (f32[16,256]{0,1:T(8,128)S(1)}, f32[16,256]{0,1:T(8,128)}, u32[]{:S(2)}) copy-start(f32[16,256]{0,1:T(8,128)} %copy.97) | copy-start | bytes 49156
  1305.2 18.3 %copy-start.23 = (f32[16,256]{0,1:T(8,128)S(1)}, f32[16,256]{0,1:T(8,128)}, u32[]{:S(2)}) copy-start(f32[16,256]{0,1:T(8,128)} %copy.95) | copy-start | bytes 49156
  1305.2 18.3 %copy-start.44 = (f32[512]{0:T(512)S(1)}, f32[512]{0:T(512)}, u32[]{:S(2)}) copy-start(f32[512]{0:T(512)} %get-tuple-element.227) | copy-start | bytes 6148
  1342.5 9.0 copy-start.26
  (11 other events, 40.4 us)
where the time goes:
time: 1410 us; the launch traced here: 1400 us
  waiting for transfers between devices  844 us (60%)
  starting transfers between devices  183 us (13%)
  matrix products  151 us (11%)
  local copies, waits for them, and re-layouts  116 us (8%)
  other arithmetic  56.9 us (4%)
  blocking collectives  30 us (2%)
  between operations  15.1 us (1%)
    ppermute x9, waiting for transfers between devices, shifted_2(): return lax.ppermute(block, axis, route)  679 us
    ppermute x9, starting transfers between devices, shifted_2(): return lax.ppermute(block, axis, route)  174 us
    all_to_all x1, waiting for transfers between devices, local(): lax.all_to_all(streams, 'fsdp', split_axis=2, concat_axis=1, tiled=True)  166 us
    dot_general x14, matrix products, contract(): jnp.einsum(pattern, left_side, right_side, precision=lax.Precision.HIGHEST)  151 us
    all_to_all x1, blocking collectives, local(): lax.all_to_all(payload, 'fsdp', split_axis=0, concat_axis=1, tiled=True)  30 us
  transfers between devices with their start and end apart: 10, of which 8 were waited for; matrix products, arithmetic and copies ran while one was open for 12% of the time, Pallas kernels for 0%

commit v1 on v0

--- a/solution.py
+++ b/solution.py
@@ -1,11 +1,296 @@
+import functools
+
 import jax
 import jax.numpy as jnp
 from jax import lax
+from jax.experimental import pallas as pl
+from jax.experimental.pallas import tpu as pltpu
 from jax.sharding import PartitionSpec as P
 
 GROUP = 16
 MODES = 16
 SHORT = 3
+LANES = 128
+TILE_GROUPS = LANES // GROUP
+F32 = jnp.float32
+BF16 = jnp.bfloat16
+VMEM_BYTES = 48 * 1024 * 1024
+
+
+def mark_rows(marks_ref, before_ref, block):
+    marks = marks_ref[0].astype(F32)
+    before = jnp.where(block > 0, before_ref[0], -1).astype(F32)
+    lane = lax.broadcasted_iota(jnp.int32, marks.shape, 1)
+    rows = [marks]
+    for offset in range(1, SHORT):
+        rows.append(
+            jnp.where(
+                lane < offset, pltpu.roll(before, offset, 1), pltpu.roll(marks, offset, 1)
+            )
+        )
+    return rows
+
+
+def as_column(row):
+    return jnp.transpose(jnp.broadcast_to(row, (LANES, row.shape[1])))
+
+
+def featured(x_ref, stream, lanes, halo, taps, agree_refs, row_block):
+    rows = x_ref.shape[1]
+    for start in range(0, rows, row_block):
+        if start == 0:
+            here = x_ref[stream, 0:row_block, lanes].astype(F32)
+            sub = lax.broadcasted_iota(jnp.int32, (8, LANES), 0)
+            ahead = jnp.where(sub == 6, halo[0:1], jnp.where(sub == 7, halo[1:2], 0.0))
+        else:
+            both = x_ref[stream, start - 16 : start + row_block, lanes].astype(F32)
+            here, ahead = both[16:], both[8:16]
+        joined = jnp.concatenate([ahead, here], axis=0)
+        span = slice(start, start + row_block)
+        summed = here * taps[0:1]
+        for offset in range(1, SHORT):
+            shifted = pltpu.roll(joined, offset, 0)[8:]
+            summed = summed + shifted * agree_refs[offset - 1, span, :] * taps[offset : offset + 1]
+        yield span, summed
+
+
+def set_agree(agree_ref, rows):
+    mark = as_column(rows[0])
+    for offset in range(1, SHORT):
+        agree_ref[offset - 1] = jnp.where(mark == as_column(rows[offset]), 1.0, 0.0)
+
+
+def state_kernel(
+    block_ref, x_ref, halo_ref, pack_ref, marks_ref, before_ref,
+    gated_ref, state_ref, rates_ref, agree_ref, last_ref,
+):
+    tokens = x_ref.shape[1]
+
+    @pl.when(pl.program_id(0) == 0)
+    def _():
+        rows = mark_rows(marks_ref, before_ref, block_ref[0])
+        set_agree(agree_ref, rows)
+        last = rows[0][:, tokens - 1 :]
+        last_ref[...] = jnp.broadcast_to(jnp.where(rows[0] == last, 1.0, 0.0), last_ref.shape)
+
+    @pl.loop(0, x_ref.shape[2] // LANES)
+    def _(tile):
+        lanes = pl.ds(pl.multiple_of(tile * LANES, LANES), LANES)
+        key_halo = halo_ref[1, :, lanes].astype(F32)
+        value_halo = halo_ref[2, :, lanes].astype(F32)
+        keys = featured(x_ref, 0, lanes, key_halo, pack_ref[3:6, lanes], agree_ref, 64)
+        values = featured(x_ref, 1, lanes, value_halo, pack_ref[6:9, lanes], agree_ref, 64)
+        for (span, key), (_, value) in zip(keys, values):
+            gated_ref[span, lanes] = (key * value).astype(BF16)
+        rate_row = pack_ref[10:11, lanes]
+        rate = as_column(rate_row)
+        rate = jnp.concatenate([rate] * (tokens // LANES), axis=1)
+        left = (tokens - 1) - lax.broadcasted_iota(jnp.int32, rate.shape, 1)
+        falling = jnp.exp(-rate * left.astype(F32)) * last_ref[0:1, :]
+        full = jnp.dot(
+            falling.astype(BF16), gated_ref[:, lanes], preferred_element_type=F32
+        )
+        own = lax.broadcasted_iota(jnp.int32, (MODES, LANES), 1) // GROUP
+        state = jnp.zeros((MODES, LANES), F32)
+        for group in range(TILE_GROUPS):
+            state = jnp.where(own == group, full[group * MODES : (group + 1) * MODES], state)
+        state_ref[:, lanes] = state.astype(BF16)
+        mode = lax.broadcasted_iota(jnp.int32, (MODES, LANES), 0)
+        rates_ref[:, lanes] = jnp.take_along_axis(
+            jnp.broadcast_to(rate_row, (MODES, LANES)), own * GROUP + mode, axis=1
+        )
+
+
+def local_kernel(
+    block_ref, gated_ref, pack_ref, marks_ref, before_ref, *rest
+):
+    out_ref, causal_ref = rest[-2:]
+    tokens = gated_ref.shape[0]
+
+    @pl.when(pl.program_id(0) == 0)
+    def _():
+        row = marks_ref[0].astype(F32)
+        column = as_column(row)
+        column = jnp.concatenate([column] * (tokens // LANES), axis=1)
+        later = lax.broadcasted_iota(jnp.int32, column.shape, 0)
+        earlier = lax.broadcasted_iota(jnp.int32, column.shape, 1)
+        causal_ref[...] = jnp.where((column == row) & (later >= earlier), 1.0, 0.0).astype(BF16)
+
+    @pl.loop(0, gated_ref.shape[1] // LANES)
+    def _(tile):
+        lanes = pl.ds(pl.multiple_of(tile * LANES, LANES), LANES)
+        rate = as_column(pack_ref[10:11, lanes])
+        gain = as_column(pack_ref[11:12, lanes])
+        rate = jnp.concatenate([rate] * (tokens // LANES), axis=1)
+        gain = jnp.concatenate([gain] * (tokens // LANES), axis=1)
+        left = (tokens - 1) - lax.broadcasted_iota(jnp.int32, rate.shape, 1)
+        terms = gain * jnp.exp(-rate * left.astype(F32))
+        taps = jnp.sum(terms.reshape(TILE_GROUPS, MODES, tokens), axis=1)
+        own = lax.broadcasted_iota(jnp.int32, (1, LANES), 1) // GROUP
+        half = tokens // 2
+        upper = jnp.zeros((half, LANES), F32)
+        lower = jnp.zeros((half, LANES), F32)
+        for group in range(TILE_GROUPS):
+            base = pltpu.roll(
+                jnp.broadcast_to(taps[group : group + 1], (8, tokens)),
+                1, 1, stride=1, stride_axis=0,
+            )
+            pieces = [base] + [pltpu.roll(base, 8 * i, 1) for i in range(1, half // 8)]
+            top = jnp.concatenate(pieces, axis=0).astype(BF16)
+            bottom = jnp.concatenate([top[:, half:], top[:, :half]], axis=1)
+            top = top[:, :half] * causal_ref[:half, :half]
+            bottom = bottom * causal_ref[half:, :]
+            upper = jnp.where(
+                own == group,
+                jnp.dot(top, gated_ref[:half, lanes], preferred_element_type=F32),
+                upper,
+            )
+            lower = jnp.where(
+                own == group,
+                jnp.dot(bottom, gated_ref[:, lanes], preferred_element_type=F32),
+                lower,
+            )
+        skip = pack_ref[9:10, lanes]
+        out_ref[:half, lanes] = upper + skip * gated_ref[:half, lanes].astype(F32)
+        out_ref[half:, lanes] = lower + skip * gated_ref[half:, lanes].astype(F32)
+
+
+def output_kernel(
+    block_ref, x_ref, halo_ref, pack_ref, marks_ref, before_ref, local_ref, carry_ref,
+    out_ref, agree_ref, follow_ref,
+):
+    tokens = x_ref.shape[1]
+
+    @pl.when(pl.program_id(0) == 0)
+    def _():
+        rows = mark_rows(marks_ref, before_ref, block_ref[0])
+        set_agree(agree_ref, rows)
+        follow_ref[...] = as_column(jnp.where(rows[0] == rows[1][:, 0:1], 1.0, 0.0))
+
+    @pl.loop(0, x_ref.shape[2] // LANES)
+    def _(tile):
+        lanes = pl.ds(pl.multiple_of(tile * LANES, LANES), LANES)
+        own = lax.broadcasted_iota(jnp.int32, (MODES, LANES), 1) // GROUP
+        mode = lax.broadcasted_iota(jnp.int32, (MODES, LANES), 0)
+        gain = jnp.take_along_axis(
+            jnp.broadcast_to(pack_ref[11:12, lanes], (MODES, LANES)), own * GROUP + mode, axis=1
+        )
+        scaled = gain * carry_ref[:, lanes].astype(F32)
+        spread = jnp.concatenate(
+            [jnp.where(own == group, scaled, 0.0) for group in range(TILE_GROUPS)], axis=0
+        ).astype(BF16)
+        age = lax.broadcasted_iota(jnp.int32, (tokens, LANES), 0) + 1
+        rising = jnp.exp(-pack_ref[10:11, lanes] * age.astype(F32)) * follow_ref[...]
+        carried = jnp.dot(rising.astype(BF16), spread, preferred_element_type=F32)
+        halo = halo_ref[0, :, lanes].astype(F32)
+        for span, query in featured(x_ref, 0, lanes, halo, pack_ref[0:3, lanes], agree_ref, 64):
+            mixed = (local_ref[span, lanes] + carried[span]).astype(BF16)
+            out_ref[span, lanes] = (
+                query.astype(BF16).astype(F32) * mixed.astype(F32)
+            ).astype(BF16)
+
+
+def cost(flops, size, exps):
+    return pl.CostEstimate(flops=flops, bytes_accessed=size, transcendentals=exps)
+
+
+def mark_specs(tokens):
+    return [
+        pl.BlockSpec((1, 1, tokens), lambda i, b: (b[0], 0, 0)),
+        pl.BlockSpec((1, 1, tokens), lambda i, b: (jnp.maximum(b[0] - 1, 0), 0, 0)),
+    ]
+
+
+def block_states(block, streams, halo, pack, marks, width):
+    _, tokens, channels = streams.shape
+    return pl.pallas_call(
+        state_kernel,
+        grid_spec=pltpu.PrefetchScalarGridSpec(
+            num_scalar_prefetch=1,
+            grid=(channels // width,),
+            in_specs=[
+                pl.BlockSpec((pl.Element(2), pl.Element(tokens), pl.Element(width)),
+                             lambda i, b: (1, 0, i * width)),
+                pl.BlockSpec((3, SHORT - 1, width), lambda i, b: (0, 0, i)),
+                pl.BlockSpec((pack.shape[0], width), lambda i, b: (0, i)),
+                *mark_specs(tokens),
+            ],
+            out_specs=[
+                pl.BlockSpec((tokens, width), lambda i, b: (0, i)),
+                pl.BlockSpec((MODES, width), lambda i, b: (0, i)),
+                pl.BlockSpec((MODES, width), lambda i, b: (0, i)),
+            ],
+            scratch_shapes=[
+                pltpu.VMEM((SHORT - 1, tokens, LANES), F32),
+                pltpu.VMEM((8, tokens), F32),
+            ],
+        ),
+        out_shape=[
+            jax.ShapeDtypeStruct((tokens, channels), BF16),
+            jax.ShapeDtypeStruct((MODES, channels), BF16),
+            jax.ShapeDtypeStruct((MODES, channels), F32),
+        ],
+        compiler_params=pltpu.CompilerParams(vmem_limit_bytes=VMEM_BYTES),
+        cost_estimate=cost(20 * tokens * channels, 6 * tokens * channels, tokens * channels),
+        name="block_states",
+    )(block, streams, halo, pack, marks, marks)
+
+
+def block_local(block, gated, pack, marks, held, first, count, width):
+    tokens, channels = gated.shape
+    at = first // width
+    return pl.pallas_call(
+        local_kernel,
+        grid_spec=pltpu.PrefetchScalarGridSpec(
+            num_scalar_prefetch=1,
+            grid=(count // width,),
+            in_specs=[
+                pl.BlockSpec((tokens, width), lambda i, b: (0, i + at)),
+                pl.BlockSpec((pack.shape[0], width), lambda i, b: (0, i + at)),
+                *mark_specs(tokens),
+                *[pl.BlockSpec(memory_space=pl.ANY) for _ in held],
+            ],
+            out_specs=pl.BlockSpec((tokens, width), lambda i, b: (0, i + at)),
+            scratch_shapes=[pltpu.VMEM((tokens, tokens), BF16)],
+        ),
+        out_shape=jax.ShapeDtypeStruct((tokens, channels), F32),
+        input_output_aliases={5: 0} if held else {},
+        compiler_params=pltpu.CompilerParams(vmem_limit_bytes=VMEM_BYTES),
+        cost_estimate=cost(
+            2 * tokens * tokens * count * TILE_GROUPS, 6 * tokens * count, tokens * count
+        ),
+        name="block_local",
+    )(block, gated, pack, marks, marks, *held)
+
+
+def block_output(block, streams, halo, pack, marks, held, carry, width):
+    _, tokens, channels = streams.shape
+    return pl.pallas_call(
+        output_kernel,
+        grid_spec=pltpu.PrefetchScalarGridSpec(
+            num_scalar_prefetch=1,
+            grid=(channels // width,),
+            in_specs=[
+                pl.BlockSpec((1, tokens, width), lambda i, b: (0, 0, i)),
+                pl.BlockSpec((3, SHORT - 1, width), lambda i, b: (0, 0, i)),
+                pl.BlockSpec((pack.shape[0], width), lambda i, b: (0, i)),
+                *mark_specs(tokens),
+                pl.BlockSpec((tokens, width), lambda i, b: (0, i)),
+                pl.BlockSpec((MODES, width), lambda i, b: (0, i)),
+            ],
+            out_specs=pl.BlockSpec((tokens, width), lambda i, b: (0, i)),
+            scratch_shapes=[
+                pltpu.VMEM((SHORT - 1, tokens, LANES), F32),
+                pltpu.VMEM((tokens, LANES), F32),
+            ],
+        ),
+        out_shape=jax.ShapeDtypeStruct((tokens, channels), BF16),
+        compiler_params=pltpu.CompilerParams(vmem_limit_bytes=VMEM_BYTES),
+        cost_estimate=cost(20 * tokens * channels, 8 * tokens * channels, tokens * channels),
+        name="block_output",
+    )(block, streams, halo, pack, marks, marks, held, carry)
+
+
 SPAN = 8
 
 
@@ -70,7 +355,7 @@
     return (jnp.concatenate(pieces, axis=0), carried)
 
 
-def local(streams, segments, short_taps, decay_rates, residues, skip_gain):
+def narrow_local(streams, segments, short_taps, decay_rates, residues, skip_gain):
     fsdp_count = lax.axis_size("fsdp")
     ctx_count = lax.axis_size("ctx")
     tile_index = lax.axis_index("ctx")
@@ -132,6 +417,115 @@
     return returned
 
 
+def half_of(array, which):
+    size = array.shape[1] // 2
+    return lax.dynamic_slice_in_dim(array, which * size, size, axis=1)
+
+
+def swap(array, distance, devices):
+    route = [(i, i ^ distance) for i in range(devices)]
+    return lax.ppermute(array.astype(BF16), ("ctx", "fsdp"), route).astype(F32)
+
+
+def ordered(which, mine, other):
+    return jnp.where(which == 0, mine, other), jnp.where(which == 0, other, mine)
+
+
+def joined_halves(which, mine, other):
+    return jnp.concatenate(ordered(which, mine, other), axis=1)
+
+
+def carry_in(state, rates, marks, block, devices, tokens):
+    ends = marks[:, 0, tokens - 1]
+    places = jnp.arange(devices)
+
+    def end_of(index):
+        return jnp.sum(jnp.where(places == index, ends, 0))
+
+    def passes(earlier, later):
+        return (end_of(earlier) == end_of(later)).astype(F32)
+
+    def decay(rate, blocks):
+        return jnp.exp(-rate * (jnp.maximum(blocks, 0) * tokens).astype(F32))
+
+    one = jnp.int32(1)
+    low, high = block & 1, (block >> 1) & 1
+    pair, quad = block & ~1, block & ~3
+    mine = half_of(state, low).astype(F32)
+    other = swap(half_of(state, 1 - low), 1, devices)
+    first, second = ordered(low, mine, other)
+    rate = half_of(rates, low)
+    pair_end = second + passes(pair, pair + 1) * decay(rate, one) * first
+    mine = half_of(pair_end, high)
+    other = swap(half_of(pair_end, 1 - high), 2, devices)
+    lower, upper = ordered(high, mine, other)
+    narrow = half_of(rate, high)
+    total = upper + passes(quad + 1, quad + 3) * decay(narrow, 2 * one) * lower
+    carry = jnp.zeros_like(total)
+    size = 4
+    while size < devices:
+        other = swap(total, size, devices)
+        start = (block // (2 * size)) * (2 * size)
+        upside = (block // size) & 1
+        middle = start + size - 1
+        weight = upside.astype(F32) * passes(middle, quad - 1)
+        carry = carry + weight * decay(narrow, quad - 1 - middle) * other
+        if 2 * size < devices:
+            before, after = ordered(upside, total, other)
+            total = after + passes(middle, middle + size) * decay(narrow, size * one) * before
+        size *= 2
+    ahead = lower + passes(quad - 1, quad + 1) * decay(narrow, 2 * one) * carry
+    keep, send = ordered(high, carry, ahead)
+    carry = joined_halves(high, keep, swap(send, 2, devices))
+    ahead = first + passes(pair - 1, pair) * decay(rate, one) * carry
+    keep, send = ordered(low, carry, ahead)
+    other = swap(send, 1, devices)
+    return joined_halves(low, keep, other).astype(BF16)
+
+
+def gather_weights(pack, fsdp_count, index):
+    if fsdp_count != 2:
+        return lax.all_gather(pack, "fsdp", axis=1, tiled=True)
+    other = lax.ppermute(pack, "fsdp", [(0, 1), (1, 0)])
+    return joined_halves(index, pack, other)
+
+
+def local(streams, segments, short_taps, decay_rates, residues, skip_gain):
+    fsdp_count, ctx_count = lax.axis_size("fsdp"), lax.axis_size("ctx")
+    devices = fsdp_count * ctx_count
+    _, tokens, channels = streams.shape
+    if tokens % LANES:
+        return narrow_local(streams, segments, short_taps, decay_rates, residues, skip_gain)
+    fsdp_index = lax.axis_index("fsdp")
+    block = lax.axis_index("ctx") * fsdp_count + fsdp_index
+    block_ref = block.astype(jnp.int32).reshape(1)
+    owned = short_taps.shape[2]
+    mode_gain = residues * jnp.sqrt(-jnp.expm1(-2.0 * decay_rates))
+    pack = jnp.concatenate(
+        [
+            short_taps.reshape(3 * SHORT, owned),
+            skip_gain.reshape(1, owned),
+            decay_rates.reshape(1, owned),
+            mode_gain.reshape(1, owned),
+        ],
+        axis=0,
+    )
+    pack = gather_weights(pack, fsdp_count, fsdp_index)
+    halo = lax.ppermute(
+        streams[:, tokens - (SHORT - 1) :, :], ("ctx", "fsdp"),
+        [(i, i + 1) for i in range(devices - 1)],
+    )
+    marks = segments.reshape(devices, 1, tokens)
+    gated, state, rates = block_states(block_ref, streams, halo, pack, marks, 1024)
+    held = []
+    parts = 4
+    span = channels // parts
+    for part in range(parts):
+        held = [block_local(block_ref, gated, pack, marks, held, part * span, span, 1024)]
+    carry = carry_in(state, rates, marks, block, devices, tokens)
+    return block_output(block_ref, streams, halo, pack, marks, held[0], carry, 1024)
+
+
 def solution(mesh):
     placed = (
         P(None, ("ctx", "fsdp"), None),

time: 1410 us -> 139 us (0.10)
  the two profiles are of different devices: /device:TPU:16 before, /device:TPU:0 now
where the time goes in v1:
time: 139 us
  Pallas kernels  94.5 us (68%)
  starting transfers between devices  15.6 us (11%)
  between operations  11.5 us (8%)
  local copies, waits for them, and re-layouts  8.95 us (6%)
  other arithmetic  4.24 us (3%)
  waiting for transfers between devices  3.87 us (3%)
    pallas_call x4, Pallas kernels, block_local(): pl.pallas_call(local_kernel, grid_spec=pltpu.PrefetchScalarGridSpec(num_s...  54.2 us
    pallas_call x1, Pallas kernels, block_states(): pl.pallas_call(state_kernel, grid_spec=pltpu.PrefetchScalarGridSpec(num_s...  21.3 us
    pallas_call x1, Pallas kernels, block_output(): pl.pallas_call(output_kernel, grid_spec=pltpu.PrefetchScalarGridSpec(num_...  19 us
    ppermute x7, starting transfers between devices, swap(): return lax.ppermute(array.astype(BF16), ('ctx', 'fsdp'), route).astype(F32)  10.6 us
    unnamed x9, local copies, waits for them, and re-layouts  5.77 us
    ppermute x1, waiting for transfers between devices, gather_weights(): other = lax.ppermute(pack, 'fsdp', [(0, 1), (1, 0)])  3.57 us
    ppermute x1, starting transfers between devices, gather_weights(): other = lax.ppermute(pack, 'fsdp', [(0, 1), (1, 0)])  3.03 us
  transfers between devices with their start and end apart: 9, of which 2 were waited for; matrix products, arithmetic and copies ran while one was open for 3% of the time, Pallas kernels for 39%

profile of v1, /device:TPU:0, one launch (start us, length us, event | category | flops | bytes accessed | tf_op | source)
XLA Modules:
  0.0 138.7 jit_solution(1457973117480967394)
XLA Ops:
  0.0 0.8 copy.12
  0.8 0.8 sqrt_multiply_fusion
  1.6 0.1 copy.13
  1.7 0.1 reshape.22
  1.8 0.1 reshape.21
  1.9 1.0 reshape.19
  2.9 0.8 pad_maximum_fusion.1
  3.7 3.0 %collective-permute-start.1 = (f32[12,4096]{1,0:T(8,128)S(1)}, f32[12,4096]{1,0:T(8,128)S(1)}, u32[]{:S(2)}, u32[]{:S(2)}) collective-permute-start(f32[12,4096]{1,0:T(8,128)S(1)} %pad_maximum_fusion.1), channel_id=1, source_target_pairs={{0,1},{1,0},{2,3},{3,2},{4,5},{5,4},{6,7},{7,6},{8,9},{9,8},{10,11... | collective-permute-start | bytes 589832 | tf_op jit(solution)/shard_map/ppermute | solution.py:489
  6.7 1.1 slice.6
  7.8 1.9 %collective-permute-start = (bf16[3,2,8192]{2,1,0:T(2,128)(2,1)S(1)}, bf16[3,2,8192]{2,1,0:T(2,128)(2,1)S(1)}, u32[]{:S(2)}, u32[]{:S(2)}) collective-permute-start(bf16[3,2,8192]{2,1,0:T(2,128)(2,1)S(1)} %slice.6), channel_id=1, source_target_pairs={{0,1},{1,2},{2,3},{3,4},{4,5},{5,6},{6,7},{7,8},{8,9},{9,10},{10,1... | collective-permute-start | bytes 294920 | tf_op jit(solution)/shard_map/ppermute | solution.py:514
  9.8 3.6 %collective-permute-done.1 = f32[12,4096]{1,0:T(8,128)S(1)} collective-permute-done((f32[12,4096]{1,0:T(8,128)S(1)}, f32[12,4096]{1,0:T(8,128)S(1)}, u32[]{:S(2)}, u32[]{:S(2)}) %collective-permute-start.1) | collective-permute-done | bytes 196640 | tf_op jit(solution)/shard_map/ppermute | solution.py:489
  13.4 0.8 broadcast_select_fusion.1
  14.2 0.0 copy-start.3
  14.2 0.2 collective-permute-done.halo_ref
  14.4 0.8 copy-done.2
  15.2 21.3 %block_states.1 = (bf16[256,8192]{1,0:T(8,128)(2,1)S(1)}, bf16[16,8192]{1,0:T(8,128)(2,1)S(1)}, f32[16,8192]{1,0:T(8,128)S(1)}) custom-call(s32[1]{0:T(128)} %bitcast.block_ref, bf16[3,256,8192]{2,1,0:T(8,128)(2,1)} %x_ref.3, bf16[3,2,8192]{2,1,0:T(2,128)(2,1)S(1)} %collective-permute-done.halo_ref, f32[12,8192]{1,0:T(8,128)S(1)} %pad_maximum_fusion.pack_ref, ...), custom_call_target="tpu_custom_call" | custom-call | flops 41943040 | bytes 12582912 | tf_op jit(solution)/shard_map/block_states/pallas_call | solution.py:206
  36.5 0.0 copy-start
  36.5 2.0 %copy-done = bf16[256,8192]{1,0:T(8,128)(2,1)} copy-done((bf16[256,8192]{1,0:T(8,128)(2,1)}, bf16[256,8192]{1,0:T(8,128)(2,1)S(1)}, u32[]{:S(2)}) %copy-start) | copy-done | bytes 4194328
  38.5 2.5 %collective-permute-start.2 = (bf16[16,4096]{1,0:T(8,128)(2,1)S(1)}, bf16[16,4096]{1,0:T(8,128)(2,1)S(1)}, u32[]{:S(2)}, u32[]{:S(2)}) collective-permute-start(bf16[16,4096]{1,0:T(8,128)(2,1)S(1)} %constant_dynamic-slice_fusion), channel_id=1, source_target_pairs={{0,1},{1,0},{2,3},{3,2},{4,5},{5,4},{6,7},{7,6},{8,9},{9,8},{10,11... | collective-permute-start | bytes 393224 | tf_op jit(solution)/shard_map/ppermute | solution.py:427
  41.1 0.7 slice_reduce_fusion
  41.8 0.9 fusion.22
  44.0 0.0 collective-permute-done.2
  44.0 0.1 fusion
  44.1 0.1 collective-permute-start.3
  45.4 0.0 collective-permute-done.3
  45.4 0.1 fusion.26
  45.6 2.3 %collective-permute-start.4 = (bf16[16,2048]{1,0:T(8,128)(2,1)S(1)}, bf16[16,2048]{1,0:T(8,128)(2,1)S(1)}, u32[]{:S(2)}, u32[]{:S(2)}) collective-permute-start(bf16[16,2048]{1,0:T(8,128)(2,1)S(1)} %get-tuple-element.27), channel_id=1, source_target_pairs={{0,4},{1,5},{2,6},{3,7},{4,0},{5,1},{6,2},{7,3},{8,12},{9,13},{10,... | collective-permute-start | bytes 196616 | tf_op jit(solution)/shard_map/ppermute | solution.py:427
  56.7 0.0 collective-permute-done.4
  56.8 0.1 fusion.23
  56.9 1.6 %collective-permute-start.5 = (bf16[16,2048]{1,0:T(8,128)(2,1)S(1)}, bf16[16,2048]{1,0:T(8,128)(2,1)S(1)}, u32[]{:S(2)}, u32[]{:S(2)}) collective-permute-start(bf16[16,2048]{1,0:T(8,128)(2,1)S(1)} %fusion.23), channel_id=1, source_target_pairs={{0,8},{1,9},{2,10},{3,11},{4,12},{5,13},{6,14},{7,15},{8,0},{9,1},... | collective-permute-start | bytes 196616 | tf_op jit(solution)/shard_map/ppermute | solution.py:427
  58.5 0.0 copy-done.3
  58.5 2.2 %copy-done.1 = bf16[256,8192]{1,0:T(8,128)(2,1)S(1)} copy-done((bf16[256,8192]{1,0:T(8,128)(2,1)S(1)}, bf16[256,8192]{1,0:T(8,128)(2,1)}, u32[]{:S(2)}) %copy-start.1) | copy-done | bytes 4194328
  60.7 13.5 %block_local.4.rest_0_ = f32[256,8192]{1,0:T(8,128)} custom-call(s32[1]{0:T(128)} %bitcast.block_ref, bf16[256,8192]{1,0:T(8,128)(2,1)S(1)} %copy-done.1, f32[12,8192]{1,0:T(8,128)S(1)} %pad_maximum_fusion.pack_ref, s32[32,1,256]{2,1,0:T(1,128)S(1)} %bitcast.6, s32[32,1,256]{2,1,0:T(1,128)S(1)} %bitcast.7), custom_call_target="tpu_custom_call" | custom-call | flops 2147483648 | bytes 3145728 | tf_op jit(solution)/shard_map/block_local/pallas_call | solution.py:242
  74.2 0.0 collective-permute-done.5
  74.2 0.2 fusion.10
  74.4 2.7 %collective-permute-start.6 = (bf16[16,2048]{1,0:T(8,128)(2,1)S(1)}, bf16[16,2048]{1,0:T(8,128)(2,1)S(1)}, u32[]{:S(2)}, u32[]{:S(2)}) collective-permute-start(bf16[16,2048]{1,0:T(8,128)(2,1)S(1)} %fusion.10), channel_id=1, source_target_pairs={{0,16},{1,17},{2,18},{3,19},{4,20},{5,21},{6,22},{7,23},{8,24},{9,... | collective-permute-start | bytes 196616 | tf_op jit(solution)/shard_map/ppermute | solution.py:427
  77.1 13.5 %block_local.5.rest_0_ = f32[256,8192]{1,0:T(8,128)} custom-call(s32[1]{0:T(128)} %bitcast.block_ref, bf16[256,8192]{1,0:T(8,128)(2,1)S(1)} %copy-done.1, f32[12,8192]{1,0:T(8,128)S(1)} %pad_maximum_fusion.pack_ref, s32[32,1,256]{2,1,0:T(1,128)S(1)} %bitcast.8, s32[32,1,256]{2,1,0:T(1,128)S(1)} %bitcast.9, ...), custom_call_target="tpu_custom_call", output_to_operand_aliasing={{}: (5, {})} | custom-call | flops 2147483648 | bytes 3145728 | tf_op jit(solution)/shard_map/block_local/pallas_call | solution.py:242
  90.6 0.0 collective-permute-done.6
  90.6 0.2 select_convert_fusion.1
  90.8 0.1 collective-permute-start.7
  90.9 13.5 %block_local.6.rest_0_ = f32[256,8192]{1,0:T(8,128)} custom-call(s32[1]{0:T(128)} %bitcast.block_ref, bf16[256,8192]{1,0:T(8,128)(2,1)S(1)} %copy-done.1, f32[12,8192]{1,0:T(8,128)S(1)} %pad_maximum_fusion.pack_ref, s32[32,1,256]{2,1,0:T(1,128)S(1)} %bitcast.10, s32[32,1,256]{2,1,0:T(1,128)S(1)} %bitcast.11, ...), custom_call_target="tpu_custom_call", output_to_operand_aliasing={{}: (5, {})} | custom-call | flops 2147483648 | bytes 3145728 | tf_op jit(solution)/shard_map/block_local/pallas_call | solution.py:242
  104.4 0.0 collective-permute-done.7
  104.5 0.1 select_convert_fusion
  104.6 1.3 collective-permute-start.8
  105.9 13.6 %block_local.7.local_ref = f32[256,8192]{1,0:T(8,128)} custom-call(s32[1]{0:T(128)} %bitcast.block_ref, bf16[256,8192]{1,0:T(8,128)(2,1)S(1)} %copy-done.1, f32[12,8192]{1,0:T(8,128)S(1)} %pad_maximum_fusion.pack_ref, s32[32,1,256]{2,1,0:T(1,128)S(1)} %bitcast.12, s32[32,1,256]{2,1,0:T(1,128)S(1)} %bitcast.13, ...), custom_call_target="tpu_custom_call", output_to_operand_aliasing={{}: (5, {})} | custom-call | flops 2147483648 | bytes 3145728 | tf_op jit(solution)/shard_map/block_local/pallas_call | solution.py:242
  119.5 0.0 collective-permute-done.8
  119.5 0.1 fusion.1
  119.7 19.0 %block_output.1 = bf16[256,8192]{1,0:T(8,128)(2,1)} custom-call(s32[1]{0:T(128)} %bitcast.block_ref, bf16[3,256,8192]{2,1,0:T(8,128)(2,1)} %x_ref.3, bf16[3,2,8192]{2,1,0:T(2,128)(2,1)S(1)} %collective-permute-done.halo_ref, f32[12,8192]{1,0:T(8,128)S(1)} %pad_maximum_fusion.pack_ref, s32[32,1,256]{2,1,0:T(1,128)S(1)} %bitcast.14, ...), custom_call_target="tpu_custom_call" | custom-call | flops 41943040 | bytes 16777216 | tf_op jit(solution)/shard_map/block_output/pallas_call | solution.py:268
  (8 shorter events, 0.1 us)
Async XLA Ops:
  3.7 9.7 %collective-permute-start.1 = (f32[12,4096]{1,0:T(8,128)S(1)}, f32[12,4096]{1,0:T(8,128)S(1)}, u32[]{:S(2)}, u32[]{:S(2)}) collective-permute-start(f32[12,4096]{1,0:T(8,128)S(1)} %pad_maximum_fusion.1), channel_id=1, source_target_pairs={{0,1},{1,0},{2,3},{3,2},{4,5},{5,4},{6,7},{7,6},{8,9},{9,8},{10,11... | collective-permute-start | bytes 589832 | tf_op jit(solution)/shard_map/ppermute | solution.py:489
  7.8 6.6 %collective-permute-start = (bf16[3,2,8192]{2,1,0:T(2,128)(2,1)S(1)}, bf16[3,2,8192]{2,1,0:T(2,128)(2,1)S(1)}, u32[]{:S(2)}, u32[]{:S(2)}) collective-permute-start(bf16[3,2,8192]{2,1,0:T(2,128)(2,1)S(1)} %slice.6), channel_id=1, source_target_pairs={{0,1},{1,2},{2,3},{3,4},{4,5},{5,6},{6,7},{7,8},{8,9},{9,10},{10,1... | collective-permute-start | bytes 294920 | tf_op jit(solution)/shard_map/ppermute | solution.py:514
  14.2 44.4 %copy-start.3 = (s32[8192]{0:T(1024)S(1)}, s32[8192]{0:T(1024)}, u32[]{:S(2)}) copy-start(s32[8192]{0:T(1024)} %param.7) | copy-start | bytes 98308
  14.4 0.8 copy-start.2
  36.5 2.0 %copy-start = (bf16[256,8192]{1,0:T(8,128)(2,1)}, bf16[256,8192]{1,0:T(8,128)(2,1)S(1)}, u32[]{:S(2)}) copy-start(bf16[256,8192]{1,0:T(8,128)(2,1)S(1)} %get-tuple-element.8.gated_ref) | copy-start | bytes 12582916
  38.5 5.5 %collective-permute-start.2 = (bf16[16,4096]{1,0:T(8,128)(2,1)S(1)}, bf16[16,4096]{1,0:T(8,128)(2,1)S(1)}, u32[]{:S(2)}, u32[]{:S(2)}) collective-permute-start(bf16[16,4096]{1,0:T(8,128)(2,1)S(1)} %constant_dynamic-slice_fusion), channel_id=1, source_target_pairs={{0,1},{1,0},{2,3},{3,2},{4,5},{5,4},{6,7},{7,6},{8,9},{9,8},{10,11... | collective-permute-start | bytes 393224 | tf_op jit(solution)/shard_map/ppermute | solution.py:427
  44.1 1.3 collective-permute-start.3
  45.6 11.2 %collective-permute-start.4 = (bf16[16,2048]{1,0:T(8,128)(2,1)S(1)}, bf16[16,2048]{1,0:T(8,128)(2,1)S(1)}, u32[]{:S(2)}, u32[]{:S(2)}) collective-permute-start(bf16[16,2048]{1,0:T(8,128)(2,1)S(1)} %get-tuple-element.27), channel_id=1, source_target_pairs={{0,4},{1,5},{2,6},{3,7},{4,0},{5,1},{6,2},{7,3},{8,12},{9,13},{10,... | collective-permute-start | bytes 196616 | tf_op jit(solution)/shard_map/ppermute | solution.py:427
  56.9 17.4 %collective-permute-start.5 = (bf16[16,2048]{1,0:T(8,128)(2,1)S(1)}, bf16[16,2048]{1,0:T(8,128)(2,1)S(1)}, u32[]{:S(2)}, u32[]{:S(2)}) collective-permute-start(bf16[16,2048]{1,0:T(8,128)(2,1)S(1)} %fusion.23), channel_id=1, source_target_pairs={{0,8},{1,9},{2,10},{3,11},{4,12},{5,13},{6,14},{7,15},{8,0},{9,1},... | collective-permute-start | bytes 196616 | tf_op jit(solution)/shard_map/ppermute | solution.py:427
  58.5 2.2 %copy-start.1 = (bf16[256,8192]{1,0:T(8,128)(2,1)S(1)}, bf16[256,8192]{1,0:T(8,128)(2,1)}, u32[]{:S(2)}) copy-start(bf16[256,8192]{1,0:T(8,128)(2,1)} %copy-done) | copy-start | bytes 12582916
  74.4 16.2 %collective-permute-start.6 = (bf16[16,2048]{1,0:T(8,128)(2,1)S(1)}, bf16[16,2048]{1,0:T(8,128)(2,1)S(1)}, u32[]{:S(2)}, u32[]{:S(2)}) collective-permute-start(bf16[16,2048]{1,0:T(8,128)(2,1)S(1)} %fusion.10), channel_id=1, source_target_pairs={{0,16},{1,17},{2,18},{3,19},{4,20},{5,21},{6,22},{7,23},{8,24},{9,... | collective-permute-start | bytes 196616 | tf_op jit(solution)/shard_map/ppermute | solution.py:427
  90.8 13.6 %collective-permute-start.7 = (bf16[16,2048]{1,0:T(8,128)(2,1)S(1)}, bf16[16,2048]{1,0:T(8,128)(2,1)S(1)}, u32[]{:S(2)}, u32[]{:S(2)}) collective-permute-start(bf16[16,2048]{1,0:T(8,128)(2,1)S(1)} %get-tuple-element.24), channel_id=1, source_target_pairs={{0,2},{1,3},{2,0},{3,1},{4,6},{5,7},{6,4},{7,5},{8,10},{9,11},{10,... | collective-permute-start | bytes 196616 | tf_op jit(solution)/shard_map/ppermute | solution.py:427
  104.6 14.9 %collective-permute-start.8 = (bf16[16,4096]{1,0:T(8,128)(2,1)S(1)}, bf16[16,4096]{1,0:T(8,128)(2,1)S(1)}, u32[]{:S(2)}, u32[]{:S(2)}) collective-permute-start(bf16[16,4096]{1,0:T(8,128)(2,1)S(1)} %select_convert_fusion), channel_id=1, source_target_pairs={{0,1},{1,0},{2,3},{3,2},{4,5},{5,4},{6,7},{7,6},{8,9},{9,8},{10,11... | collective-permute-start | bytes 393224 | tf_op jit(solution)/shard_map/ppermute | solution.py:427

commit v2 on v0

--- a/solution.py
+++ b/solution.py
@@ -1,11 +1,655 @@
 import jax
 import jax.numpy as jnp
 from jax import lax
+from jax.experimental import pallas as pl
+from jax.experimental.pallas import tpu as pltpu
 from jax.sharding import PartitionSpec as P
 
 GROUP = 16
 MODES = 16
 SHORT = 3
+LANES = 128
+PART = 128
+PARTS = 2
+WIDE = 256
+COPIES = 4
+TILES = 4
+TILE_GROUPS = LANES // GROUP
+ROWS = 64
+LOG2E = 1.4426950408889634
+F32 = jnp.float32
+BF16 = jnp.bfloat16
+VMEM = pl.BlockSpec(memory_space=pltpu.VMEM)
+SMEM = pl.BlockSpec(memory_space=pltpu.SMEM)
+HBM = pl.BlockSpec(memory_space=pltpu.HBM)
+ANY = pl.BlockSpec(memory_space=pl.ANY)
+SKIP, RATE, GAIN, PACKED = 9, 10, 11, 16
+OWN, OTHER, LOW, HIGH, UPSIDES = 0, 1, 2, 3, 4
+PAIR_PASS, QUAD_PASS, QUAD_FROM, PAIR_FROM, ROUNDS = 0, 1, 2, 3, 4
+
+
+def iota(shape, axis):
+    return lax.broadcasted_iota(jnp.int32, shape, axis)
+
+
+def flag(condition):
+    return jnp.where(condition, 1.0, 0.0)
+
+
+def as_column(row):
+    return jnp.transpose(jnp.broadcast_to(row, (LANES, row.shape[1])))
+
+
+def lanes_at(start, size=LANES):
+    return pl.ds(pl.multiple_of(start, LANES), size)
+
+
+def weave(*lists):
+    order = sorted(
+        ((i + 0.5) / len(jobs), n, i) for n, jobs in enumerate(lists) for i in range(len(jobs))
+    )
+    for _, n, i in order:
+        lists[n][i]()
+
+
+def featured(x_ref, lanes, taps, agree_ref, start, halo):
+    if start == 0:
+        here = x_ref[0:ROWS, lanes].astype(F32)
+        sub = iota((8, LANES), 0)
+        ahead = jnp.where(sub == 6, halo[0:1], jnp.where(sub == 7, halo[1:2], 0.0))
+    else:
+        both = x_ref[start - 16 : start + ROWS, lanes].astype(F32)
+        here, ahead = both[16:], both[8:16]
+    joined = jnp.concatenate([ahead, here], axis=0)
+    summed = here * taps[0:1]
+    for offset in range(1, SHORT):
+        shifted = pltpu.roll(joined, offset, 0)[8:]
+        agree = agree_ref[offset - 1, start : start + ROWS, :]
+        summed = summed + shifted * agree * taps[offset : offset + 1]
+    return summed
+
+
+def spread(state):
+    own = iota(state.shape, 1) // GROUP
+    return jnp.concatenate(
+        [jnp.where(own == group, state, 0.0) for group in range(TILE_GROUPS)], axis=0
+    ).astype(BF16)
+
+
+def diagonal(full):
+    own = iota((MODES, LANES), 1) // GROUP
+    state = full[:MODES]
+    for group in range(1, TILE_GROUPS):
+        state = jnp.where(own == group, full[group * MODES : (group + 1) * MODES], state)
+    return state
+
+
+def pack_weights(short_ref, skip_ref, rates_ref, residues_ref, pack_ref):
+    for stream in range(3):
+        pack_ref[stream * SHORT : (stream + 1) * SHORT, :] = short_ref[stream]
+    pack_ref[SKIP : SKIP + 1, :] = skip_ref[...]
+    pack_ref[GAIN + 1 :, :] = jnp.zeros((PACKED - GAIN - 1, pack_ref.shape[1]), F32)
+    shape = (MODES, LANES)
+    own = iota(shape, 1) % MODES == iota(shape, 0)
+
+    def tile(number, carried):
+        at = lanes_at(number * LANES)
+        first = number * TILE_GROUPS
+        source = lanes_at(first // LANES * LANES)
+        index = first % LANES + iota(shape, 1) // MODES
+        rate = jnp.take_along_axis(rates_ref[:, source], index, axis=1)
+        factor = jnp.take_along_axis(residues_ref[:, source], index, axis=1)
+        rate = jnp.sum(jnp.where(own, rate, 0.0), axis=0, keepdims=True)
+        factor = jnp.sum(jnp.where(own, factor, 0.0), axis=0, keepdims=True)
+        half = jnp.tanh(rate)
+        pack_ref[RATE : RATE + 1, at] = rate
+        pack_ref[GAIN : GAIN + 1, at] = factor * jnp.sqrt(2.0 * half / (1.0 + half))
+        return carried
+
+    lax.fori_loop(0, pack_ref.shape[1] // LANES, tile, 0, unroll=4)
+
+
+def place_kernel(
+    spots_ref, marks_ref, short_ref, skip_ref, rates_ref, residues_ref, x_ref,
+    place_ref, weights_ref, agree_ref, causal_ref, follow_ref, enter_ref, chosen_ref, pack_ref, tail_ref,
+    ends_ref, sem, *, devices, tokens, fsdp_count,
+):
+    owned = pack_ref.shape[1]
+    lines = tokens // LANES
+    tail = pltpu.make_async_copy(x_ref.at[:, pl.ds(tokens - 16, 16), :], ends_ref, sem)
+    tail.start()
+    pack_weights(short_ref, skip_ref, rates_ref, residues_ref, pack_ref)
+    fsdp_index = lax.axis_index("fsdp")
+    block = lax.axis_index("ctx") * fsdp_count + fsdp_index
+    place_ref[OWN] = fsdp_index * owned
+    place_ref[OTHER] = (1 - fsdp_index) * owned
+    place_ref[LOW] = lax.rem(block, 2)
+    place_ref[HIGH] = lax.rem(lax.div(block, 2), 2)
+    pair = block - lax.rem(block, 2)
+    quad = block - lax.rem(block, 4)
+
+    def end_of(index):
+        return spots_ref[jnp.maximum(index, 0) * lines + lines - 1, LANES - 1]
+
+    def passes(earlier, later):
+        return jnp.where(end_of(earlier) == end_of(later), 1.0, 0.0)
+
+    weights_ref[PAIR_PASS] = passes(pair, pair + 1)
+    weights_ref[QUAD_PASS] = passes(quad + 1, quad + 3)
+    weights_ref[QUAD_FROM] = passes(quad - 1, quad + 1)
+    weights_ref[PAIR_FROM] = passes(pair - 1, pair)
+    size, number = 4, 0
+    while size < devices:
+        start = block - lax.rem(block, 2 * size)
+        upside = lax.rem(lax.div(block, size), 2)
+        middle = start + size - 1
+        place_ref[UPSIDES + number] = upside
+        at = ROUNDS + 3 * number
+        weights_ref[at] = jnp.where(upside == 1, passes(middle, quad - 1), 0.0)
+        weights_ref[at + 1] = (jnp.maximum(quad - 1 - middle, 0) * tokens).astype(F32)
+        weights_ref[at + 2] = passes(middle, middle + size)
+        size, number = 2 * size, number + 1
+
+    def marks_of(index):
+        return jnp.concatenate(
+            [marks_ref[pl.ds(index * lines + line, 1), :] for line in range(lines)], axis=1
+        ).astype(F32)
+
+    marks = marks_of(block)
+    before = jnp.where(block > 0, marks_of(jnp.maximum(block - 1, 0)), -1.0)
+    column = as_column(marks)
+    lane = iota(marks.shape, 1)
+    for offset in range(1, SHORT):
+        row = jnp.where(lane < offset, pltpu.roll(before, offset, 1), pltpu.roll(marks, offset, 1))
+        agree_ref[offset - 1] = flag(column == as_column(row))
+    for part in range(PARTS):
+        span = slice(part * PART, (part + 1) * PART)
+        same = column[span] == marks[:, span]
+        mask = flag(same & (iota((PART, LANES), 0) >= iota((PART, LANES), 1))).astype(BF16)
+        causal_ref[part] = jnp.concatenate([mask] * 2, axis=1)
+        last = marks[:, (part + 1) * PART - 1 : (part + 1) * PART]
+        chosen_ref[part] = jnp.broadcast_to(flag(marks[:, span] == last), (LANES, PART)).astype(BF16)
+    follow_ref[...] = flag(column[PART:] == marks[:, PART - 1 : PART]).astype(BF16)
+    enter_ref[...] = flag(column == before[:, tokens - 1 :]).astype(BF16)
+    inside = spots_ref[block * lines + PART // LANES - 1, LANES - 1] == end_of(block)
+    weights_ref[ROUNDS + 3 * number] = jnp.where(inside, 1.0, 0.0)
+    tail.wait()
+    for stream in range(3):
+        tail_ref[stream] = ends_ref[stream, 16 - (SHORT - 1) :, :]
+
+
+def start_copies(x_ref, origin, moves, sems):
+    copies = []
+    for stream, ref in moves:
+        rows = ref.shape[0] // COPIES
+        for number in range(COPIES):
+            span = slice(number * rows, (number + 1) * rows)
+            there = pl.ds(pl.multiple_of(origin, ref.shape[1]), ref.shape[1])
+            copies.append(
+                pltpu.make_async_copy(x_ref.at[stream, span, there], ref.at[span, :], sems.at[len(copies)])
+            )
+            copies[-1].start()
+    return copies
+
+
+def lag_kernel(*refs, side):
+    copies = []
+    if side == OWN:
+        place_ref, x_ref, pack_ref, taps_ref, fall_ref, keys_ref, values_ref, sems = refs
+        copies = start_copies(x_ref, place_ref[OWN], ((1, keys_ref), (2, values_ref)), sems)
+    else:
+        pack_ref, taps_ref, fall_ref = refs
+    left = (PART - 1 - iota((LANES, PART), 1)).astype(F32)
+
+    def tile(number, carried):
+        at = lanes_at(number * LANES)
+        fall = jnp.exp2(as_column(pack_ref[RATE : RATE + 1, at] * -LOG2E) * left)
+        fall_ref[pl.ds(pl.multiple_of(number * LANES, LANES), LANES), :] = fall.astype(BF16)
+        terms = (as_column(pack_ref[GAIN : GAIN + 1, at]) * fall).reshape(TILE_GROUPS, MODES, PART)
+        groups = pl.ds(pl.multiple_of(number * TILE_GROUPS, TILE_GROUPS), TILE_GROUPS)
+        taps_ref[groups, :] = jnp.sum(terms, axis=1)
+        return carried
+
+    lax.fori_loop(0, pack_ref.shape[1] // LANES, tile, 0, unroll=4)
+    for copy in copies:
+        copy.wait()
+
+
+def state_kernel(
+    place_ref, weights_ref, x_ref, keys_ref, values_ref, halo_ref, pack_ref, fall_ref, agree_ref, chosen_ref,
+    gated_ref, query_ref, state_ref, middle_ref, rates_ref, *rest, side, passing,
+):
+    tokens, channels = gated_ref.shape
+    copies = start_copies(x_ref, place_ref[side], ((0, query_ref),), rest[-1])
+    if side == OWN:
+        copies += start_copies(
+            x_ref, place_ref[OTHER], ((1, rest[0]), (2, rest[1])), rest[-1].at[pl.ds(COPIES, 2 * COPIES)]
+        )
+    origin = place_ref[side]
+    shape = (MODES, LANES)
+    index = iota(shape, 1) // GROUP * GROUP + iota(shape, 0)
+
+    def feature_jobs(start, made):
+        at = lanes_at(start)
+
+        def one(row):
+            halos = [halo_ref[stream, :, lanes_at(origin + start)].astype(F32) for stream in (1, 2)]
+            key = featured(keys_ref, at, pack_ref[SHORT : 2 * SHORT, at], agree_ref, row, halos[0])
+            value = featured(values_ref, at, pack_ref[2 * SHORT : 3 * SHORT, at], agree_ref, row, halos[1])
+            made[row] = (key * value).astype(BF16)
+            gated_ref[row : row + ROWS, at] = made[row]
+
+        return [lambda row=row: one(row) for row in range(0, tokens, ROWS)]
+
+    def state_jobs(start, made):
+        at = lanes_at(start)
+        held = {}
+
+        def product(part):
+            fall = fall_ref[pl.ds(pl.multiple_of(start, LANES), LANES), :]
+            right = [made[row] for row in range(part * PART, (part + 1) * PART, ROWS)]
+            held[part] = jnp.dot(
+                fall * chosen_ref[part], jnp.concatenate(right, axis=0), preferred_element_type=F32
+            )
+
+        def finish():
+            first, last = diagonal(held[0]), diagonal(held[1])
+            row = jnp.broadcast_to(pack_ref[RATE : RATE + 1, at], shape)
+            rate = jnp.take_along_axis(row, index, axis=1)
+            rates_ref[:, at] = rate
+            middle_ref[:, at] = first
+            onward = jnp.exp(-rate * PART) * weights_ref[passing] * first
+            state_ref[:, at] = (last + onward).astype(BF16)
+
+        return [lambda part=part: product(part) for part in range(PARTS)] + [finish]
+
+    @pl.loop(0, channels // (TILES * LANES))
+    def _(step):
+        made, jobs = {}, []
+        for tile in range(TILES):
+            start = step * TILES * LANES + tile * LANES
+            made = {}
+            ahead = feature_jobs(start, made)
+            weave(ahead, jobs)
+            jobs = state_jobs(start, made)
+        weave(jobs)
+
+    for copy in copies:
+        copy.wait()
+
+
+def lag_jobs(step, first, taps_ref, mats_ref):
+    held = {}
+
+    def bases(tile):
+        at = pl.multiple_of((first + step * WIDE) // GROUP, 8) + tile * TILE_GROUPS
+        taps = taps_ref[pl.ds(pl.multiple_of(at, 8), TILE_GROUPS), :]
+        index = (iota((8, LANES), 1) + (LANES - 1) - iota((8, LANES), 0)) & (LANES - 1)
+        rows = [jnp.broadcast_to(taps[group : group + 1], (8, LANES)) for group in range(TILE_GROUPS)]
+        early = [jnp.take_along_axis(row, index, axis=1) for row in rows]
+        late = [pltpu.roll(base, 8, 1) for base in early]
+        held[tile] = [jnp.concatenate(both, axis=0).astype(BF16) for both in zip(early, late)]
+
+    def rolls(tile, row):
+        for group in range(TILE_GROUPS):
+            both = held[tile][group]
+            odd = group % 2
+            mats_ref[tile * 4 + group // 2, row : row + 16, odd * LANES : (odd + 1) * LANES] = (
+                pltpu.roll(both, row, 1) if row else both
+            )
+
+    jobs = []
+    for tile in range(WIDE // LANES):
+        jobs.append(lambda tile=tile: bases(tile))
+        jobs += [lambda tile=tile, row=row: rolls(tile, row) for row in range(0, PART, 16)]
+    return jobs
+
+
+def filter_jobs(
+    step, first, gated_ref, pack_ref, middle_ref, mats_ref, causal_ref, follow_ref,
+    local_ref, onward_ref,
+):
+    held = {}
+    odd = iota((16, LANES), 1) // GROUP % 2
+    keep = [jnp.concatenate([flag(odd == i).astype(BF16)] * (PART // 16), axis=0) for i in (0, 1)]
+    own = iota((1, LANES), 1) // (2 * GROUP)
+
+    def source(tile):
+        return lanes_at(first + step * WIDE + tile * LANES)
+
+    def target(tile):
+        return lanes_at(step * WIDE + tile * LANES)
+
+    def span(part):
+        return slice(part * PART, (part + 1) * PART)
+
+    def inner(part, tile):
+        values = gated_ref[span(part), source(tile)]
+        right = jnp.concatenate([values * keep[0], values * keep[1]], axis=0)
+        left = jnp.concatenate([mats_ref[tile * 4 + i] * causal_ref[part] for i in range(4)], axis=0)
+        held["full", part, tile] = jnp.dot(left, right, preferred_element_type=F32)
+
+    def pick(part, tile):
+        full = held["full", part, tile]
+        value = full[:PART]
+        for i in range(1, 4):
+            value = jnp.where(own == i, full[i * PART : (i + 1) * PART], value)
+        held[part, tile] = value
+
+    def carry(tile):
+        at = source(tile)
+        age = (iota((PART, LANES), 0) + 1).astype(F32)
+        onward = jnp.exp2(pack_ref[RATE : RATE + 1, at] * -LOG2E * age) * pack_ref[GAIN : GAIN + 1, at]
+        onward = onward.astype(BF16)
+        onward_ref[:, target(tile)] = onward
+        held["carry", tile] = jnp.dot(
+            onward * follow_ref[...], spread(middle_ref[:, at]), preferred_element_type=F32
+        )
+
+    def finish(part, tile):
+        at = source(tile)
+        value = held[part, tile] + pack_ref[SKIP : SKIP + 1, at] * gated_ref[span(part), at].astype(F32)
+        if part:
+            value = value + held["carry", tile]
+        local_ref[span(part), target(tile)] = value
+
+    return [
+        lambda: carry(0), lambda: inner(0, 0), lambda: carry(1), lambda: inner(1, 0),
+        lambda: pick(0, 0), lambda: finish(0, 0), lambda: inner(0, 1), lambda: pick(1, 0),
+        lambda: finish(1, 0), lambda: inner(1, 1), lambda: pick(0, 1), lambda: finish(0, 1),
+        lambda: pick(1, 1), lambda: finish(1, 1),
+    ]
+
+
+def local_kernel(
+    place_ref, query_ref, halo_ref, gated_ref, pack_ref, taps_ref, middle_ref,
+    agree_ref, causal_ref, follow_ref, _,
+    local_ref, queries_ref, onward_ref, token_ref,
+    mats_a, mats_b, *, side, first,
+):
+    tokens, channels = local_ref.shape
+    token_ref[...] = jnp.zeros_like(token_ref)
+    origin = place_ref[side] + first
+
+    def query_jobs(step):
+        def one(tile, start):
+            at = step * WIDE + tile * LANES
+            halo = halo_ref[0, :, lanes_at(origin + at)].astype(F32)
+            source = lanes_at(first + at)
+            summed = featured(query_ref, source, pack_ref[0:SHORT, source], agree_ref, start, halo)
+            queries_ref[start : start + ROWS, lanes_at(at)] = summed.astype(BF16)
+
+        return [
+            lambda tile=tile, start=start: one(tile, start)
+            for tile in range(2) for start in range(0, tokens, ROWS)
+        ]
+
+    def work(step, mats_ref):
+        return filter_jobs(
+            step, first, gated_ref, pack_ref, middle_ref, mats_ref, causal_ref, follow_ref,
+            local_ref, onward_ref,
+        )
+
+    chunks = channels // WIDE
+    weave(lag_jobs(0, first, taps_ref, mats_a))
+
+    @pl.loop(0, chunks // 2)
+    def _(pair):
+        step = pair * 2
+        weave(work(step, mats_a), lag_jobs(step + 1, first, taps_ref, mats_b), query_jobs(step))
+        after = jnp.minimum(step + 2, chunks - 1)
+        weave(work(step + 1, mats_b), lag_jobs(after, first, taps_ref, mats_a), query_jobs(step + 1))
+
+
+def output_kernel(place_ref, enter_ref, *refs, pieces, chunk):
+    inputs, (out_ref, held_ref, sems) = refs[:-3], refs[-3:]
+    pending = []
+    done = 0
+    for index, (side, first, count) in enumerate(pieces):
+        local_ref, queries_ref, onward_ref = inputs[3 * index : 3 * index + 3]
+        carry_ref, rates_ref = inputs[3 * len(pieces) + 2 * side : 3 * len(pieces) + 2 * side + 2]
+
+        def tile(start):
+            at, source = lanes_at(start), lanes_at(first + start)
+            carry = carry_ref[:, source].astype(F32)
+            for part in range(PARTS):
+                span = slice(part * PART, (part + 1) * PART)
+                if part:
+                    carry = carry * jnp.exp(-rates_ref[:, source] * PART)
+                carried = jnp.dot(
+                    onward_ref[:, at] * enter_ref[span, :], spread(carry), preferred_element_type=F32
+                )
+                mixed = (local_ref[span, at] + carried).astype(BF16).astype(F32)
+                held_ref[span, lanes_at(done + start)] = (
+                    queries_ref[span, at].astype(F32) * mixed
+                ).astype(BF16)
+
+        for begin in range(0, count, chunk):
+
+            def step(number, carried):
+                tile(begin + number * LANES)
+                return carried
+
+            lax.fori_loop(0, chunk // LANES, step, 0, unroll=4)
+            where = pl.multiple_of(place_ref[side] + (first + begin), chunk)
+            copy = pltpu.make_async_copy(
+                held_ref.at[:, done + begin : done + begin + chunk],
+                out_ref.at[:, pl.ds(where, chunk)],
+                sems.at[len(pending)],
+            )
+            copy.start()
+            pending.append(copy)
+        done += count
+    for copy in pending:
+        copy.wait()
+
+
+def ordered(upper, mine, other):
+    mine, other = mine.astype(F32), other.astype(F32)
+    return jnp.where(upper, other, mine), jnp.where(upper, mine, other)
+
+
+def decay(rate, span):
+    return jnp.exp(-rate * span)
+
+
+def pair_kernel(place_ref, weights_ref, kept_ref, got_ref, rate_ref, first_ref, mine_ref, send_ref, *, tokens):
+    first, second = ordered(place_ref[LOW] == 1, kept_ref[...], got_ref[...])
+    first_ref[...] = first
+    ends = second + weights_ref[PAIR_PASS] * decay(rate_ref[...], tokens) * first
+    half = ends.shape[1] // 2
+    mine, send = ordered(place_ref[HIGH] == 1, ends[:, :half], ends[:, half:])
+    mine_ref[...] = mine
+    send_ref[...] = send.astype(BF16)
+
+
+def narrowed(place_ref, rate_ref):
+    half = rate_ref.shape[1] // 2
+    return jnp.where(place_ref[HIGH] == 1, rate_ref[:, half:], rate_ref[:, :half])
+
+
+def quad_kernel(place_ref, weights_ref, mine_ref, got_ref, rate_ref, lower_ref, total_ref, send_ref, *, tokens):
+    lower, upper = ordered(place_ref[HIGH] == 1, mine_ref[...], got_ref[...])
+    rate = narrowed(place_ref, rate_ref)
+    lower_ref[...] = lower
+    total = upper + weights_ref[QUAD_PASS] * decay(rate, 2 * tokens) * lower
+    total_ref[...] = total
+    send_ref[...] = total.astype(BF16)
+
+
+def round_kernel(place_ref, weights_ref, total_ref, got_ref, rate_ref, *refs, tokens, number, last):
+    rate = narrowed(place_ref, rate_ref)
+    got = got_ref[...].astype(F32)
+    at = ROUNDS + 3 * number
+    carry = weights_ref[at] * decay(rate, weights_ref[at + 1]) * got
+    if number:
+        carry, refs = refs[0][...] + carry, refs[1:]
+    if not last:
+        carry_ref, sum_ref, send_ref = refs
+        carry_ref[...] = carry
+        before, after = ordered(place_ref[UPSIDES + number] == 1, total_ref[...], got)
+        total = after + weights_ref[at + 2] * decay(rate, (4 << number) * tokens) * before
+        sum_ref[...] = total
+        send_ref[...] = total.astype(BF16)
+        return
+    lower_ref, keep_ref, send_ref = refs
+    ahead = lower_ref[...] + weights_ref[QUAD_FROM] * decay(rate, 2 * tokens) * carry
+    keep, send = ordered(place_ref[HIGH] == 1, carry, ahead)
+    keep_ref[...] = keep
+    send_ref[...] = send.astype(BF16)
+
+
+def back_kernel(place_ref, weights_ref, mine_ref, got_ref, rate_ref, first_ref, keep_ref, send_ref, *, tokens):
+    carry = jnp.concatenate(ordered(place_ref[HIGH] == 1, mine_ref[...], got_ref[...]), axis=1)
+    ahead = first_ref[...] + weights_ref[PAIR_FROM] * decay(rate_ref[...], tokens) * carry
+    keep, send = ordered(place_ref[LOW] == 1, carry, ahead)
+    keep_ref[...] = keep.astype(BF16)
+    send_ref[...] = send.astype(BF16)
+
+
+def params(mebibytes=20):
+    return pltpu.CompilerParams(vmem_limit_bytes=mebibytes * 1024 * 1024)
+
+
+def cost(flops, size):
+    return pl.CostEstimate(flops=flops, bytes_accessed=size, transcendentals=0)
+
+
+def shaped(shape, dtype):
+    return jax.ShapeDtypeStruct(shape, dtype)
+
+
+def small_call(kernel, name, place, weights, *operands, outs, tokens_before=(), **static):
+    waits = len(tokens_before)
+    return pl.pallas_call(
+        lambda *refs: kernel(*refs[waits:], **static),
+        in_specs=[ANY] * waits + [SMEM, SMEM] + [VMEM] * len(operands),
+        out_specs=[VMEM] * len(outs),
+        out_shape=outs,
+        compiler_params=params(),
+        cost_estimate=cost(1 << 18, 1 << 18),
+        name=name,
+    )(*tokens_before, place, weights, *operands)
+
+
+def placing(segments, weights, streams, devices, fsdp_count):
+    _, tokens, channels = streams.shape
+    marks = segments.reshape(-1, LANES)
+    short, skip, rates, residues = weights
+    owned = short.shape[2]
+    arrays = (marks, short, skip.reshape(1, owned), rates.T, residues.T)
+
+    def whole(array):
+        return pl.BlockSpec(array.shape, lambda i: (0,) * len(array.shape))
+
+    outs = [
+        shaped((16,), jnp.int32),
+        shaped((32,), F32),
+        shaped((SHORT - 1, tokens, LANES), F32),
+        shaped((PARTS, PART, WIDE), BF16),
+        shaped((PART, LANES), BF16),
+        shaped((tokens, LANES), BF16),
+        shaped((PARTS, LANES, PART), BF16),
+        shaped((PACKED, owned), F32),
+        shaped((3, SHORT - 1, channels), BF16),
+    ]
+    return pl.pallas_call(
+        lambda *refs: place_kernel(*refs, devices=devices, tokens=tokens, fsdp_count=fsdp_count),
+        grid=(1,),
+        in_specs=[SMEM] + [whole(array) for array in arrays] + [HBM],
+        out_specs=[SMEM, SMEM] + [whole(out) for out in outs[2:]],
+        out_shape=outs,
+        scratch_shapes=[pltpu.VMEM((3, 16, channels), BF16), pltpu.SemaphoreType.DMA],
+        compiler_params=params(54),
+        cost_estimate=cost(1 << 20, 1 << 20),
+        name="placing",
+    )(marks, *arrays, streams)
+
+
+def lags(place, streams, pack, side, name):
+    _, tokens, _ = streams.shape
+    channels = pack.shape[1]
+    outs = [shaped((channels // GROUP, PART), F32), shaped((channels, PART), BF16)]
+    operands, specs, scratch = [pack], [VMEM], []
+    if side == OWN:
+        outs += [shaped((tokens, channels), BF16)] * 2
+        operands, specs = [place, streams, pack], [SMEM, HBM, VMEM]
+        scratch = [pltpu.SemaphoreType.DMA((2 * COPIES,))]
+    return pl.pallas_call(
+        lambda *refs: lag_kernel(*refs, side=side),
+        in_specs=specs,
+        out_specs=[VMEM] * len(outs),
+        out_shape=outs,
+        scratch_shapes=scratch,
+        compiler_params=params(46 if side == OWN else 20),
+        cost_estimate=cost(10 * channels * PART, 16 * channels * PART),
+        name="lags_" + name,
+    )(*operands)
+
+
+def block_states(place, weights, streams, operands, side, passing, name):
+    _, tokens, _ = streams.shape
+    channels = operands[0].shape[1]
+    outs = [
+        shaped((tokens, channels), BF16),
+        shaped((tokens, channels), BF16),
+        shaped((MODES, channels), BF16),
+        shaped((MODES, channels), F32),
+        shaped((MODES, channels), F32),
+    ]
+    if side == OWN:
+        outs += [shaped((tokens, channels), BF16)] * 2
+    return pl.pallas_call(
+        lambda *refs: state_kernel(*refs, side=side, passing=passing),
+        in_specs=[SMEM, SMEM, HBM] + [VMEM] * len(operands),
+        out_specs=[VMEM] * len(outs),
+        out_shape=outs,
+        scratch_shapes=[pltpu.SemaphoreType.DMA((3 * COPIES,))],
+        compiler_params=params(40),
+        cost_estimate=cost(20 * tokens * channels, 16 * tokens * channels),
+        name="block_states_" + name,
+    )(place, weights, streams, *operands)
+
+
+def block_local(place, operands, after, side, first, count, name):
+    tokens = operands[0].shape[0]
+    return pl.pallas_call(
+        lambda *refs: local_kernel(*refs, side=side, first=first),
+        in_specs=[SMEM] + [VMEM] * len(operands) + [ANY],
+        out_specs=[VMEM] * 4,
+        out_shape=[
+            shaped((tokens, count), F32),
+            shaped((tokens, count), BF16),
+            shaped((PART, count), BF16),
+            shaped((8, LANES), F32),
+        ],
+        scratch_shapes=[
+            pltpu.VMEM((WIDE // GROUP // 2, PART, WIDE), BF16),
+            pltpu.VMEM((WIDE // GROUP // 2, PART, WIDE), BF16),
+        ],
+        compiler_params=params(),
+        cost_estimate=cost(2 * PART * PART * 2 * count * TILE_GROUPS, 40 * tokens * count),
+        name="block_local_" + name,
+    )(place, *operands, after)
+
+
+def block_output(place, enter, pieces, locals_, carries, tokens, channels):
+    chunk = 1024
+    return pl.pallas_call(
+        lambda *refs: output_kernel(*refs, pieces=pieces, chunk=chunk),
+        in_specs=[SMEM] + [VMEM] * (1 + len(locals_) + len(carries)),
+        out_specs=HBM,
+        out_shape=shaped((tokens, channels), BF16),
+        scratch_shapes=[
+            pltpu.VMEM((tokens, channels), BF16),
+            pltpu.SemaphoreType.DMA((channels // chunk,)),
+        ],
+        compiler_params=params(),
+        cost_estimate=cost(20 * tokens * channels, 8 * tokens * channels),
+        name="block_output",
+    )(place, enter, *locals_, *carries)
+
+
 SPAN = 8
 
 
@@ -70,7 +714,7 @@
     return (jnp.concatenate(pieces, axis=0), carried)
 
 
-def local(streams, segments, short_taps, decay_rates, residues, skip_gain):
+def narrow_local(streams, segments, short_taps, decay_rates, residues, skip_gain):
     fsdp_count = lax.axis_size("fsdp")
     ctx_count = lax.axis_size("ctx")
     tile_index = lax.axis_index("ctx")
@@ -132,6 +776,92 @@
     return returned
 
 
+def swap(array, distance, devices):
+    route = [(i, i ^ distance) for i in range(devices)]
+    return lax.ppermute(array, ("ctx", "fsdp"), route)
+
+
+def carry_in(place, weights, sent, kept, rate, devices, tokens, beside):
+    full, half = kept.shape, (kept.shape[0], kept.shape[1] // 2)
+    wide, narrow, lean = shaped(full, F32), shaped(half, F32), shaped(half, BF16)
+
+    def call(kernel, name, send, distance, *operands, outs, **static):
+        got = swap(send, distance, devices)
+        return small_call(
+            kernel, name, place, weights, operands[0], got, rate, *operands[1:], outs=outs, tokens=tokens,
+            tokens_before=beside(name, send), **static,
+        )
+
+    first, mine, send = call(pair_kernel, "pairs", sent, 1, kept, outs=[wide, narrow, lean])
+    lower, total, send = call(quad_kernel, "quads", send, 2, mine, outs=[narrow, narrow, lean])
+    carry, number, size = [], 0, 4
+    while size < devices:
+        name = "round" + str(number)
+        if 2 * size < devices:
+            held, total, send = call(
+                round_kernel, name, send, size, total, *carry, outs=[narrow, narrow, lean],
+                number=number, last=False,
+            )
+            carry = [held]
+        else:
+            keep, send = call(
+                round_kernel, name, send, size, total, *carry, lower, outs=[narrow, lean],
+                number=number, last=True,
+            )
+        size, number = 2 * size, number + 1
+    full_lean = shaped(full, BF16)
+    keep, send = call(back_kernel, "back", send, 2, keep, first, outs=[full_lean, full_lean])
+    beside("end", send)
+    return swap(send, 1, devices), keep
+
+
+def local(streams, segments, short_taps, decay_rates, residues, skip_gain):
+    fsdp_count, ctx_count = lax.axis_size("fsdp"), lax.axis_size("ctx")
+    devices = fsdp_count * ctx_count
+    _, tokens, channels = streams.shape
+    if tokens != PARTS * PART or fsdp_count != 2 or devices < 8:
+        return narrow_local(streams, segments, short_taps, decay_rates, residues, skip_gain)
+    owned = short_taps.shape[2]
+    place, weights, agree, causal, follow, enter, chosen, own_pack, tail = placing(
+        segments, (short_taps, skip_gain, decay_rates, residues), streams, devices, fsdp_count
+    )
+    halo = lax.ppermute(tail, ("ctx", "fsdp"), [(i, i + 1) for i in range(devices - 1)])
+    other_pack = lax.ppermute(own_pack, "fsdp", [(0, 1), (1, 0)])
+    passing = ROUNDS + 3 * ((devices // 4).bit_length() - 1)
+    found, brought = [], ()
+    for side, (name, pack) in enumerate((("own", own_pack), ("other", other_pack))):
+        taps, fall, *loaded = lags(place, streams, pack, side, name)
+        brought = loaded or brought
+        gated, query, state, middle, spread_rates, *brought = block_states(
+            place, weights, streams, (*brought, halo, pack, fall, agree, chosen), side, passing, name
+        )
+        operands = (query, halo, gated, pack, taps, middle, agree, causal, follow)
+        found.append((operands, state, spread_rates))
+    span = owned // 2
+    pieces = [(side, first, span) for side in (OWN, OTHER) for first in range(0, owned, span)]
+    beside_rounds = {"round0": 1, "round1": 1, "round2": 1}
+    waiting, locals_ = list(pieces), []
+
+    def beside(name, array):
+        count = len(waiting) if name == "end" else beside_rounds.get(name, 0)
+        given = []
+        for _ in range(min(count, len(waiting))):
+            side, first, size = waiting.pop(0)
+            label = "own" if side == OWN else "other"
+            *made, token = block_local(
+                place, found[side][0], array, side, first, size, label + str(first // size)
+            )
+            locals_.extend(made)
+            given.append(token)
+        return given
+
+    carries = carry_in(
+        place, weights, found[0][1], found[1][1], found[1][2], devices, tokens, beside
+    )
+    sides = [carries[0], found[0][2], carries[1], found[1][2]]
+    return block_output(place, enter, pieces, locals_, sides, tokens, channels)
+
+
 def solution(mesh):
     placed = (
         P(None, ("ctx", "fsdp"), None),

time: 1410 us -> 73.9 us (0.05)
  the two profiles are of different devices: /device:TPU:16 before, /device:TPU:0 now
where the time goes in v2:
time: 73.9 us; the launch traced here: 73.6 us
  Pallas kernels  54.1 us (73%)
  starting transfers between devices  13.5 us (18%)
  local copies, waits for them, and re-layouts  2.95 us (4%)
  waiting for transfers between devices  2.81 us (4%)
    pallas_call x4, Pallas kernels, block_local(): pl.pallas_call(lambda *refs: local_kernel(*refs, side=side, first=first),...  23.9 us
    pallas_call x2, Pallas kernels, block_states(): pl.pallas_call(lambda *refs: state_kernel(*refs, side=side, passing=passi...  12.8 us
    ppermute x7, starting transfers between devices, swap(): return lax.ppermute(array, ('ctx', 'fsdp'), route)  8.57 us
    pallas_call x1, Pallas kernels, block_output(): pl.pallas_call(lambda *refs: output_kernel(*refs, pieces=pieces, chunk=ch...  5.46 us
    pallas_call x2, Pallas kernels, lags(): pl.pallas_call(lambda *refs: lag_kernel(*refs, side=side), in_specs=specs...  4.52 us
    pallas_call x6, Pallas kernels, small_call(): pl.pallas_call(lambda *refs: kernel(*refs[waits:], **static), in_specs=[A...  3.81 us
    pallas_call x1, Pallas kernels, placing(): pl.pallas_call(lambda *refs: place_kernel(*refs, devices=devices, tokens=...  3.64 us
    ppermute x1, starting transfers between devices, local(): other_pack = lax.ppermute(own_pack, 'fsdp', [(0, 1), (1, 0)])  3.03 us
  transfers between devices with their start and end apart: 9, of which 3 were waited for; matrix products, arithmetic and copies ran while one was open for 0% of the time, Pallas kernels for 56%

profile of v2, /device:TPU:0, one launch (start us, length us, event | category | flops | bytes accessed | tf_op | source)
XLA Modules:
  0.0 73.6 jit_solution(17363527031236071693)
XLA Ops:
  0.0 3.6 %placing.1 = (s32[16]{0:T(128)}, f32[32]{0:T(128)}, f32[2,256,128]{2,1,0:T(8,128)}, bf16[2,128,256]{2,1,0:T(8,128)(2,1)}, bf16[128,128]{1,0:T(8,128)(2,1)}, /*in...) custom-call(s32[64,128]{1,0:T(8,128)} %bitcast.4, ...), custom_call_target="tpu_custom_call" | custom-call | flops 1048576 | bytes 1048576 | tf_op jit(solution)/shard_map/placing/pallas_call | solution.py:556
  3.7 3.0 %collective-permute-start.1 = (f32[16,4096]{1,0:T(8,128)}, f32[16,4096]{1,0:T(8,128)S(1)}, u32[]{:S(2)}, u32[]{:S(2)}) collective-permute-start(f32[16,4096]{1,0:T(8,128)} %get-tuple-element.66.refs_2_.refs_6_.refs_4_), channel_id=1, source_target_pairs={{0,1},{1,0},{2,3},{3,2},{4,5},{5,4},{6,7},{7,6},{8,9},{9,8},{10,11... | collective-permute-start | bytes 786440 | tf_op jit(solution)/shard_map/ppermute | solution.py:829
  6.7 1.9 %collective-permute-start = (bf16[3,2,8192]{2,1,0:T(2,128)(2,1)}, bf16[3,2,8192]{2,1,0:T(2,128)(2,1)S(1)}, u32[]{:S(2)}, u32[]{:S(2)}) collective-permute-start(bf16[3,2,8192]{2,1,0:T(2,128)(2,1)} %get-tuple-element.69), channel_id=1, source_target_pairs={{0,1},{1,2},{2,3},{3,4},{4,5},{5,6},{6,7},{7,8},{8,9},{9,10},{10,1... | collective-permute-start | bytes 294920 | tf_op jit(solution)/shard_map/ppermute | solution.py:828
  8.6 0.0 copy-start.1
  8.6 0.9 %copy-done.1 = f32[16,4096]{1,0:T(8,128)S(1)} copy-done((f32[16,4096]{1,0:T(8,128)S(1)}, f32[16,4096]{1,0:T(8,128)}, u32[]{:S(2)}) %copy-start.1) | copy-done | bytes 262168
  9.6 0.7 copy-done.7
  10.2 2.8 %lags_own.1 = (f32[256,128]{1,0:T(8,128)S(1)}, bf16[4096,128]{1,0:T(8,128)(2,1)S(1)}, bf16[256,4096]{1,0:T(8,128)(2,1)S(1)}, bf16[256,4096]{1,0:T(8,128)(2,1)S(1)}) custom-call(s32[16]{0:T(128)S(1)} %copy-done.7, bf16[3,256,8192]{2,1,0:T(8,128)(2,1)} %refs_2_.5, f32[16,4096]{1,0:T(8,128)S(1)} %copy-done.1), custom_call_target="tpu_custom_call" | custom-call | flops 5242880 | bytes 8388608 | tf_op jit(solution)/shard_map/lags_own/pallas_call | solution.py:578
  13.0 0.0 copy-start.3
  13.0 1.3 %copy-done.3 = bf16[256,4096]{1,0:T(8,128)(2,1)} copy-done((bf16[256,4096]{1,0:T(8,128)(2,1)}, bf16[256,4096]{1,0:T(8,128)(2,1)S(1)}, u32[]{:S(2)}) %copy-start.3) | copy-done | bytes 2097176
  14.3 0.3 collective-permute-done.refs_5_.refs_2_
  14.7 0.0 copy-done
  14.7 0.0 copy-done.6
  14.7 0.0 copy-done.10
  14.7 6.9 %block_states_own.1 = (bf16[256,4096]{1,0:T(8,128)(2,1)S(1)}, bf16[256,4096]{1,0:T(8,128)(2,1)S(1)}, bf16[16,4096]{1,0:T(8,128)(2,1)S(1)}, f32[16,4096]{1,0:T(8,...) custom-call(s32[16]{0:T(128)S(1)} %copy-done.7, f32[32]{0:T(128)S(1)} %copy-done.10, ...), custom_call_target="tpu_custom_call" | custom-call | flops 20971520 | bytes 16777216 | tf_op jit(solution)/shard_map/block_states_own/pallas_call | solution.py:602
  21.6 2.4 %collective-permute-start.2 = (bf16[16,4096]{1,0:T(8,128)(2,1)S(1)}, bf16[16,4096]{1,0:T(8,128)(2,1)S(1)}, u32[]{:S(2)}, u32[]{:S(2)}) collective-permute-start(bf16[16,4096]{1,0:T(8,128)(2,1)S(1)} %get-tuple-element.83), channel_id=1, source_target_pairs={{0,1},{1,0},{2,3},{3,2},{4,5},{5,4},{6,7},{7,6},{8,9},{9,8},{10,11... | collective-permute-start | bytes 393224 | tf_op jit(solution)/shard_map/ppermute | solution.py:781
  24.1 0.0 collective-permute-done.1.refs_0_.refs_6_.refs_4_
  24.1 1.8 %lags_other.1 = (f32[256,128]{1,0:T(8,128)S(1)}, bf16[4096,128]{1,0:T(8,128)(2,1)S(1)}) custom-call(f32[16,4096]{1,0:T(8,128)S(1)} %collective-permute-done.1.refs_0_.refs_6_.refs_4_), custom_call_target="tpu_custom_call" | custom-call | flops 5242880 | bytes 8388608 | tf_op jit(solution)/shard_map/lags_other/pallas_call | solution.py:578
  25.8 0.0 copy-done.8
  25.8 0.0 copy-start.2
  25.9 0.0 copy-start.4
  25.9 5.9 %block_states_other.1 = (bf16[256,4096]{1,0:T(8,128)(2,1)S(1)}, bf16[256,4096]{1,0:T(8,128)(2,1)S(1)}, bf16[16,4096]{1,0:T(8,128)(2,1)S(1)}, f32[16,4096]{1,0:T(8,128)S(1)}, f32[16,4096]{1,0:T(8,128)S(1)}) custom-call(s32[16]{0:T(128)S(1)} %copy-done.8, f32[32]{0:T(128)S(1)} %copy-done.10, bf16[3,256,8192]{2,1,0:T(8,128)(2,1)} %refs_2_.5, ...), custom_call_target="tpu_custom_call" | custom-call | flops 20971520 | bytes 16777216 | tf_op jit(solution)/shard_map/block_states_other/pallas_call | solution.py:602
  31.7 0.0 collective-permute-done.2.refs_3_
  31.8 0.7 pairs.1
  32.4 0.1 collective-permute-start.3
  32.5 1.2 %collective-permute-done.3.refs_3_ = bf16[16,2048]{1,0:T(8,128)(2,1)S(1)} collective-permute-done((bf16[16,2048]{1,0:T(8,128)(2,1)S(1)}, bf16[16,2048]{1,0:T(8,128)(2,1)S(1)}, u32[]{:S(2)}, u32[]{:S(2)}) %collective-permute-start.3) | collective-permute-done | bytes 65568 | tf_op jit(solution)/shard_map/ppermute | solution.py:781
  33.7 0.6 quads.1
  34.3 1.6 %collective-permute-start.4 = (bf16[16,2048]{1,0:T(8,128)(2,1)S(1)}, bf16[16,2048]{1,0:T(8,128)(2,1)S(1)}, u32[]{:S(2)}, u32[]{:S(2)}) collective-permute-start(bf16[16,2048]{1,0:T(8,128)(2,1)S(1)} %get-tuple-element.87.refs_10_), channel_id=1, source_target_pairs={{0,4},{1,5},{2,6},{3,7},{4,0},{5,1},{6,2},{7,3},{8,12},{9,13},{10,... | collective-permute-start | bytes 196616 | tf_op jit(solution)/shard_map/ppermute | solution.py:781
  35.9 0.0 copy-done.4
  35.9 5.8 %block_local_own0.1 = (f32[256,2048]{1,0:T(8,128)S(1)}, bf16[256,2048]{1,0:T(8,128)(2,1)S(1)}, bf16[128,2048]{1,0:T(8,128)(2,1)S(1)}, f32[8,128]{1,0:T(8,128)S(1)}) custom-call(s32[16]{0:T(128)S(1)} %copy-done.8, bf16[256,4096]{1,0:T(8,128)(2,1)S(1)} %get-tuple-element.73.refs_1_, bf16[3,2,8192]{2,1,0:T(2,128)(2,1)S(1)} %collective-permute-done.refs_5_.refs_2_, ...), custom_call_target="tpu_custom_call" | custom-call | flops 1073741824 | bytes 20971520 | tf_op jit(solution)/shard_map/block_local_own0/pallas_call | solution.py:616
  41.7 0.0 collective-permute-done.4.refs_4_
  41.7 0.6 round0.1
  42.3 1.6 %collective-permute-start.5 = (bf16[16,2048]{1,0:T(8,128)(2,1)S(1)}, bf16[16,2048]{1,0:T(8,128)(2,1)S(1)}, u32[]{:S(2)}, u32[]{:S(2)}) collective-permute-start(bf16[16,2048]{1,0:T(8,128)(2,1)S(1)} %get-tuple-element.93.refs_10_), channel_id=1, source_target_pairs={{0,8},{1,9},{2,10},{3,11},{4,12},{5,13},{6,14},{7,15},{8,0},{9,1},... | collective-permute-start | bytes 196616 | tf_op jit(solution)/shard_map/ppermute | solution.py:781
  44.0 5.9 %block_local_own1.1 = (f32[256,2048]{1,0:T(8,128)S(1)}, bf16[256,2048]{1,0:T(8,128)(2,1)S(1)}, bf16[128,2048]{1,0:T(8,128)(2,1)S(1)}, f32[8,128]{1,0:T(8,128)S(1)}) custom-call(s32[16]{0:T(128)S(1)} %copy-done.8, bf16[256,4096]{1,0:T(8,128)(2,1)S(1)} %get-tuple-element.73.refs_1_, bf16[3,2,8192]{2,1,0:T(2,128)(2,1)S(1)} %collective-permute-done.refs_5_.refs_2_, ...), custom_call_target="tpu_custom_call" | custom-call | flops 1073741824 | bytes 20971520 | tf_op jit(solution)/shard_map/block_local_own1/pallas_call | solution.py:616
  49.9 0.0 collective-permute-done.5.refs_4_
  49.9 0.6 round1.1
  50.6 2.6 %collective-permute-start.6 = (bf16[16,2048]{1,0:T(8,128)(2,1)S(1)}, bf16[16,2048]{1,0:T(8,128)(2,1)S(1)}, u32[]{:S(2)}, u32[]{:S(2)}) collective-permute-start(bf16[16,2048]{1,0:T(8,128)(2,1)S(1)} %get-tuple-element.104.refs_10_), channel_id=1, source_target_pairs={{0,16},{1,17},{2,18},{3,19},{4,20},{5,21},{6,22},{7,23},{8,24},{9,... | collective-permute-start | bytes 196616 | tf_op jit(solution)/shard_map/ppermute | solution.py:781
  53.2 5.8 %block_local_other0.1 = (f32[256,2048]{1,0:T(8,128)S(1)}, bf16[256,2048]{1,0:T(8,128)(2,1)S(1)}, bf16[128,2048]{1,0:T(8,128)(2,1)S(1)}, f32[8,128]{1,0:T(8,128)S(1)}) custom-call(s32[16]{0:T(128)S(1)} %copy-done.8, bf16[256,4096]{1,0:T(8,128)(2,1)S(1)} %get-tuple-element.97.refs_1_, bf16[3,2,8192]{2,1,0:T(2,128)(2,1)S(1)} %collective-permute-done.refs_5_.refs_2_, ...), custom_call_target="tpu_custom_call" | custom-call | flops 1073741824 | bytes 20971520 | tf_op jit(solution)/shard_map/block_local_other0/pallas_call | solution.py:616
  59.0 0.0 collective-permute-done.6.refs_4_
  59.0 0.6 round2.1
  59.6 0.1 collective-permute-start.7
  59.7 1.2 %collective-permute-done.7.refs_3_ = bf16[16,2048]{1,0:T(8,128)(2,1)S(1)} collective-permute-done((bf16[16,2048]{1,0:T(8,128)(2,1)S(1)}, bf16[16,2048]{1,0:T(8,128)(2,1)S(1)}, u32[]{:S(2)}, u32[]{:S(2)}) %collective-permute-start.7) | collective-permute-done | bytes 65568 | tf_op jit(solution)/shard_map/ppermute | solution.py:781
  60.9 0.7 back.1
  61.6 0.0 copy-start.9
  61.6 0.1 collective-permute-start.8
  61.7 6.4 %block_local_other1.1 = (f32[256,2048]{1,0:T(8,128)S(1)}, bf16[256,2048]{1,0:T(8,128)(2,1)S(1)}, bf16[128,2048]{1,0:T(8,128)(2,1)S(1)}, f32[8,128]{1,0:T(8,128)}) custom-call(s32[16]{0:T(128)S(1)} %copy-done.8, bf16[256,4096]{1,0:T(8,128)(2,1)S(1)} %get-tuple-element.97.refs_1_, bf16[3,2,8192]{2,1,0:T(2,128)(2,1)S(1)} %collective-permute-done.refs_5_.refs_2_, ...), custom_call_target="tpu_custom_call" | custom-call | flops 1073741824 | bytes 20971520 | tf_op jit(solution)/shard_map/block_local_other1/pallas_call | solution.py:616
  68.1 0.0 collective-permute-done.8.refs_14_
  68.1 0.0 copy-done.9
  68.1 5.5 %block_output.1 = bf16[256,8192]{1,0:T(8,128)(2,1)} custom-call(s32[16]{0:T(128)S(1)} %copy-done.8, bf16[256,128]{1,0:T(8,128)(2,1)S(1)} %copy-done.9, f32[256,2048]{1,0:T(8,128)S(1)} %get-tuple-element.88.refs_2_, bf16[256,2048]{1,0:T(8,128)(2,1)S(1)} %get-tuple-element.89.refs_3_, bf16[128,2048]{1,0:T(8,128)(2,1)S(1)} %get-tuple-element.90.refs_4_, ...), custom_call_target="tpu_custom_call" | custom-call | flops 41943040 | bytes 16777216 | tf_op jit(solution)/shard_map/block_output/pallas_call | solution.py:638
  (8 shorter events, 0.0 us)
Async XLA Ops:
  3.7 20.4 %collective-permute-start.1 = (f32[16,4096]{1,0:T(8,128)}, f32[16,4096]{1,0:T(8,128)S(1)}, u32[]{:S(2)}, u32[]{:S(2)}) collective-permute-start(f32[16,4096]{1,0:T(8,128)} %get-tuple-element.66.refs_2_.refs_6_.refs_4_), channel_id=1, source_target_pairs={{0,1},{1,0},{2,3},{3,2},{4,5},{5,4},{6,7},{7,6},{8,9},{9,8},{10,11... | collective-permute-start | bytes 786440 | tf_op jit(solution)/shard_map/ppermute | solution.py:829
  6.7 8.0 %collective-permute-start = (bf16[3,2,8192]{2,1,0:T(2,128)(2,1)}, bf16[3,2,8192]{2,1,0:T(2,128)(2,1)S(1)}, u32[]{:S(2)}, u32[]{:S(2)}) collective-permute-start(bf16[3,2,8192]{2,1,0:T(2,128)(2,1)} %get-tuple-element.69), channel_id=1, source_target_pairs={{0,1},{1,2},{2,3},{3,4},{4,5},{5,6},{6,7},{7,8},{8,9},{9,10},{10,1... | collective-permute-start | bytes 294920 | tf_op jit(solution)/shard_map/ppermute | solution.py:828
  8.6 1.0 %copy-start.1 = (f32[16,4096]{1,0:T(8,128)S(1)}, f32[16,4096]{1,0:T(8,128)}, u32[]{:S(2)}) copy-start(f32[16,4096]{1,0:T(8,128)} %get-tuple-element.66.refs_2_.refs_6_.refs_4_) | copy-start | bytes 786436
  9.6 0.7 copy-start.7
  10.2 4.4 %copy-start = (f32[2,256,128]{2,1,0:T(8,128)S(1)}, f32[2,256,128]{2,1,0:T(8,128)}, u32[]{:S(2)}) copy-start(f32[2,256,128]{2,1,0:T(8,128)} %get-tuple-element.71.refs_8_.refs_7_) | copy-start | bytes 786436
  10.2 4.4 %copy-start.6 = (bf16[2,128,128]{2,1,0:T(8,128)(2,1)S(1)}, bf16[2,128,128]{2,1,0:T(8,128)(2,1)}, u32[]{:S(2)}) copy-start(bf16[2,128,128]{2,1,0:T(8,128)(2,1)} %get-tuple-element.72.refs_9_) | copy-start | bytes 196612
  10.2 4.4 %copy-start.10 = (f32[32]{0:T(128)S(1)}, f32[32]{0:T(128)}, u32[]{:S(2)}) copy-start(f32[32]{0:T(128)} %get-tuple-element.65.refs_1_.refs_2_) | copy-start | bytes 388
  13.0 1.3 %copy-start.3 = (bf16[256,4096]{1,0:T(8,128)(2,1)}, bf16[256,4096]{1,0:T(8,128)(2,1)S(1)}, u32[]{:S(2)}) copy-start(bf16[256,4096]{1,0:T(8,128)(2,1)S(1)} %get-tuple-element.68.refs_4_) | copy-start | bytes 6291460
  14.7 11.2 %copy-start.8 = (s32[16]{0:T(128)S(1)}, s32[16]{0:T(128)}, u32[]{:S(2)}) copy-start(s32[16]{0:T(128)} %get-tuple-element.63.refs_0_.refs_1_) | copy-start | bytes 196
  21.6 10.1 %collective-permute-start.2 = (bf16[16,4096]{1,0:T(8,128)(2,1)S(1)}, bf16[16,4096]{1,0:T(8,128)(2,1)S(1)}, u32[]{:S(2)}, u32[]{:S(2)}) collective-permute-start(bf16[16,4096]{1,0:T(8,128)(2,1)S(1)} %get-tuple-element.83), channel_id=1, source_target_pairs={{0,1},{1,0},{2,3},{3,2},{4,5},{5,4},{6,7},{7,6},{8,9},{9,8},{10,11... | collective-permute-start | bytes 393224 | tf_op jit(solution)/shard_map/ppermute | solution.py:781
  25.8 10.1 %copy-start.2 = (f32[16,4096]{1,0:T(8,128)S(1)}, f32[16,4096]{1,0:T(8,128)}, u32[]{:S(2)}) copy-start(f32[16,4096]{1,0:T(8,128)} %get-tuple-element.66.refs_2_.refs_6_.refs_4_) | copy-start | bytes 786436
  25.9 10.1 %copy-start.4 = (bf16[2,128,256]{2,1,0:T(8,128)(2,1)S(1)}, bf16[2,128,256]{2,1,0:T(8,128)(2,1)}, u32[]{:S(2)}) copy-start(bf16[2,128,256]{2,1,0:T(8,128)(2,1)} %get-tuple-element.77.refs_8_) | copy-start | bytes 393220
  25.9 10.1 %copy-start.5 = (bf16[128,128]{1,0:T(8,128)(2,1)S(1)}, bf16[128,128]{1,0:T(8,128)(2,1)}, u32[]{:S(2)}) copy-start(bf16[128,128]{1,0:T(8,128)(2,1)} %get-tuple-element.78.refs_9_) | copy-start | bytes 98308
  32.4 1.3 %collective-permute-start.3 = (bf16[16,2048]{1,0:T(8,128)(2,1)S(1)}, bf16[16,2048]{1,0:T(8,128)(2,1)S(1)}, u32[]{:S(2)}, u32[]{:S(2)}) collective-permute-start(bf16[16,2048]{1,0:T(8,128)(2,1)S(1)} %get-tuple-element.86), channel_id=1, source_target_pairs={{0,2},{1,3},{2,0},{3,1},{4,6},{5,7},{6,4},{7,5},{8,10},{9,11},{10,... | collective-permute-start | bytes 196616 | tf_op jit(solution)/shard_map/ppermute | solution.py:781
  34.3 7.4 %collective-permute-start.4 = (bf16[16,2048]{1,0:T(8,128)(2,1)S(1)}, bf16[16,2048]{1,0:T(8,128)(2,1)S(1)}, u32[]{:S(2)}, u32[]{:S(2)}) collective-permute-start(bf16[16,2048]{1,0:T(8,128)(2,1)S(1)} %get-tuple-element.87.refs_10_), channel_id=1, source_target_pairs={{0,4},{1,5},{2,6},{3,7},{4,0},{5,1},{6,2},{7,3},{8,12},{9,13},{10,... | collective-permute-start | bytes 196616 | tf_op jit(solution)/shard_map/ppermute | solution.py:781
  42.3 7.6 %collective-permute-start.5 = (bf16[16,2048]{1,0:T(8,128)(2,1)S(1)}, bf16[16,2048]{1,0:T(8,128)(2,1)S(1)}, u32[]{:S(2)}, u32[]{:S(2)}) collective-permute-start(bf16[16,2048]{1,0:T(8,128)(2,1)S(1)} %get-tuple-element.93.refs_10_), channel_id=1, source_target_pairs={{0,8},{1,9},{2,10},{3,11},{4,12},{5,13},{6,14},{7,15},{8,0},{9,1},... | collective-permute-start | bytes 196616 | tf_op jit(solution)/shard_map/ppermute | solution.py:781
  50.6 8.4 %collective-permute-start.6 = (bf16[16,2048]{1,0:T(8,128)(2,1)S(1)}, bf16[16,2048]{1,0:T(8,128)(2,1)S(1)}, u32[]{:S(2)}, u32[]{:S(2)}) collective-permute-start(bf16[16,2048]{1,0:T(8,128)(2,1)S(1)} %get-tuple-element.104.refs_10_), channel_id=1, source_target_pairs={{0,16},{1,17},{2,18},{3,19},{4,20},{5,21},{6,22},{7,23},{8,24},{9,... | collective-permute-start | bytes 196616 | tf_op jit(solution)/shard_map/ppermute | solution.py:781
  59.6 1.3 %collective-permute-start.7 = (bf16[16,2048]{1,0:T(8,128)(2,1)S(1)}, bf16[16,2048]{1,0:T(8,128)(2,1)S(1)}, u32[]{:S(2)}, u32[]{:S(2)}) collective-permute-start(bf16[16,2048]{1,0:T(8,128)(2,1)S(1)} %get-tuple-element.113), channel_id=1, source_target_pairs={{0,2},{1,3},{2,0},{3,1},{4,6},{5,7},{6,4},{7,5},{8,10},{9,11},{10,... | collective-permute-start | bytes 196616 | tf_op jit(solution)/shard_map/ppermute | solution.py:781
  61.6 6.5 %copy-start.9 = (bf16[256,128]{1,0:T(8,128)(2,1)S(1)}, bf16[256,128]{1,0:T(8,128)(2,1)}, u32[]{:S(2)}) copy-start(bf16[256,128]{1,0:T(8,128)(2,1)} %get-tuple-element.64.refs_1_) | copy-start | bytes 196612
  61.6 6.5 %collective-permute-start.8 = (bf16[16,4096]{1,0:T(8,128)(2,1)S(1)}, bf16[16,4096]{1,0:T(8,128)(2,1)S(1)}, u32[]{:S(2)}, u32[]{:S(2)}) collective-permute-start(bf16[16,4096]{1,0:T(8,128)(2,1)S(1)} %get-tuple-element.115.refs_10_), channel_id=1, source_target_pairs={{0,1},{1,0},{2,3},{3,2},{4,5},{5,4},{6,7},{7,6},{8,9},{9,8},{10,11... | collective-permute-start | bytes 393224 | tf_op jit(solution)/shard_map/ppermute | solution.py:781

commit v3 on v2

--- a/solution.py
+++ b/solution.py
@@ -13,7 +13,7 @@
 PARTS = 2
 WIDE = 256
 COPIES = 4
-TILES = 4
+TILES = 8
 TILE_GROUPS = LANES // GROUP
 ROWS = 64
 LOG2E = 1.4426950408889634
@@ -26,6 +26,7 @@
 SKIP, RATE, GAIN, PACKED = 9, 10, 11, 16
 OWN, OTHER, LOW, HIGH, UPSIDES = 0, 1, 2, 3, 4
 PAIR_PASS, QUAD_PASS, QUAD_FROM, PAIR_FROM, ROUNDS = 0, 1, 2, 3, 4
+ROWS_OF_PLACE, PLACES = 32, 16
 
 
 def iota(shape, axis):
@@ -84,7 +85,17 @@
     return state
 
 
-def pack_weights(short_ref, skip_ref, rates_ref, residues_ref, pack_ref):
+def packing_kernel(*refs):
+    sources, pack_ref, held, sems = refs[1:5], refs[5], refs[6:10], refs[10]
+    short_ref, skip_ref, rates_ref, residues_ref = held
+    copies = [
+        pltpu.make_async_copy(source, target, sems.at[number])
+        for number, (source, target) in enumerate(zip(sources, held))
+    ]
+    for copy in copies:
+        copy.start()
+    for copy in copies:
+        copy.wait()
     for stream in range(3):
         pack_ref[stream * SHORT : (stream + 1) * SHORT, :] = short_ref[stream]
     pack_ref[SKIP : SKIP + 1, :] = skip_ref[...]
@@ -110,17 +121,17 @@
 
 
 def place_kernel(
-    spots_ref, marks_ref, short_ref, skip_ref, rates_ref, residues_ref, x_ref,
-    place_ref, weights_ref, agree_ref, causal_ref, follow_ref, enter_ref, chosen_ref, pack_ref, tail_ref,
-    ends_ref, sem, *, devices, tokens, fsdp_count,
+    x_ref, spots_ref, marks_ref,
+    place_ref, weights_ref, rows_ref, agree_ref, causal_ref, follow_ref, enter_ref, chosen_ref, keys_ref,
+    held_ref, sem, moves, *, devices, tokens, fsdp_count,
 ):
-    owned = pack_ref.shape[1]
+    copy = pltpu.make_async_copy(marks_ref, held_ref, sem)
+    copy.start()
+    owned = keys_ref.shape[1]
     lines = tokens // LANES
-    tail = pltpu.make_async_copy(x_ref.at[:, pl.ds(tokens - 16, 16), :], ends_ref, sem)
-    tail.start()
-    pack_weights(short_ref, skip_ref, rates_ref, residues_ref, pack_ref)
     fsdp_index = lax.axis_index("fsdp")
     block = lax.axis_index("ctx") * fsdp_count + fsdp_index
+    brought = start_copies(x_ref, fsdp_index * owned, ((1, keys_ref),), moves)
     place_ref[OWN] = fsdp_index * owned
     place_ref[OTHER] = (1 - fsdp_index) * owned
     place_ref[LOW] = lax.rem(block, 2)
@@ -150,9 +161,11 @@
         weights_ref[at + 2] = passes(middle, middle + size)
         size, number = 2 * size, number + 1
 
+    copy.wait()
+
     def marks_of(index):
         return jnp.concatenate(
-            [marks_ref[pl.ds(index * lines + line, 1), :] for line in range(lines)], axis=1
+            [held_ref[pl.ds(index * lines + line, 1), :] for line in range(lines)], axis=1
         ).astype(F32)
 
     marks = marks_of(block)
@@ -173,9 +186,15 @@
     enter_ref[...] = flag(column == before[:, tokens - 1 :]).astype(BF16)
     inside = spots_ref[block * lines + PART // LANES - 1, LANES - 1] == end_of(block)
     weights_ref[ROUNDS + 3 * number] = jnp.where(inside, 1.0, 0.0)
-    tail.wait()
-    for stream in range(3):
-        tail_ref[stream] = ends_ref[stream, 16 - (SHORT - 1) :, :]
+    for spare in range(ROUNDS + 3 * number + 1, ROWS_OF_PLACE):
+        weights_ref[spare] = 0.0
+    for spare in range(UPSIDES + number, PLACES):
+        place_ref[spare] = 0
+    for number in range(rows_ref.shape[0]):
+        value = weights_ref[number] if number < ROWS_OF_PLACE else place_ref[number - ROWS_OF_PLACE].astype(F32)
+        rows_ref[number : number + 1, :] = jnp.full((1, LANES), value, F32)
+    for copy in brought:
+        copy.wait()
 
 
 def start_copies(x_ref, origin, moves, sems):
@@ -195,8 +214,8 @@
 def lag_kernel(*refs, side):
     copies = []
     if side == OWN:
-        place_ref, x_ref, pack_ref, taps_ref, fall_ref, keys_ref, values_ref, sems = refs
-        copies = start_copies(x_ref, place_ref[OWN], ((1, keys_ref), (2, values_ref)), sems)
+        place_ref, x_ref, pack_ref, taps_ref, fall_ref, values_ref, sems = refs
+        copies = start_copies(x_ref, place_ref[OWN], ((2, values_ref),), sems)
     else:
         pack_ref, taps_ref, fall_ref = refs
     left = (PART - 1 - iota((LANES, PART), 1)).astype(F32)
@@ -222,9 +241,7 @@
     tokens, channels = gated_ref.shape
     copies = start_copies(x_ref, place_ref[side], ((0, query_ref),), rest[-1])
     if side == OWN:
-        copies += start_copies(
-            x_ref, place_ref[OTHER], ((1, rest[0]), (2, rest[1])), rest[-1].at[pl.ds(COPIES, 2 * COPIES)]
-        )
+        copies += start_copies(x_ref, place_ref[OTHER], ((1, rest[0]), (2, rest[1])), rest[2])
     origin = place_ref[side]
     shape = (MODES, LANES)
     index = iota(shape, 1) // GROUP * GROUP + iota(shape, 0)
@@ -310,7 +327,7 @@
     local_ref, onward_ref,
 ):
     held = {}
-    odd = iota((16, LANES), 1) // GROUP % 2
+    odd = iota((16, WIDE), 1) // GROUP % 2
     keep = [jnp.concatenate([flag(odd == i).astype(BF16)] * (PART // 16), axis=0) for i in (0, 1)]
     own = iota((1, LANES), 1) // (2 * GROUP)
 
@@ -323,17 +340,19 @@
     def span(part):
         return slice(part * PART, (part + 1) * PART)
 
-    def inner(part, tile):
-        values = gated_ref[span(part), source(tile)]
+    def inner(part):
+        values = gated_ref[span(part), lanes_at(first + step * WIDE, WIDE)]
         right = jnp.concatenate([values * keep[0], values * keep[1]], axis=0)
-        left = jnp.concatenate([mats_ref[tile * 4 + i] * causal_ref[part] for i in range(4)], axis=0)
-        held["full", part, tile] = jnp.dot(left, right, preferred_element_type=F32)
+        for pair in range(WIDE // GROUP // 2):
+            held["full", part, pair] = jnp.dot(
+                mats_ref[pair] * causal_ref[part], right, preferred_element_type=F32
+            )
 
     def pick(part, tile):
-        full = held["full", part, tile]
-        value = full[:PART]
-        for i in range(1, 4):
-            value = jnp.where(own == i, full[i * PART : (i + 1) * PART], value)
+        value = None
+        for i in range(4):
+            piece = held["full", part, tile * 4 + i][:, tile * LANES : (tile + 1) * LANES]
+            value = piece if value is None else jnp.where(own == i, piece, value)
         held[part, tile] = value
 
     def carry(tile):
@@ -354,10 +373,9 @@
         local_ref[span(part), target(tile)] = value
 
     return [
-        lambda: carry(0), lambda: inner(0, 0), lambda: carry(1), lambda: inner(1, 0),
-        lambda: pick(0, 0), lambda: finish(0, 0), lambda: inner(0, 1), lambda: pick(1, 0),
-        lambda: finish(1, 0), lambda: inner(1, 1), lambda: pick(0, 1), lambda: finish(0, 1),
-        lambda: pick(1, 1), lambda: finish(1, 1),
+        lambda: carry(0), lambda: inner(0), lambda: carry(1), lambda: inner(1),
+        lambda: pick(0, 0), lambda: finish(0, 0), lambda: pick(1, 0), lambda: finish(1, 0),
+        lambda: pick(0, 1), lambda: finish(0, 1), lambda: pick(1, 1), lambda: finish(1, 1),
     ]
 
 
@@ -453,56 +471,51 @@
     return jnp.exp(-rate * span)
 
 
-def pair_kernel(place_ref, weights_ref, kept_ref, got_ref, rate_ref, first_ref, mine_ref, send_ref, *, tokens):
-    first, second = ordered(place_ref[LOW] == 1, kept_ref[...], got_ref[...])
+def weight(flags_ref, index):
+    return flags_ref[index : index + 1, 0:1]
+
+
+def above(flags_ref, index, like):
+    row = weight(flags_ref, ROWS_OF_PLACE + index)
+    return jnp.broadcast_to(row, like.shape) > 0.5
+
+
+def pair_kernel(flags_ref, kept_ref, got_ref, rate_ref, first_ref, ends_ref, send_ref, *, tokens):
+    first, second = ordered(above(flags_ref, LOW, kept_ref), kept_ref[...], got_ref[...])
     first_ref[...] = first
-    ends = second + weights_ref[PAIR_PASS] * decay(rate_ref[...], tokens) * first
-    half = ends.shape[1] // 2
-    mine, send = ordered(place_ref[HIGH] == 1, ends[:, :half], ends[:, half:])
-    mine_ref[...] = mine
-    send_ref[...] = send.astype(BF16)
-
-
-def narrowed(place_ref, rate_ref):
-    half = rate_ref.shape[1] // 2
-    return jnp.where(place_ref[HIGH] == 1, rate_ref[:, half:], rate_ref[:, :half])
-
-
-def quad_kernel(place_ref, weights_ref, mine_ref, got_ref, rate_ref, lower_ref, total_ref, send_ref, *, tokens):
-    lower, upper = ordered(place_ref[HIGH] == 1, mine_ref[...], got_ref[...])
-    rate = narrowed(place_ref, rate_ref)
+    ends = second + weight(flags_ref, PAIR_PASS) * decay(rate_ref[...], tokens) * first
+    ends_ref[...] = ends
+    send_ref[...] = ends.astype(BF16)
+
+
+def quad_kernel(flags_ref, mine_ref, got_ref, rate_ref, lower_ref, total_ref, send_ref, *, tokens):
+    lower, upper = ordered(above(flags_ref, HIGH, mine_ref), mine_ref[...], got_ref[...])
     lower_ref[...] = lower
-    total = upper + weights_ref[QUAD_PASS] * decay(rate, 2 * tokens) * lower
+    total = upper + weight(flags_ref, QUAD_PASS) * decay(rate_ref[...], 2 * tokens) * lower
     total_ref[...] = total
     send_ref[...] = total.astype(BF16)
 
 
-def round_kernel(place_ref, weights_ref, total_ref, got_ref, rate_ref, *refs, tokens, number, last):
-    rate = narrowed(place_ref, rate_ref)
+def round_kernel(flags_ref, total_ref, got_ref, rate_ref, *refs, tokens, number, last):
+    rate = rate_ref[...]
     got = got_ref[...].astype(F32)
     at = ROUNDS + 3 * number
-    carry = weights_ref[at] * decay(rate, weights_ref[at + 1]) * got
+    carry = weight(flags_ref, at) * decay(rate, weight(flags_ref, at + 1)) * got
     if number:
         carry, refs = refs[0][...] + carry, refs[1:]
     if not last:
         carry_ref, sum_ref, send_ref = refs
         carry_ref[...] = carry
-        before, after = ordered(place_ref[UPSIDES + number] == 1, total_ref[...], got)
-        total = after + weights_ref[at + 2] * decay(rate, (4 << number) * tokens) * before
+        before, after = ordered(above(flags_ref, UPSIDES + number, rate), total_ref[...], got)
+        total = after + weight(flags_ref, at + 2) * decay(rate, (4 << number) * tokens) * before
         sum_ref[...] = total
         send_ref[...] = total.astype(BF16)
         return
-    lower_ref, keep_ref, send_ref = refs
-    ahead = lower_ref[...] + weights_ref[QUAD_FROM] * decay(rate, 2 * tokens) * carry
-    keep, send = ordered(place_ref[HIGH] == 1, carry, ahead)
-    keep_ref[...] = keep
-    send_ref[...] = send.astype(BF16)
-
-
-def back_kernel(place_ref, weights_ref, mine_ref, got_ref, rate_ref, first_ref, keep_ref, send_ref, *, tokens):
-    carry = jnp.concatenate(ordered(place_ref[HIGH] == 1, mine_ref[...], got_ref[...]), axis=1)
-    ahead = first_ref[...] + weights_ref[PAIR_FROM] * decay(rate_ref[...], tokens) * carry
-    keep, send = ordered(place_ref[LOW] == 1, carry, ahead)
+    lower_ref, first_ref, keep_ref, send_ref = refs
+    ahead = lower_ref[...] + weight(flags_ref, QUAD_FROM) * decay(rate, 2 * tokens) * carry
+    carry = jnp.where(above(flags_ref, HIGH, carry), ahead, carry)
+    ahead = first_ref[...] + weight(flags_ref, PAIR_FROM) * decay(rate, tokens) * carry
+    keep, send = ordered(above(flags_ref, LOW, carry), carry, ahead)
     keep_ref[...] = keep.astype(BF16)
     send_ref[...] = send.astype(BF16)
 
@@ -519,51 +532,65 @@
     return jax.ShapeDtypeStruct(shape, dtype)
 
 
-def small_call(kernel, name, place, weights, *operands, outs, tokens_before=(), **static):
+def small_call(kernel, name, flags, *operands, outs, tokens_before=(), **static):
     waits = len(tokens_before)
     return pl.pallas_call(
         lambda *refs: kernel(*refs[waits:], **static),
-        in_specs=[ANY] * waits + [SMEM, SMEM] + [VMEM] * len(operands),
+        in_specs=[ANY] * waits + [VMEM] * (1 + len(operands)),
         out_specs=[VMEM] * len(outs),
         out_shape=outs,
         compiler_params=params(),
         cost_estimate=cost(1 << 18, 1 << 18),
         name=name,
-    )(*tokens_before, place, weights, *operands)
-
-
-def placing(segments, weights, streams, devices, fsdp_count):
-    _, tokens, channels = streams.shape
-    marks = segments.reshape(-1, LANES)
+    )(*tokens_before, flags, *operands)
+
+
+def packing(weights, after):
     short, skip, rates, residues = weights
     owned = short.shape[2]
-    arrays = (marks, short, skip.reshape(1, owned), rates.T, residues.T)
-
-    def whole(array):
-        return pl.BlockSpec(array.shape, lambda i: (0,) * len(array.shape))
-
+    arrays = (short, skip.reshape(1, owned), rates.T, residues.T)
+    arrays = [pltpu.with_memory_space_constraint(array, pltpu.HBM) for array in arrays]
+    return pl.pallas_call(
+        packing_kernel,
+        in_specs=[ANY] + [HBM] * len(arrays),
+        out_specs=VMEM,
+        out_shape=shaped((PACKED, owned), F32),
+        scratch_shapes=[pltpu.VMEM(array.shape, array.dtype) for array in arrays]
+        + [pltpu.SemaphoreType.DMA((len(arrays),))],
+        compiler_params=params(),
+        cost_estimate=cost(1024, 1024),
+        name="packing",
+    )(after, *arrays)
+
+
+def placing(segments, streams, owned, devices, fsdp_count):
+    tokens = segments.shape[0] // devices
+    marks = segments.reshape(-1, LANES)
     outs = [
-        shaped((16,), jnp.int32),
-        shaped((32,), F32),
+        shaped((PLACES,), jnp.int32),
+        shaped((ROWS_OF_PLACE,), F32),
+        shaped((ROWS_OF_PLACE + PLACES, LANES), F32),
         shaped((SHORT - 1, tokens, LANES), F32),
         shaped((PARTS, PART, WIDE), BF16),
         shaped((PART, LANES), BF16),
         shaped((tokens, LANES), BF16),
         shaped((PARTS, LANES, PART), BF16),
-        shaped((PACKED, owned), F32),
-        shaped((3, SHORT - 1, channels), BF16),
+        shaped((tokens, owned), BF16),
     ]
     return pl.pallas_call(
         lambda *refs: place_kernel(*refs, devices=devices, tokens=tokens, fsdp_count=fsdp_count),
-        grid=(1,),
-        in_specs=[SMEM] + [whole(array) for array in arrays] + [HBM],
-        out_specs=[SMEM, SMEM] + [whole(out) for out in outs[2:]],
+        in_specs=[HBM, SMEM, HBM],
+        out_specs=[SMEM, SMEM] + [VMEM] * (len(outs) - 2),
         out_shape=outs,
-        scratch_shapes=[pltpu.VMEM((3, 16, channels), BF16), pltpu.SemaphoreType.DMA],
-        compiler_params=params(54),
-        cost_estimate=cost(1 << 20, 1 << 20),
+        scratch_shapes=[
+            pltpu.VMEM(marks.shape, marks.dtype),
+            pltpu.SemaphoreType.DMA,
+            pltpu.SemaphoreType.DMA((COPIES,)),
+        ],
+        compiler_params=params(),
+        cost_estimate=cost(1024, 1024),
         name="placing",
-    )(marks, *arrays, streams)
+    )(streams, marks, pltpu.with_memory_space_constraint(marks, pltpu.HBM))
 
 
 def lags(place, streams, pack, side, name):
@@ -572,17 +599,17 @@
     outs = [shaped((channels // GROUP, PART), F32), shaped((channels, PART), BF16)]
     operands, specs, scratch = [pack], [VMEM], []
     if side == OWN:
-        outs += [shaped((tokens, channels), BF16)] * 2
         operands, specs = [place, streams, pack], [SMEM, HBM, VMEM]
-        scratch = [pltpu.SemaphoreType.DMA((2 * COPIES,))]
+        outs.append(shaped((tokens, channels), BF16))
+        scratch.append(pltpu.SemaphoreType.DMA((COPIES,)))
     return pl.pallas_call(
         lambda *refs: lag_kernel(*refs, side=side),
         in_specs=specs,
         out_specs=[VMEM] * len(outs),
         out_shape=outs,
         scratch_shapes=scratch,
-        compiler_params=params(46 if side == OWN else 20),
-        cost_estimate=cost(10 * channels * PART, 16 * channels * PART),
+        compiler_params=params(),
+        cost_estimate=cost(1024, 1024),
         name="lags_" + name,
     )(*operands)
 
@@ -597,15 +624,17 @@
         shaped((MODES, channels), F32),
         shaped((MODES, channels), F32),
     ]
+    scratch = [pltpu.SemaphoreType.DMA((COPIES,))]
     if side == OWN:
         outs += [shaped((tokens, channels), BF16)] * 2
+        scratch = [pltpu.SemaphoreType.DMA((2 * COPIES,))] + scratch
     return pl.pallas_call(
         lambda *refs: state_kernel(*refs, side=side, passing=passing),
         in_specs=[SMEM, SMEM, HBM] + [VMEM] * len(operands),
         out_specs=[VMEM] * len(outs),
         out_shape=outs,
-        scratch_shapes=[pltpu.SemaphoreType.DMA((3 * COPIES,))],
-        compiler_params=params(40),
+        scratch_shapes=scratch,
+        compiler_params=params(),
         cost_estimate=cost(20 * tokens * channels, 16 * tokens * channels),
         name="block_states_" + name,
     )(place, weights, streams, *operands)
@@ -634,7 +663,7 @@
 
 
 def block_output(place, enter, pieces, locals_, carries, tokens, channels):
-    chunk = 1024
+    chunk = 512
     return pl.pallas_call(
         lambda *refs: output_kernel(*refs, pieces=pieces, chunk=chunk),
         in_specs=[SMEM] + [VMEM] * (1 + len(locals_) + len(carries)),
@@ -781,36 +810,30 @@
     return lax.ppermute(array, ("ctx", "fsdp"), route)
 
 
-def carry_in(place, weights, sent, kept, rate, devices, tokens, beside):
-    full, half = kept.shape, (kept.shape[0], kept.shape[1] // 2)
-    wide, narrow, lean = shaped(full, F32), shaped(half, F32), shaped(half, BF16)
+def carry_in(flags, sent, kept, rate, devices, tokens, beside):
+    wide, lean = shaped(kept.shape, F32), shaped(kept.shape, BF16)
 
     def call(kernel, name, send, distance, *operands, outs, **static):
         got = swap(send, distance, devices)
         return small_call(
-            kernel, name, place, weights, operands[0], got, rate, *operands[1:], outs=outs, tokens=tokens,
+            kernel, name, flags, operands[0], got, rate, *operands[1:], outs=outs, tokens=tokens,
             tokens_before=beside(name, send), **static,
         )
 
-    first, mine, send = call(pair_kernel, "pairs", sent, 1, kept, outs=[wide, narrow, lean])
-    lower, total, send = call(quad_kernel, "quads", send, 2, mine, outs=[narrow, narrow, lean])
+    first, ends, send = call(pair_kernel, "pairs", sent, 1, kept, outs=[wide, wide, lean])
+    lower, total, send = call(quad_kernel, "quads", send, 2, ends, outs=[wide, wide, lean])
     carry, number, size = [], 0, 4
-    while size < devices:
-        name = "round" + str(number)
-        if 2 * size < devices:
-            held, total, send = call(
-                round_kernel, name, send, size, total, *carry, outs=[narrow, narrow, lean],
-                number=number, last=False,
-            )
-            carry = [held]
-        else:
-            keep, send = call(
-                round_kernel, name, send, size, total, *carry, lower, outs=[narrow, lean],
-                number=number, last=True,
-            )
+    while 2 * size < devices:
+        held, total, send = call(
+            round_kernel, "round" + str(number), send, size, total, *carry, outs=[wide, wide, lean],
+            number=number, last=False,
+        )
+        carry = [held]
         size, number = 2 * size, number + 1
-    full_lean = shaped(full, BF16)
-    keep, send = call(back_kernel, "back", send, 2, keep, first, outs=[full_lean, full_lean])
+    keep, send = call(
+        round_kernel, "round" + str(number), send, size, total, *carry, lower, first, outs=[lean, lean],
+        number=number, last=True,
+    )
     beside("end", send)
     return swap(send, 1, devices), keep
 
@@ -822,19 +845,24 @@
     if tokens != PARTS * PART or fsdp_count != 2 or devices < 8:
         return narrow_local(streams, segments, short_taps, decay_rates, residues, skip_gain)
     owned = short_taps.shape[2]
-    place, weights, agree, causal, follow, enter, chosen, own_pack, tail = placing(
-        segments, (short_taps, skip_gain, decay_rates, residues), streams, devices, fsdp_count
+    tail = streams[:, tokens - (SHORT - 1) :, :]
+    halo = lax.ppermute(tail, ("ctx", "fsdp"), [(i, i + 1) for i in range(devices - 1)])
+    streams = pltpu.with_memory_space_constraint(streams, pltpu.HBM)
+    own_pack = packing((short_taps, skip_gain, decay_rates, residues), tail)
+    place, weights, flags, agree, causal, follow, enter, chosen, keys = placing(
+        segments, streams, owned, devices, fsdp_count
     )
-    halo = lax.ppermute(tail, ("ctx", "fsdp"), [(i, i + 1) for i in range(devices - 1)])
     other_pack = lax.ppermute(own_pack, "fsdp", [(0, 1), (1, 0)])
     passing = ROUNDS + 3 * ((devices // 4).bit_length() - 1)
-    found, brought = [], ()
+    found = []
     for side, (name, pack) in enumerate((("own", own_pack), ("other", other_pack))):
         taps, fall, *loaded = lags(place, streams, pack, side, name)
-        brought = loaded or brought
+        values = loaded[0] if loaded else values
         gated, query, state, middle, spread_rates, *brought = block_states(
-            place, weights, streams, (*brought, halo, pack, fall, agree, chosen), side, passing, name
+            place, weights, streams, (keys, values, halo, pack, fall, agree, chosen), side, passing, name
         )
+        if brought:
+            keys, values = brought
         operands = (query, halo, gated, pack, taps, middle, agree, causal, follow)
         found.append((operands, state, spread_rates))
     span = owned // 2
@@ -856,7 +884,7 @@
         return given
 
     carries = carry_in(
-        place, weights, found[0][1], found[1][1], found[1][2], devices, tokens, beside
+        flags, found[0][1], found[1][1], found[1][2], devices, tokens, beside
     )
     sides = [carries[0], found[0][2], carries[1], found[1][2]]
     return block_output(place, enter, pieces, locals_, sides, tokens, channels)

time: 73.9 us -> 65.2 us (0.88)
  Pallas kernels: 54.1 us -> 47.3 us
  local copies, waits for them, and re-layouts: 2.95 us -> 1.1 us
  waiting for transfers between devices: 2.81 us -> 2.04 us
    unnamed x22 -> x0, local copies, waits for them, and re-layouts: 2.95 us -> none
    pallas_call x6 -> x5, Pallas kernels: 3.81 us -> 1.24 us  [small_call(): pl.pallas_call(lambda *refs: kernel(*refs[waits:], **static), in_specs=[A...]
    pallas_call x2, Pallas kernels: 12.8 us -> 10.5 us  [block_states(): pl.pallas_call(lambda *refs: state_kernel(*refs, side=side, passing=passi...]
    pallas_call x4, Pallas kernels: 23.9 us -> 21.7 us  [block_local(): pl.pallas_call(lambda *refs: local_kernel(*refs, side=side, first=first),...]
    pallas_call x0 -> x1, Pallas kernels: none -> 2.04 us  [packing(): pl.pallas_call(packing_kernel, in_specs=[ANY] + [HBM] * len(arrays), out_...]
    pallas_call x1, Pallas kernels: 5.46 us -> 4.29 us  [block_output(): pl.pallas_call(lambda *refs: output_kernel(*refs, pieces=pieces, chunk=ch...]
    slice x0 -> x1, local copies, waits for them, and re-layouts: none -> 1.1 us  [local(): tail = streams[:, tokens - (SHORT - 1):, :]]
    ppermute x7 -> x6, starting transfers between devices: 8.57 us -> 9.12 us  [swap(): return lax.ppermute(array, ('ctx', 'fsdp'), route)]
  transfers between devices with their start and end apart: 9 -> 8, of which waited for: 3 -> 2; matrix products, arithmetic and copies ran while one was open for 0% -> 0% of each run, Pallas kernels for 56% -> 61%
where the time goes in v3:
time: 65.2 us; the launch traced here: 64.8 us
  Pallas kernels  47.3 us (73%)
  starting transfers between devices  14.1 us (22%)
  waiting for transfers between devices  2.04 us (3%)
  local copies, waits for them, and re-layouts  1.1 us (2%)
    pallas_call x4, Pallas kernels, block_local(): pl.pallas_call(lambda *refs: local_kernel(*refs, side=side, first=first),...  21.7 us
    pallas_call x2, Pallas kernels, block_states(): pl.pallas_call(lambda *refs: state_kernel(*refs, side=side, passing=passi...  10.5 us
    ppermute x6, starting transfers between devices, swap(): return lax.ppermute(array, ('ctx', 'fsdp'), route)  9.12 us
    pallas_call x1, Pallas kernels, block_output(): pl.pallas_call(lambda *refs: output_kernel(*refs, pieces=pieces, chunk=ch...  4.29 us
    pallas_call x2, Pallas kernels, lags(): pl.pallas_call(lambda *refs: lag_kernel(*refs, side=side), in_specs=specs...  4.11 us
    pallas_call x1, Pallas kernels, placing(): pl.pallas_call(lambda *refs: place_kernel(*refs, devices=devices, tokens=...  3.4 us
    ppermute x1, starting transfers between devices, local(): other_pack = lax.ppermute(own_pack, 'fsdp', [(0, 1), (1, 0)])  3.03 us
    pallas_call x1, Pallas kernels, packing(): pl.pallas_call(packing_kernel, in_specs=[ANY] + [HBM] * len(arrays), out_...  2.04 us
  transfers between devices with their start and end apart: 8, of which 2 were waited for; matrix products, arithmetic and copies ran while one was open for 0% of the time, Pallas kernels for 61%

profile of v3, /device:TPU:0, one launch (start us, length us, event | category | flops | bytes accessed | tf_op | source)
XLA Modules:
  0.0 64.8 jit_solution(7044773407367898843)
XLA Ops:
  0.0 1.1 %slice.3.refs_0_ = bf16[3,2,8192]{2,1,0:T(2,128)(2,1)S(1)} slice(bf16[3,256,8192]{2,1,0:T(8,128)(2,1)} %refs_2_.3), slice={[0:3], [254:256], [0:8192]} | slice | bytes 196608 | tf_op jit(solution)/shard_map/slice | solution.py:848
  1.1 2.0 %packing.1.refs_2_.refs_6_.refs_4_ = f32[16,4096]{1,0:T(8,128)S(1)} custom-call(bf16[3,2,8192]{2,1,0:T(2,128)(2,1)S(1)} %slice.3.refs_0_, f32[3,3,4096]{2,1,0:T(4,128)} %refs_1_.2, f32[1,4096]{1,0:T(1,128)} %bitcast.6, f32[16,256]{1,0:T(8,128)} %bitcast.7, f32[16,256]{1,0:T(8,128)} %bitcast.8), custom_call_target="tpu_custom_call" | custom-call | flops 1024 | bytes 1024 | tf_op jit(solution)/shard_map/packing/pallas_call | solution.py:553
  3.1 3.0 %collective-permute-start.1 = (f32[16,4096]{1,0:T(8,128)S(1)}, f32[16,4096]{1,0:T(8,128)S(1)}, u32[]{:S(2)}, u32[]{:S(2)}) collective-permute-start(f32[16,4096]{1,0:T(8,128)S(1)} %packing.1.refs_2_.refs_6_.refs_4_), channel_id=1, source_target_pairs={{0,1},{1,0},{2,3},{3,2},{4,5},{5,4},{6,7},{7,6},{8,9},{9,8},{10,11... | collective-permute-start | bytes 786440 | tf_op jit(solution)/shard_map/ppermute | solution.py:855
  6.2 1.9 %collective-permute-start = (bf16[3,2,8192]{2,1,0:T(2,128)(2,1)S(1)}, bf16[3,2,8192]{2,1,0:T(2,128)(2,1)S(1)}, u32[]{:S(2)}, u32[]{:S(2)}) collective-permute-start(bf16[3,2,8192]{2,1,0:T(2,128)(2,1)S(1)} %slice.3.refs_0_), channel_id=1, source_target_pairs={{0,1},{1,2},{2,3},{3,4},{4,5},{5,6},{6,7},{7,8},{8,9},{9,10},{10,1... | collective-permute-start | bytes 294920 | tf_op jit(solution)/shard_map/ppermute | solution.py:849
  8.1 3.4 %placing.1 = (s32[16]{0:T(128)S(1)}, f32[32]{0:T(128)S(1)}, f32[48,128]{1,0:T(8,128)S(1)}, f32[2,256,128]{2,1,0:T(8,128)S(1)}, bf16[2,128,256]{2,1,0:T(8,128)(2,...) custom-call(bf16[3,256,8192]{2,1,0:T(8,128)(2,1)} %refs_2_.3, ...), custom_call_target="tpu_custom_call" | custom-call | flops 1024 | bytes 1024 | tf_op jit(solution)/shard_map/placing/pallas_call | solution.py:580
  11.5 2.3 %lags_own.1 = (f32[256,128]{1,0:T(8,128)S(1)}, bf16[4096,128]{1,0:T(8,128)(2,1)S(1)}, bf16[256,4096]{1,0:T(8,128)(2,1)S(1)}) custom-call(s32[16]{0:T(128)S(1)} %get-tuple-element.60.refs_0_, bf16[3,256,8192]{2,1,0:T(8,128)(2,1)} %refs_2_.3, f32[16,4096]{1,0:T(8,128)S(1)} %packing.1.refs_2_.refs_6_.refs_4_), custom_call_target="tpu_custom_call" | custom-call | flops 1024 | bytes 1024 | tf_op jit(solution)/shard_map/lags_own/pallas_call | solution.py:605
  13.9 0.0 collective-permute-done.refs_5_.refs_2_
  13.9 5.3 %block_states_own.1 = (bf16[256,4096]{1,0:T(8,128)(2,1)S(1)}, bf16[256,4096]{1,0:T(8,128)(2,1)S(1)}, bf16[16,4096]{1,0:T(8,128)(2,1)S(1)}, f32[16,4096]{1,0:T(8,...) custom-call(s32[16]{0:T(128)S(1)} %get-tuple-element.60.refs_0_, ...), custom_call_target="tpu_custom_call" | custom-call | flops 20971520 | bytes 16777216 | tf_op jit(solution)/shard_map/block_states_own/pallas_call | solution.py:631
  19.2 2.5 %collective-permute-start.2 = (bf16[16,4096]{1,0:T(8,128)(2,1)S(1)}, bf16[16,4096]{1,0:T(8,128)(2,1)S(1)}, u32[]{:S(2)}, u32[]{:S(2)}) collective-permute-start(bf16[16,4096]{1,0:T(8,128)(2,1)S(1)} %get-tuple-element.79), channel_id=1, source_target_pairs={{0,1},{1,0},{2,3},{3,2},{4,5},{5,4},{6,7},{7,6},{8,9},{9,8},{10,11... | collective-permute-start | bytes 393224 | tf_op jit(solution)/shard_map/ppermute | solution.py:810
  21.7 0.0 collective-permute-done.1.refs_0_.refs_6_.refs_4_
  21.7 1.8 %lags_other.1 = (f32[256,128]{1,0:T(8,128)S(1)}, bf16[4096,128]{1,0:T(8,128)(2,1)S(1)}) custom-call(f32[16,4096]{1,0:T(8,128)S(1)} %collective-permute-done.1.refs_0_.refs_6_.refs_4_), custom_call_target="tpu_custom_call" | custom-call | flops 1024 | bytes 1024 | tf_op jit(solution)/shard_map/lags_other/pallas_call | solution.py:605
  23.5 5.2 %block_states_other.1 = (bf16[256,4096]{1,0:T(8,128)(2,1)S(1)}, bf16[256,4096]{1,0:T(8,128)(2,1)S(1)}, bf16[16,4096]{1,0:T(8,128)(2,1)S(1)}, f32[16,4096]{1,0:T(8,128)S(1)}, f32[16,4096]{1,0:T(8,128)S(1)}) custom-call(s32[16]{0:T(128)S(1)} %get-tuple-element.60.refs_0_, f32[32]{0:T(128)S(1)} %get-tuple-element.62.refs_1_, bf16[3,256,8192]{2,1,0:T(8,128)(2,1)} %refs_2_.3, ...), custom_call_target="tpu_custom_call" | custom-call | flops 20971520 | bytes 16777216 | tf_op jit(solution)/shard_map/block_states_other/pallas_call | solution.py:631
  28.7 0.0 collective-permute-done.2.refs_2_
  28.7 0.2 pairs.1
  28.9 0.4 collective-permute-start.3
  29.3 1.0 %collective-permute-done.3.refs_2_ = bf16[16,4096]{1,0:T(8,128)(2,1)S(1)} collective-permute-done((bf16[16,4096]{1,0:T(8,128)(2,1)S(1)}, bf16[16,4096]{1,0:T(8,128)(2,1)S(1)}, u32[]{:S(2)}, u32[]{:S(2)}) %collective-permute-start.3) | collective-permute-done | bytes 131104 | tf_op jit(solution)/shard_map/ppermute | solution.py:810
  30.3 0.2 quads.1
  30.5 1.6 %collective-permute-start.4 = (bf16[16,4096]{1,0:T(8,128)(2,1)S(1)}, bf16[16,4096]{1,0:T(8,128)(2,1)S(1)}, u32[]{:S(2)}, u32[]{:S(2)}) collective-permute-start(bf16[16,4096]{1,0:T(8,128)(2,1)S(1)} %get-tuple-element.83.refs_10_), channel_id=1, source_target_pairs={{0,4},{1,5},{2,6},{3,7},{4,0},{5,1},{6,2},{7,3},{8,12},{9,13},{10,... | collective-permute-start | bytes 393224 | tf_op jit(solution)/shard_map/ppermute | solution.py:810
  32.1 5.2 %block_local_own0.1 = (f32[256,2048]{1,0:T(8,128)S(1)}, bf16[256,2048]{1,0:T(8,128)(2,1)S(1)}, bf16[128,2048]{1,0:T(8,128)(2,1)S(1)}, f32[8,128]{1,0:T(8,128)S(1)}) custom-call(s32[16]{0:T(128)S(1)} %get-tuple-element.60.refs_0_, bf16[256,4096]{1,0:T(8,128)(2,1)S(1)} %get-tuple-element.68.refs_1_, ...), custom_call_target="tpu_custom_call" | custom-call | flops 1073741824 | bytes 20971520 | tf_op jit(solution)/shard_map/block_local_own0/pallas_call | solution.py:645
  37.3 0.0 collective-permute-done.4.refs_3_
  37.3 0.2 round0.1
  37.6 1.6 %collective-permute-start.5 = (bf16[16,4096]{1,0:T(8,128)(2,1)S(1)}, bf16[16,4096]{1,0:T(8,128)(2,1)S(1)}, u32[]{:S(2)}, u32[]{:S(2)}) collective-permute-start(bf16[16,4096]{1,0:T(8,128)(2,1)S(1)} %get-tuple-element.89.refs_10_), channel_id=1, source_target_pairs={{0,8},{1,9},{2,10},{3,11},{4,12},{5,13},{6,14},{7,15},{8,0},{9,1},... | collective-permute-start | bytes 393224 | tf_op jit(solution)/shard_map/ppermute | solution.py:810
  39.2 5.4 %block_local_own1.1 = (f32[256,2048]{1,0:T(8,128)S(1)}, bf16[256,2048]{1,0:T(8,128)(2,1)S(1)}, bf16[128,2048]{1,0:T(8,128)(2,1)S(1)}, f32[8,128]{1,0:T(8,128)S(1)}) custom-call(s32[16]{0:T(128)S(1)} %get-tuple-element.60.refs_0_, bf16[256,4096]{1,0:T(8,128)(2,1)S(1)} %get-tuple-element.68.refs_1_, ...), custom_call_target="tpu_custom_call" | custom-call | flops 1073741824 | bytes 20971520 | tf_op jit(solution)/shard_map/block_local_own1/pallas_call | solution.py:645
  44.6 0.0 collective-permute-done.5.refs_3_
  44.6 0.3 round1.1
  44.9 2.6 %collective-permute-start.6 = (bf16[16,4096]{1,0:T(8,128)(2,1)S(1)}, bf16[16,4096]{1,0:T(8,128)(2,1)S(1)}, u32[]{:S(2)}, u32[]{:S(2)}) collective-permute-start(bf16[16,4096]{1,0:T(8,128)(2,1)S(1)} %get-tuple-element.100.refs_10_), channel_id=1, source_target_pairs={{0,16},{1,17},{2,18},{3,19},{4,20},{5,21},{6,22},{7,23},{8,24},{9,... | collective-permute-start | bytes 393224 | tf_op jit(solution)/shard_map/ppermute | solution.py:810
  47.5 5.2 %block_local_other0.1 = (f32[256,2048]{1,0:T(8,128)S(1)}, bf16[256,2048]{1,0:T(8,128)(2,1)S(1)}, bf16[128,2048]{1,0:T(8,128)(2,1)S(1)}, f32[8,128]{1,0:T(8,128)S(1)}) custom-call(s32[16]{0:T(128)S(1)} %get-tuple-element.60.refs_0_, bf16[256,4096]{1,0:T(8,128)(2,1)S(1)} %get-tuple-element.93.refs_1_, ...), custom_call_target="tpu_custom_call" | custom-call | flops 1073741824 | bytes 20971520 | tf_op jit(solution)/shard_map/block_local_other0/pallas_call | solution.py:645
  52.7 1.0 %collective-permute-done.6.refs_3_ = bf16[16,4096]{1,0:T(8,128)(2,1)S(1)} collective-permute-done((bf16[16,4096]{1,0:T(8,128)(2,1)S(1)}, bf16[16,4096]{1,0:T(8,128)(2,1)S(1)}, u32[]{:S(2)}, u32[]{:S(2)}) %collective-permute-start.6) | collective-permute-done | bytes 131104 | tf_op jit(solution)/shard_map/ppermute | solution.py:810
  53.7 0.4 round2.1
  54.1 0.4 collective-permute-start.7
  54.5 5.9 %block_local_other1.1 = (f32[256,2048]{1,0:T(8,128)S(1)}, bf16[256,2048]{1,0:T(8,128)(2,1)S(1)}, bf16[128,2048]{1,0:T(8,128)(2,1)S(1)}, f32[8,128]{1,0:T(8,128)}) custom-call(s32[16]{0:T(128)S(1)} %get-tuple-element.60.refs_0_, bf16[256,4096]{1,0:T(8,128)(2,1)S(1)} %get-tuple-element.93.refs_1_, ...), custom_call_target="tpu_custom_call" | custom-call | flops 1073741824 | bytes 20971520 | tf_op jit(solution)/shard_map/block_local_other1/pallas_call | solution.py:645
  60.4 0.0 collective-permute-done.7.refs_14_
  60.4 4.3 %block_output.1 = bf16[256,8192]{1,0:T(8,128)(2,1)} custom-call(s32[16]{0:T(128)S(1)} %get-tuple-element.60.refs_0_, bf16[256,128]{1,0:T(8,128)(2,1)S(1)} %get-tuple-element.61.refs_1_, f32[256,2048]{1,0:T(8,128)S(1)} %get-tuple-element.84.refs_2_, bf16[256,2048]{1,0:T(8,128)(2,1)S(1)} %get-tuple-element.85.refs_3_, ...), custom_call_target="tpu_custom_call" | custom-call | flops 41943040 | bytes 16777216 | tf_op jit(solution)/shard_map/block_output/pallas_call | solution.py:667
Async XLA Ops:
  3.1 18.6 %collective-permute-start.1 = (f32[16,4096]{1,0:T(8,128)S(1)}, f32[16,4096]{1,0:T(8,128)S(1)}, u32[]{:S(2)}, u32[]{:S(2)}) collective-permute-start(f32[16,4096]{1,0:T(8,128)S(1)} %packing.1.refs_2_.refs_6_.refs_4_), channel_id=1, source_target_pairs={{0,1},{1,0},{2,3},{3,2},{4,5},{5,4},{6,7},{7,6},{8,9},{9,8},{10,11... | collective-permute-start | bytes 786440 | tf_op jit(solution)/shard_map/ppermute | solution.py:855
  6.2 7.7 %collective-permute-start = (bf16[3,2,8192]{2,1,0:T(2,128)(2,1)S(1)}, bf16[3,2,8192]{2,1,0:T(2,128)(2,1)S(1)}, u32[]{:S(2)}, u32[]{:S(2)}) collective-permute-start(bf16[3,2,8192]{2,1,0:T(2,128)(2,1)S(1)} %slice.3.refs_0_), channel_id=1, source_target_pairs={{0,1},{1,2},{2,3},{3,4},{4,5},{5,6},{6,7},{7,8},{8,9},{9,10},{10,1... | collective-permute-start | bytes 294920 | tf_op jit(solution)/shard_map/ppermute | solution.py:849
  19.2 9.5 %collective-permute-start.2 = (bf16[16,4096]{1,0:T(8,128)(2,1)S(1)}, bf16[16,4096]{1,0:T(8,128)(2,1)S(1)}, u32[]{:S(2)}, u32[]{:S(2)}) collective-permute-start(bf16[16,4096]{1,0:T(8,128)(2,1)S(1)} %get-tuple-element.79), channel_id=1, source_target_pairs={{0,1},{1,0},{2,3},{3,2},{4,5},{5,4},{6,7},{7,6},{8,9},{9,8},{10,11... | collective-permute-start | bytes 393224 | tf_op jit(solution)/shard_map/ppermute | solution.py:810
  28.9 1.4 %collective-permute-start.3 = (bf16[16,4096]{1,0:T(8,128)(2,1)S(1)}, bf16[16,4096]{1,0:T(8,128)(2,1)S(1)}, u32[]{:S(2)}, u32[]{:S(2)}) collective-permute-start(bf16[16,4096]{1,0:T(8,128)(2,1)S(1)} %get-tuple-element.82), channel_id=1, source_target_pairs={{0,2},{1,3},{2,0},{3,1},{4,6},{5,7},{6,4},{7,5},{8,10},{9,11},{10,... | collective-permute-start | bytes 393224 | tf_op jit(solution)/shard_map/ppermute | solution.py:810
  30.5 6.8 %collective-permute-start.4 = (bf16[16,4096]{1,0:T(8,128)(2,1)S(1)}, bf16[16,4096]{1,0:T(8,128)(2,1)S(1)}, u32[]{:S(2)}, u32[]{:S(2)}) collective-permute-start(bf16[16,4096]{1,0:T(8,128)(2,1)S(1)} %get-tuple-element.83.refs_10_), channel_id=1, source_target_pairs={{0,4},{1,5},{2,6},{3,7},{4,0},{5,1},{6,2},{7,3},{8,12},{9,13},{10,... | collective-permute-start | bytes 393224 | tf_op jit(solution)/shard_map/ppermute | solution.py:810
  37.6 7.0 %collective-permute-start.5 = (bf16[16,4096]{1,0:T(8,128)(2,1)S(1)}, bf16[16,4096]{1,0:T(8,128)(2,1)S(1)}, u32[]{:S(2)}, u32[]{:S(2)}) collective-permute-start(bf16[16,4096]{1,0:T(8,128)(2,1)S(1)} %get-tuple-element.89.refs_10_), channel_id=1, source_target_pairs={{0,8},{1,9},{2,10},{3,11},{4,12},{5,13},{6,14},{7,15},{8,0},{9,1},... | collective-permute-start | bytes 393224 | tf_op jit(solution)/shard_map/ppermute | solution.py:810
  44.9 8.8 %collective-permute-start.6 = (bf16[16,4096]{1,0:T(8,128)(2,1)S(1)}, bf16[16,4096]{1,0:T(8,128)(2,1)S(1)}, u32[]{:S(2)}, u32[]{:S(2)}) collective-permute-start(bf16[16,4096]{1,0:T(8,128)(2,1)S(1)} %get-tuple-element.100.refs_10_), channel_id=1, source_target_pairs={{0,16},{1,17},{2,18},{3,19},{4,20},{5,21},{6,22},{7,23},{8,24},{9,... | collective-permute-start | bytes 393224 | tf_op jit(solution)/shard_map/ppermute | solution.py:810
  54.1 6.3 %collective-permute-start.7 = (bf16[16,4096]{1,0:T(8,128)(2,1)S(1)}, bf16[16,4096]{1,0:T(8,128)(2,1)S(1)}, u32[]{:S(2)}, u32[]{:S(2)}) collective-permute-start(bf16[16,4096]{1,0:T(8,128)(2,1)S(1)} %get-tuple-element.109.refs_10_), channel_id=1, source_target_pairs={{0,1},{1,0},{2,3},{3,2},{4,5},{5,4},{6,7},{7,6},{8,9},{9,8},{10,11... | collective-permute-start | bytes 393224 | tf_op jit(solution)/shard_map/ppermute | solution.py:810

commit v4 on v3

--- a/solution.py
+++ b/solution.py
@@ -13,7 +13,7 @@
 PARTS = 2
 WIDE = 256
 COPIES = 4
-TILES = 8
+TILES = 16
 TILE_GROUPS = LANES // GROUP
 ROWS = 64
 LOG2E = 1.4426950408889634
@@ -86,8 +86,11 @@
 
 
 def packing_kernel(*refs):
-    sources, pack_ref, held, sems = refs[1:5], refs[5], refs[6:10], refs[10]
+    sources, x_ref, pack_ref, tail_ref, held, ends_ref, sems = refs[:4], *refs[4:7], refs[7:11], *refs[11:]
     short_ref, skip_ref, rates_ref, residues_ref = held
+    last = x_ref.shape[1] - ends_ref.shape[1]
+    tail = pltpu.make_async_copy(x_ref.at[:, pl.ds(last, ends_ref.shape[1]), :], ends_ref, sems.at[4])
+    tail.start()
     copies = [
         pltpu.make_async_copy(source, target, sems.at[number])
         for number, (source, target) in enumerate(zip(sources, held))
@@ -117,7 +120,10 @@
         pack_ref[GAIN : GAIN + 1, at] = factor * jnp.sqrt(2.0 * half / (1.0 + half))
         return carried
 
-    lax.fori_loop(0, pack_ref.shape[1] // LANES, tile, 0, unroll=4)
+    lax.fori_loop(0, pack_ref.shape[1] // LANES, tile, 0, unroll=8)
+    tail.wait()
+    for stream in range(3):
+        tail_ref[stream] = ends_ref[stream, ends_ref.shape[1] - (SHORT - 1) :, :]
 
 
 def place_kernel(
@@ -229,7 +235,7 @@
         taps_ref[groups, :] = jnp.sum(terms, axis=1)
         return carried
 
-    lax.fori_loop(0, pack_ref.shape[1] // LANES, tile, 0, unroll=4)
+    lax.fori_loop(0, pack_ref.shape[1] // LANES, tile, 0, unroll=8)
     for copy in copies:
         copy.wait()
 
@@ -358,9 +364,11 @@
     def carry(tile):
         at = source(tile)
         age = (iota((PART, LANES), 0) + 1).astype(F32)
-        onward = jnp.exp2(pack_ref[RATE : RATE + 1, at] * -LOG2E * age) * pack_ref[GAIN : GAIN + 1, at]
+        rate = pack_ref[RATE : RATE + 1, at] * -LOG2E
+        onward = jnp.exp2(rate * age) * pack_ref[GAIN : GAIN + 1, at]
+        onward_ref[PART:, target(tile)] = (onward * jnp.exp2(rate * PART)).astype(BF16)
         onward = onward.astype(BF16)
-        onward_ref[:, target(tile)] = onward
+        onward_ref[:PART, target(tile)] = onward
         held["carry", tile] = jnp.dot(
             onward * follow_ref[...], spread(middle_ref[:, at]), preferred_element_type=F32
         )
@@ -425,22 +433,17 @@
     done = 0
     for index, (side, first, count) in enumerate(pieces):
         local_ref, queries_ref, onward_ref = inputs[3 * index : 3 * index + 3]
-        carry_ref, rates_ref = inputs[3 * len(pieces) + 2 * side : 3 * len(pieces) + 2 * side + 2]
+        carry_ref = inputs[3 * len(pieces) + side]
 
         def tile(start):
             at, source = lanes_at(start), lanes_at(first + start)
-            carry = carry_ref[:, source].astype(F32)
-            for part in range(PARTS):
-                span = slice(part * PART, (part + 1) * PART)
-                if part:
-                    carry = carry * jnp.exp(-rates_ref[:, source] * PART)
-                carried = jnp.dot(
-                    onward_ref[:, at] * enter_ref[span, :], spread(carry), preferred_element_type=F32
-                )
-                mixed = (local_ref[span, at] + carried).astype(BF16).astype(F32)
-                held_ref[span, lanes_at(done + start)] = (
-                    queries_ref[span, at].astype(F32) * mixed
-                ).astype(BF16)
+            carried = jnp.dot(
+                onward_ref[:, at] * enter_ref[...],
+                spread(carry_ref[:, source].astype(F32)),
+                preferred_element_type=F32,
+            )
+            mixed = (local_ref[:, at] + carried).astype(BF16).astype(F32)
+            held_ref[:, lanes_at(done + start)] = (queries_ref[:, at].astype(F32) * mixed).astype(BF16)
 
         for begin in range(0, count, chunk):
 
@@ -545,22 +548,22 @@
     )(*tokens_before, flags, *operands)
 
 
-def packing(weights, after):
+def packing(weights, streams):
     short, skip, rates, residues = weights
-    owned = short.shape[2]
+    owned, channels = short.shape[2], streams.shape[2]
     arrays = (short, skip.reshape(1, owned), rates.T, residues.T)
     arrays = [pltpu.with_memory_space_constraint(array, pltpu.HBM) for array in arrays]
     return pl.pallas_call(
         packing_kernel,
-        in_specs=[ANY] + [HBM] * len(arrays),
-        out_specs=VMEM,
-        out_shape=shaped((PACKED, owned), F32),
+        in_specs=[HBM] * (len(arrays) + 1),
+        out_specs=[VMEM, VMEM],
+        out_shape=[shaped((PACKED, owned), F32), shaped((3, SHORT - 1, channels), BF16)],
         scratch_shapes=[pltpu.VMEM(array.shape, array.dtype) for array in arrays]
-        + [pltpu.SemaphoreType.DMA((len(arrays),))],
+        + [pltpu.VMEM((3, 16, channels), BF16), pltpu.SemaphoreType.DMA((len(arrays) + 1,))],
         compiler_params=params(),
         cost_estimate=cost(1024, 1024),
         name="packing",
-    )(after, *arrays)
+    )(*arrays, streams)
 
 
 def placing(segments, streams, owned, devices, fsdp_count):
@@ -649,7 +652,7 @@
         out_shape=[
             shaped((tokens, count), F32),
             shaped((tokens, count), BF16),
-            shaped((PART, count), BF16),
+            shaped((tokens, count), BF16),
             shaped((8, LANES), F32),
         ],
         scratch_shapes=[
@@ -845,10 +848,9 @@
     if tokens != PARTS * PART or fsdp_count != 2 or devices < 8:
         return narrow_local(streams, segments, short_taps, decay_rates, residues, skip_gain)
     owned = short_taps.shape[2]
-    tail = streams[:, tokens - (SHORT - 1) :, :]
+    streams = pltpu.with_memory_space_constraint(streams, pltpu.HBM)
+    own_pack, tail = packing((short_taps, skip_gain, decay_rates, residues), streams)
     halo = lax.ppermute(tail, ("ctx", "fsdp"), [(i, i + 1) for i in range(devices - 1)])
-    streams = pltpu.with_memory_space_constraint(streams, pltpu.HBM)
-    own_pack = packing((short_taps, skip_gain, decay_rates, residues), tail)
     place, weights, flags, agree, causal, follow, enter, chosen, keys = placing(
         segments, streams, owned, devices, fsdp_count
     )
@@ -865,8 +867,9 @@
             keys, values = brought
         operands = (query, halo, gated, pack, taps, middle, agree, causal, follow)
         found.append((operands, state, spread_rates))
-    span = owned // 2
-    pieces = [(side, first, span) for side in (OWN, OTHER) for first in range(0, owned, span)]
+    half = owned // 2
+    more = half + half // 4
+    pieces = [(OWN, 0, half), (OWN, half, half), (OTHER, 0, more), (OTHER, more, owned - more)]
     beside_rounds = {"round0": 1, "round1": 1, "round2": 1}
     waiting, locals_ = list(pieces), []
 
@@ -877,7 +880,7 @@
             side, first, size = waiting.pop(0)
             label = "own" if side == OWN else "other"
             *made, token = block_local(
-                place, found[side][0], array, side, first, size, label + str(first // size)
+                place, found[side][0], array, side, first, size, label + str(first)
             )
             locals_.extend(made)
             given.append(token)
@@ -886,8 +889,7 @@
     carries = carry_in(
         flags, found[0][1], found[1][1], found[1][2], devices, tokens, beside
     )
-    sides = [carries[0], found[0][2], carries[1], found[1][2]]
-    return block_output(place, enter, pieces, locals_, sides, tokens, channels)
+    return block_output(place, enter, pieces, locals_, carries, tokens, channels)
 
 
 def solution(mesh):

time: 65.2 us -> 62.8 us (0.963)
  local copies, waits for them, and re-layouts: 1.1 us -> 0 us
    slice x1 -> x0, local copies, waits for them, and re-layouts: 1.1 us -> none  [local(): tail = streams[:, tokens - (SHORT - 1):, :]]
    ppermute x6, waiting for transfers between devices: 2.03 us -> 1.37 us  [swap(): return lax.ppermute(array, ('ctx', 'fsdp'), route)]
  transfers between devices with their start and end apart: 8 -> 8, of which waited for: 2 -> 3; matrix products, arithmetic and copies ran while one was open for 0% -> 0% of each run, Pallas kernels for 61% -> 64%
where the time goes in v4:
time: 62.8 us; the launch traced here: 62.5 us
  Pallas kernels  47 us (75%)
  starting transfers between devices  13.6 us (22%)
  waiting for transfers between devices  1.6 us (3%)
    pallas_call x4, Pallas kernels, block_local(): pl.pallas_call(lambda *refs: local_kernel(*refs, side=side, first=first),...  21.9 us
    pallas_call x2, Pallas kernels, block_states(): pl.pallas_call(lambda *refs: state_kernel(*refs, side=side, passing=passi...  11 us
    ppermute x6, starting transfers between devices, swap(): return lax.ppermute(array, ('ctx', 'fsdp'), route)  8.63 us
    pallas_call x1, Pallas kernels, block_output(): pl.pallas_call(lambda *refs: output_kernel(*refs, pieces=pieces, chunk=ch...  3.97 us
    pallas_call x2, Pallas kernels, lags(): pl.pallas_call(lambda *refs: lag_kernel(*refs, side=side), in_specs=specs...  3.51 us
    pallas_call x1, Pallas kernels, placing(): pl.pallas_call(lambda *refs: place_kernel(*refs, devices=devices, tokens=...  3.4 us
    ppermute x1, starting transfers between devices, local(): other_pack = lax.ppermute(own_pack, 'fsdp', [(0, 1), (1, 0)])  3.03 us
    pallas_call x1, Pallas kernels, packing(): pl.pallas_call(packing_kernel, in_specs=[HBM] * (len(arrays) + 1), out_sp...  1.98 us
  transfers between devices with their start and end apart: 8, of which 3 were waited for; matrix products, arithmetic and copies ran while one was open for 0% of the time, Pallas kernels for 64%

profile of v4, /device:TPU:0, one launch (start us, length us, event | category | flops | bytes accessed | tf_op | source)
XLA Modules:
  0.0 62.5 jit_solution(4548505910911992)
XLA Ops:
  0.0 2.0 %packing.1 = (f32[16,4096]{1,0:T(8,128)S(1)}, bf16[3,2,8192]{2,1,0:T(2,128)(2,1)S(1)}) custom-call(f32[3,3,4096]{2,1,0:T(4,128)} %refs_0_.3, f32[1,4096]{1,0:T(1,128)} %bitcast.6, f32[16,256]{1,0:T(8,128)} %bitcast.7, f32[16,256]{1,0:T(8,128)} %bitcast.8, bf16[3,256,8192]{2,1,0:T(8,128)(2,1)} %refs_2_.3), custom_call_target="tpu_custom_call" | custom-call | flops 1024 | bytes 1024 | tf_op jit(solution)/shard_map/packing/pallas_call | solution.py:556
  2.0 3.0 %collective-permute-start.1 = (f32[16,4096]{1,0:T(8,128)S(1)}, f32[16,4096]{1,0:T(8,128)S(1)}, u32[]{:S(2)}, u32[]{:S(2)}) collective-permute-start(f32[16,4096]{1,0:T(8,128)S(1)} %get-tuple-element.65.refs_2_.refs_6_.refs_4_), channel_id=1, source_target_pairs={{0,1},{1,0},{2,3},{3,2},{4,5},{5,4},{6,7},{7,6},{8,9},{9,8},{10,11... | collective-permute-start | bytes 786440 | tf_op jit(solution)/shard_map/ppermute | solution.py:857
  5.0 1.9 %collective-permute-start = (bf16[3,2,8192]{2,1,0:T(2,128)(2,1)S(1)}, bf16[3,2,8192]{2,1,0:T(2,128)(2,1)S(1)}, u32[]{:S(2)}, u32[]{:S(2)}) collective-permute-start(bf16[3,2,8192]{2,1,0:T(2,128)(2,1)S(1)} %get-tuple-element.67), channel_id=1, source_target_pairs={{0,1},{1,2},{2,3},{3,4},{4,5},{5,6},{6,7},{7,8},{8,9},{9,10},{10,1... | collective-permute-start | bytes 294920 | tf_op jit(solution)/shard_map/ppermute | solution.py:853
  6.9 3.4 %placing.1 = (s32[16]{0:T(128)S(1)}, f32[32]{0:T(128)S(1)}, f32[48,128]{1,0:T(8,128)S(1)}, f32[2,256,128]{2,1,0:T(8,128)S(1)}, bf16[2,128,256]{2,1,0:T(8,128)(2,...) custom-call(bf16[3,256,8192]{2,1,0:T(8,128)(2,1)} %refs_2_.3, ...), custom_call_target="tpu_custom_call" | custom-call | flops 1024 | bytes 1024 | tf_op jit(solution)/shard_map/placing/pallas_call | solution.py:583
  10.4 2.1 %lags_own.1 = (f32[256,128]{1,0:T(8,128)S(1)}, bf16[4096,128]{1,0:T(8,128)(2,1)S(1)}, bf16[256,4096]{1,0:T(8,128)(2,1)S(1)}) custom-call(s32[16]{0:T(128)S(1)} %get-tuple-element.61.refs_0_, bf16[3,256,8192]{2,1,0:T(8,128)(2,1)} %refs_2_.3, f32[16,4096]{1,0:T(8,128)S(1)} %get-tuple-element.65.refs_2_.refs_6_.refs_4_), custom_call_target="tpu_custom_call" | custom-call | flops 1024 | bytes 1024 | tf_op jit(solution)/shard_map/lags_own/pallas_call | solution.py:608
  12.5 0.2 collective-permute-done.refs_5_.refs_2_
  12.7 5.9 %block_states_own.1 = (bf16[256,4096]{1,0:T(8,128)(2,1)S(1)}, bf16[256,4096]{1,0:T(8,128)(2,1)S(1)}, bf16[16,4096]{1,0:T(8,128)(2,1)S(1)}, f32[16,4096]{1,0:T(8,...) custom-call(s32[16]{0:T(128)S(1)} %get-tuple-element.61.refs_0_, ...), custom_call_target="tpu_custom_call" | custom-call | flops 20971520 | bytes 16777216 | tf_op jit(solution)/shard_map/block_states_own/pallas_call | solution.py:634
  18.6 2.5 %collective-permute-start.2 = (bf16[16,4096]{1,0:T(8,128)(2,1)S(1)}, bf16[16,4096]{1,0:T(8,128)(2,1)S(1)}, u32[]{:S(2)}, u32[]{:S(2)}) collective-permute-start(bf16[16,4096]{1,0:T(8,128)(2,1)S(1)} %get-tuple-element.82), channel_id=1, source_target_pairs={{0,1},{1,0},{2,3},{3,2},{4,5},{5,4},{6,7},{7,6},{8,9},{9,8},{10,11... | collective-permute-start | bytes 393224 | tf_op jit(solution)/shard_map/ppermute | solution.py:813
  21.1 0.0 collective-permute-done.1.refs_0_.refs_6_.refs_4_
  21.1 1.4 %lags_other.1 = (f32[256,128]{1,0:T(8,128)S(1)}, bf16[4096,128]{1,0:T(8,128)(2,1)S(1)}) custom-call(f32[16,4096]{1,0:T(8,128)S(1)} %collective-permute-done.1.refs_0_.refs_6_.refs_4_), custom_call_target="tpu_custom_call" | custom-call | flops 1024 | bytes 1024 | tf_op jit(solution)/shard_map/lags_other/pallas_call | solution.py:608
  22.5 5.1 %block_states_other.1 = (bf16[256,4096]{1,0:T(8,128)(2,1)S(1)}, bf16[256,4096]{1,0:T(8,128)(2,1)S(1)}, bf16[16,4096]{1,0:T(8,128)(2,1)S(1)}, f32[16,4096]{1,0:T(8,128)S(1)}, f32[16,4096]{1,0:T(8,128)S(1)}) custom-call(s32[16]{0:T(128)S(1)} %get-tuple-element.61.refs_0_, f32[32]{0:T(128)S(1)} %get-tuple-element.63.refs_1_, bf16[3,256,8192]{2,1,0:T(8,128)(2,1)} %refs_2_.3, ...), custom_call_target="tpu_custom_call" | custom-call | flops 20971520 | bytes 16777216 | tf_op jit(solution)/shard_map/block_states_other/pallas_call | solution.py:634
  27.6 0.0 collective-permute-done.2.refs_2_
  27.6 0.2 pairs.1
  27.8 0.1 collective-permute-start.3
  28.0 1.3 %collective-permute-done.3.refs_2_ = bf16[16,4096]{1,0:T(8,128)(2,1)S(1)} collective-permute-done((bf16[16,4096]{1,0:T(8,128)(2,1)S(1)}, bf16[16,4096]{1,0:T(8,128)(2,1)S(1)}, u32[]{:S(2)}, u32[]{:S(2)}) %collective-permute-start.3) | collective-permute-done | bytes 131104 | tf_op jit(solution)/shard_map/ppermute | solution.py:813
  29.3 0.2 quads.1
  29.4 1.6 %collective-permute-start.4 = (bf16[16,4096]{1,0:T(8,128)(2,1)S(1)}, bf16[16,4096]{1,0:T(8,128)(2,1)S(1)}, u32[]{:S(2)}, u32[]{:S(2)}) collective-permute-start(bf16[16,4096]{1,0:T(8,128)(2,1)S(1)} %get-tuple-element.86.refs_10_), channel_id=1, source_target_pairs={{0,4},{1,5},{2,6},{3,7},{4,0},{5,1},{6,2},{7,3},{8,12},{9,13},{10,... | collective-permute-start | bytes 393224 | tf_op jit(solution)/shard_map/ppermute | solution.py:813
  31.0 5.3 %block_local_own0.1 = (f32[256,2048]{1,0:T(8,128)S(1)}, bf16[256,2048]{1,0:T(8,128)(2,1)S(1)}, bf16[256,2048]{1,0:T(8,128)(2,1)S(1)}, f32[8,128]{1,0:T(8,128)S(1)}) custom-call(s32[16]{0:T(128)S(1)} %get-tuple-element.61.refs_0_, bf16[256,4096]{1,0:T(8,128)(2,1)S(1)} %get-tuple-element.71.refs_1_, ...), custom_call_target="tpu_custom_call" | custom-call | flops 1073741824 | bytes 20971520 | tf_op jit(solution)/shard_map/block_local_own0/pallas_call | solution.py:648
  36.3 0.0 collective-permute-done.4.refs_3_
  36.4 0.2 round0.1
  36.6 1.6 %collective-permute-start.5 = (bf16[16,4096]{1,0:T(8,128)(2,1)S(1)}, bf16[16,4096]{1,0:T(8,128)(2,1)S(1)}, u32[]{:S(2)}, u32[]{:S(2)}) collective-permute-start(bf16[16,4096]{1,0:T(8,128)(2,1)S(1)} %get-tuple-element.92.refs_10_), channel_id=1, source_target_pairs={{0,8},{1,9},{2,10},{3,11},{4,12},{5,13},{6,14},{7,15},{8,0},{9,1},... | collective-permute-start | bytes 393224 | tf_op jit(solution)/shard_map/ppermute | solution.py:813
  38.2 5.3 %block_local_own2048.1 = (f32[256,2048]{1,0:T(8,128)S(1)}, bf16[256,2048]{1,0:T(8,128)(2,1)S(1)}, bf16[256,2048]{1,0:T(8,128)(2,1)S(1)}, f32[8,128]{1,0:T(8,128)S(1)}) custom-call(s32[16]{0:T(128)S(1)} %get-tuple-element.61.refs_0_, bf16[256,4096]{1,0:T(8,128)(2,1)S(1)} %get-tuple-element.71.refs_1_, ...), custom_call_target="tpu_custom_call" | custom-call | flops 1073741824 | bytes 20971520 | tf_op jit(solution)/shard_map/block_local_own2048/pallas_call | solution.py:648
  43.6 0.0 collective-permute-done.5.refs_3_
  43.6 0.3 round1.1
  43.8 2.7 %collective-permute-start.6 = (bf16[16,4096]{1,0:T(8,128)(2,1)S(1)}, bf16[16,4096]{1,0:T(8,128)(2,1)S(1)}, u32[]{:S(2)}, u32[]{:S(2)}) collective-permute-start(bf16[16,4096]{1,0:T(8,128)(2,1)S(1)} %get-tuple-element.103.refs_10_), channel_id=1, source_target_pairs={{0,16},{1,17},{2,18},{3,19},{4,20},{5,21},{6,22},{7,23},{8,24},{9,... | collective-permute-start | bytes 393224 | tf_op jit(solution)/shard_map/ppermute | solution.py:813
  46.5 6.4 %block_local_other0.1 = (f32[256,2560]{1,0:T(8,128)S(1)}, bf16[256,2560]{1,0:T(8,128)(2,1)S(1)}, bf16[256,2560]{1,0:T(8,128)(2,1)S(1)}, f32[8,128]{1,0:T(8,128)S(1)}) custom-call(s32[16]{0:T(128)S(1)} %get-tuple-element.61.refs_0_, bf16[256,4096]{1,0:T(8,128)(2,1)S(1)} %get-tuple-element.96.refs_1_, ...), custom_call_target="tpu_custom_call" | custom-call | flops 1342177280 | bytes 26214400 | tf_op jit(solution)/shard_map/block_local_other0/pallas_call | solution.py:648
  52.9 0.0 collective-permute-done.6.refs_3_
  52.9 0.4 round2.1
  53.3 0.1 collective-permute-start.7
  53.4 4.9 %block_local_other2560.1 = (f32[256,1536]{1,0:T(8,128)S(1)}, bf16[256,1536]{1,0:T(8,128)(2,1)S(1)}, bf16[256,1536]{1,0:T(8,128)(2,1)S(1)}, f32[8,128]{1,0:T(8,128)}) custom-call(s32[16]{0:T(128)S(1)} %get-tuple-element.61.refs_0_, bf16[256,4096]{1,0:T(8,128)(2,1)S(1)} %get-tuple-element.96.refs_1_, ...), custom_call_target="tpu_custom_call" | custom-call | flops 805306368 | bytes 15728640 | tf_op jit(solution)/shard_map/block_local_other2560/pallas_call | solution.py:648
  58.2 0.1 collective-permute-done.7.refs_14_
  58.3 4.0 %block_output.1 = bf16[256,8192]{1,0:T(8,128)(2,1)} custom-call(s32[16]{0:T(128)S(1)} %get-tuple-element.61.refs_0_, bf16[256,128]{1,0:T(8,128)(2,1)S(1)} %get-tuple-element.62.refs_1_, f32[256,2048]{1,0:T(8,128)S(1)} %get-tuple-element.87.refs_2_, bf16[256,2048]{1,0:T(8,128)(2,1)S(1)} %get-tuple-element.88.refs_3_, ...), custom_call_target="tpu_custom_call" | custom-call | flops 41943040 | bytes 16777216 | tf_op jit(solution)/shard_map/block_output/pallas_call | solution.py:670
Async XLA Ops:
  2.0 19.1 %collective-permute-start.1 = (f32[16,4096]{1,0:T(8,128)S(1)}, f32[16,4096]{1,0:T(8,128)S(1)}, u32[]{:S(2)}, u32[]{:S(2)}) collective-permute-start(f32[16,4096]{1,0:T(8,128)S(1)} %get-tuple-element.65.refs_2_.refs_6_.refs_4_), channel_id=1, source_target_pairs={{0,1},{1,0},{2,3},{3,2},{4,5},{5,4},{6,7},{7,6},{8,9},{9,8},{10,11... | collective-permute-start | bytes 786440 | tf_op jit(solution)/shard_map/ppermute | solution.py:857
  5.0 7.7 %collective-permute-start = (bf16[3,2,8192]{2,1,0:T(2,128)(2,1)S(1)}, bf16[3,2,8192]{2,1,0:T(2,128)(2,1)S(1)}, u32[]{:S(2)}, u32[]{:S(2)}) collective-permute-start(bf16[3,2,8192]{2,1,0:T(2,128)(2,1)S(1)} %get-tuple-element.67), channel_id=1, source_target_pairs={{0,1},{1,2},{2,3},{3,4},{4,5},{5,6},{6,7},{7,8},{8,9},{9,10},{10,1... | collective-permute-start | bytes 294920 | tf_op jit(solution)/shard_map/ppermute | solution.py:853
  18.6 9.1 %collective-permute-start.2 = (bf16[16,4096]{1,0:T(8,128)(2,1)S(1)}, bf16[16,4096]{1,0:T(8,128)(2,1)S(1)}, u32[]{:S(2)}, u32[]{:S(2)}) collective-permute-start(bf16[16,4096]{1,0:T(8,128)(2,1)S(1)} %get-tuple-element.82), channel_id=1, source_target_pairs={{0,1},{1,0},{2,3},{3,2},{4,5},{5,4},{6,7},{7,6},{8,9},{9,8},{10,11... | collective-permute-start | bytes 393224 | tf_op jit(solution)/shard_map/ppermute | solution.py:813
  27.8 1.4 %collective-permute-start.3 = (bf16[16,4096]{1,0:T(8,128)(2,1)S(1)}, bf16[16,4096]{1,0:T(8,128)(2,1)S(1)}, u32[]{:S(2)}, u32[]{:S(2)}) collective-permute-start(bf16[16,4096]{1,0:T(8,128)(2,1)S(1)} %get-tuple-element.85), channel_id=1, source_target_pairs={{0,2},{1,3},{2,0},{3,1},{4,6},{5,7},{6,4},{7,5},{8,10},{9,11},{10,... | collective-permute-start | bytes 393224 | tf_op jit(solution)/shard_map/ppermute | solution.py:813
  29.4 6.9 %collective-permute-start.4 = (bf16[16,4096]{1,0:T(8,128)(2,1)S(1)}, bf16[16,4096]{1,0:T(8,128)(2,1)S(1)}, u32[]{:S(2)}, u32[]{:S(2)}) collective-permute-start(bf16[16,4096]{1,0:T(8,128)(2,1)S(1)} %get-tuple-element.86.refs_10_), channel_id=1, source_target_pairs={{0,4},{1,5},{2,6},{3,7},{4,0},{5,1},{6,2},{7,3},{8,12},{9,13},{10,... | collective-permute-start | bytes 393224 | tf_op jit(solution)/shard_map/ppermute | solution.py:813
  36.6 7.0 %collective-permute-start.5 = (bf16[16,4096]{1,0:T(8,128)(2,1)S(1)}, bf16[16,4096]{1,0:T(8,128)(2,1)S(1)}, u32[]{:S(2)}, u32[]{:S(2)}) collective-permute-start(bf16[16,4096]{1,0:T(8,128)(2,1)S(1)} %get-tuple-element.92.refs_10_), channel_id=1, source_target_pairs={{0,8},{1,9},{2,10},{3,11},{4,12},{5,13},{6,14},{7,15},{8,0},{9,1},... | collective-permute-start | bytes 393224 | tf_op jit(solution)/shard_map/ppermute | solution.py:813
  43.8 9.1 %collective-permute-start.6 = (bf16[16,4096]{1,0:T(8,128)(2,1)S(1)}, bf16[16,4096]{1,0:T(8,128)(2,1)S(1)}, u32[]{:S(2)}, u32[]{:S(2)}) collective-permute-start(bf16[16,4096]{1,0:T(8,128)(2,1)S(1)} %get-tuple-element.103.refs_10_), channel_id=1, source_target_pairs={{0,16},{1,17},{2,18},{3,19},{4,20},{5,21},{6,22},{7,23},{8,24},{9,... | collective-permute-start | bytes 393224 | tf_op jit(solution)/shard_map/ppermute | solution.py:813
  53.3 5.1 %collective-permute-start.7 = (bf16[16,4096]{1,0:T(8,128)(2,1)S(1)}, bf16[16,4096]{1,0:T(8,128)(2,1)S(1)}, u32[]{:S(2)}, u32[]{:S(2)}) collective-permute-start(bf16[16,4096]{1,0:T(8,128)(2,1)S(1)} %get-tuple-element.112.refs_10_), channel_id=1, source_target_pairs={{0,1},{1,0},{2,3},{3,2},{4,5},{5,4},{6,7},{7,6},{8,9},{9,8},{10,11... | collective-permute-start | bytes 393224 | tf_op jit(solution)/shard_map/ppermute | solution.py:813

commit v5 on v4

--- a/solution.py
+++ b/solution.py
@@ -42,6 +42,8 @@
 
 
 def lanes_at(start, size=LANES):
+    if isinstance(start, int):
+        return slice(start, start + size)
     return pl.ds(pl.multiple_of(start, LANES), size)
 
 
@@ -305,8 +307,8 @@
     held = {}
 
     def bases(tile):
-        at = pl.multiple_of((first + step * WIDE) // GROUP, 8) + tile * TILE_GROUPS
-        taps = taps_ref[pl.ds(pl.multiple_of(at, 8), TILE_GROUPS), :]
+        at = (first + step * WIDE) // GROUP + tile * TILE_GROUPS
+        taps = taps_ref[at : at + TILE_GROUPS, :]
         index = (iota((8, LANES), 1) + (LANES - 1) - iota((8, LANES), 0)) & (LANES - 1)
         rows = [jnp.broadcast_to(taps[group : group + 1], (8, LANES)) for group in range(TILE_GROUPS)]
         early = [jnp.take_along_axis(row, index, axis=1) for row in rows]
@@ -419,12 +421,12 @@
     chunks = channels // WIDE
     weave(lag_jobs(0, first, taps_ref, mats_a))
 
-    @pl.loop(0, chunks // 2)
-    def _(pair):
-        step = pair * 2
-        weave(work(step, mats_a), lag_jobs(step + 1, first, taps_ref, mats_b), query_jobs(step))
-        after = jnp.minimum(step + 2, chunks - 1)
-        weave(work(step + 1, mats_b), lag_jobs(after, first, taps_ref, mats_a), query_jobs(step + 1))
+    buffers = (mats_a, mats_b)
+    for step in range(chunks):
+        ahead = []
+        if step + 1 < chunks:
+            ahead = lag_jobs(step + 1, first, taps_ref, buffers[(step + 1) % 2])
+        weave(work(step, buffers[step % 2]), ahead, query_jobs(step))
 
 
 def output_kernel(place_ref, enter_ref, *refs, pieces, chunk):

time: 62.8 us -> 62.5 us (level)
  Pallas kernels: 47 us -> 46.3 us
    pallas_call x4, Pallas kernels: 21.9 us -> 21.1 us  [block_local(): pl.pallas_call(lambda *refs: local_kernel(*refs, side=side, first=first),...]
  transfers between devices with their start and end apart: 8 -> 8, of which waited for: 3 -> 3; matrix products, arithmetic and copies ran while one was open for 0% -> 0% of each run, Pallas kernels for 64% -> 63%
where the time goes in v5:
time: 62.5 us; the launch traced here: 62.2 us
  Pallas kernels  46.3 us (74%)
  starting transfers between devices  13.6 us (22%)
  waiting for transfers between devices  2.02 us (3%)
    pallas_call x4, Pallas kernels, block_local(): pl.pallas_call(lambda *refs: local_kernel(*refs, side=side, first=first),...  21.1 us
    pallas_call x2, Pallas kernels, block_states(): pl.pallas_call(lambda *refs: state_kernel(*refs, side=side, passing=passi...  11.1 us
    ppermute x6, starting transfers between devices, swap(): return lax.ppermute(array, ('ctx', 'fsdp'), route)  8.63 us
    pallas_call x1, Pallas kernels, block_output(): pl.pallas_call(lambda *refs: output_kernel(*refs, pieces=pieces, chunk=ch...  3.97 us
    pallas_call x2, Pallas kernels, lags(): pl.pallas_call(lambda *refs: lag_kernel(*refs, side=side), in_specs=specs...  3.51 us
    pallas_call x1, Pallas kernels, placing(): pl.pallas_call(lambda *refs: place_kernel(*refs, devices=devices, tokens=...  3.4 us
    ppermute x1, starting transfers between devices, local(): other_pack = lax.ppermute(own_pack, 'fsdp', [(0, 1), (1, 0)])  3.03 us
    pallas_call x1, Pallas kernels, packing(): pl.pallas_call(packing_kernel, in_specs=[HBM] * (len(arrays) + 1), out_sp...  1.98 us
  transfers between devices with their start and end apart: 8, of which 3 were waited for; matrix products, arithmetic and copies ran while one was open for 0% of the time, Pallas kernels for 63%

profile of v5, /device:TPU:0, one launch (start us, length us, event | category | flops | bytes accessed | tf_op | source)
XLA Modules:
  0.0 62.2 jit_solution(9176992718187974756)
XLA Ops:
  0.0 2.0 %packing.1 = (f32[16,4096]{1,0:T(8,128)S(1)}, bf16[3,2,8192]{2,1,0:T(2,128)(2,1)S(1)}) custom-call(f32[3,3,4096]{2,1,0:T(4,128)} %refs_0_.3, f32[1,4096]{1,0:T(1,128)} %bitcast.6, f32[16,256]{1,0:T(8,128)} %bitcast.7, f32[16,256]{1,0:T(8,128)} %bitcast.8, bf16[3,256,8192]{2,1,0:T(8,128)(2,1)} %refs_2_.3), custom_call_target="tpu_custom_call" | custom-call | flops 1024 | bytes 1024 | tf_op jit(solution)/shard_map/packing/pallas_call | solution.py:558
  2.0 3.0 %collective-permute-start.1 = (f32[16,4096]{1,0:T(8,128)S(1)}, f32[16,4096]{1,0:T(8,128)S(1)}, u32[]{:S(2)}, u32[]{:S(2)}) collective-permute-start(f32[16,4096]{1,0:T(8,128)S(1)} %get-tuple-element.65.refs_2_.refs_6_.refs_4_), channel_id=1, source_target_pairs={{0,1},{1,0},{2,3},{3,2},{4,5},{5,4},{6,7},{7,6},{8,9},{9,8},{10,11... | collective-permute-start | bytes 786440 | tf_op jit(solution)/shard_map/ppermute | solution.py:859
  5.0 1.9 %collective-permute-start = (bf16[3,2,8192]{2,1,0:T(2,128)(2,1)S(1)}, bf16[3,2,8192]{2,1,0:T(2,128)(2,1)S(1)}, u32[]{:S(2)}, u32[]{:S(2)}) collective-permute-start(bf16[3,2,8192]{2,1,0:T(2,128)(2,1)S(1)} %get-tuple-element.67), channel_id=1, source_target_pairs={{0,1},{1,2},{2,3},{3,4},{4,5},{5,6},{6,7},{7,8},{8,9},{9,10},{10,1... | collective-permute-start | bytes 294920 | tf_op jit(solution)/shard_map/ppermute | solution.py:855
  6.9 3.4 %placing.1 = (s32[16]{0:T(128)S(1)}, f32[32]{0:T(128)S(1)}, f32[48,128]{1,0:T(8,128)S(1)}, f32[2,256,128]{2,1,0:T(8,128)S(1)}, bf16[2,128,256]{2,1,0:T(8,128)(2,...) custom-call(bf16[3,256,8192]{2,1,0:T(8,128)(2,1)} %refs_2_.3, ...), custom_call_target="tpu_custom_call" | custom-call | flops 1024 | bytes 1024 | tf_op jit(solution)/shard_map/placing/pallas_call | solution.py:585
  10.4 2.1 %lags_own.1 = (f32[256,128]{1,0:T(8,128)S(1)}, bf16[4096,128]{1,0:T(8,128)(2,1)S(1)}, bf16[256,4096]{1,0:T(8,128)(2,1)S(1)}) custom-call(s32[16]{0:T(128)S(1)} %get-tuple-element.61.refs_0_, bf16[3,256,8192]{2,1,0:T(8,128)(2,1)} %refs_2_.3, f32[16,4096]{1,0:T(8,128)S(1)} %get-tuple-element.65.refs_2_.refs_6_.refs_4_), custom_call_target="tpu_custom_call" | custom-call | flops 1024 | bytes 1024 | tf_op jit(solution)/shard_map/lags_own/pallas_call | solution.py:610
  12.5 0.2 collective-permute-done.refs_5_.refs_2_
  12.7 5.9 %block_states_own.1 = (bf16[256,4096]{1,0:T(8,128)(2,1)S(1)}, bf16[256,4096]{1,0:T(8,128)(2,1)S(1)}, bf16[16,4096]{1,0:T(8,128)(2,1)S(1)}, f32[16,4096]{1,0:T(8,...) custom-call(s32[16]{0:T(128)S(1)} %get-tuple-element.61.refs_0_, ...), custom_call_target="tpu_custom_call" | custom-call | flops 20971520 | bytes 16777216 | tf_op jit(solution)/shard_map/block_states_own/pallas_call | solution.py:636
  18.6 2.5 %collective-permute-start.2 = (bf16[16,4096]{1,0:T(8,128)(2,1)S(1)}, bf16[16,4096]{1,0:T(8,128)(2,1)S(1)}, u32[]{:S(2)}, u32[]{:S(2)}) collective-permute-start(bf16[16,4096]{1,0:T(8,128)(2,1)S(1)} %get-tuple-element.82), channel_id=1, source_target_pairs={{0,1},{1,0},{2,3},{3,2},{4,5},{5,4},{6,7},{7,6},{8,9},{9,8},{10,11... | collective-permute-start | bytes 393224 | tf_op jit(solution)/shard_map/ppermute | solution.py:815
  21.1 0.0 collective-permute-done.1.refs_0_.refs_6_.refs_4_
  21.1 1.4 %lags_other.1 = (f32[256,128]{1,0:T(8,128)S(1)}, bf16[4096,128]{1,0:T(8,128)(2,1)S(1)}) custom-call(f32[16,4096]{1,0:T(8,128)S(1)} %collective-permute-done.1.refs_0_.refs_6_.refs_4_), custom_call_target="tpu_custom_call" | custom-call | flops 1024 | bytes 1024 | tf_op jit(solution)/shard_map/lags_other/pallas_call | solution.py:610
  22.5 5.2 %block_states_other.1 = (bf16[256,4096]{1,0:T(8,128)(2,1)S(1)}, bf16[256,4096]{1,0:T(8,128)(2,1)S(1)}, bf16[16,4096]{1,0:T(8,128)(2,1)S(1)}, f32[16,4096]{1,0:T(8,128)S(1)}, f32[16,4096]{1,0:T(8,128)S(1)}) custom-call(s32[16]{0:T(128)S(1)} %get-tuple-element.61.refs_0_, f32[32]{0:T(128)S(1)} %get-tuple-element.63.refs_1_, bf16[3,256,8192]{2,1,0:T(8,128)(2,1)} %refs_2_.3, ...), custom_call_target="tpu_custom_call" | custom-call | flops 20971520 | bytes 16777216 | tf_op jit(solution)/shard_map/block_states_other/pallas_call | solution.py:636
  27.8 0.0 collective-permute-done.2.refs_2_
  27.8 0.2 pairs.1
  28.0 0.1 collective-permute-start.3
  28.1 1.3 %collective-permute-done.3.refs_2_ = bf16[16,4096]{1,0:T(8,128)(2,1)S(1)} collective-permute-done((bf16[16,4096]{1,0:T(8,128)(2,1)S(1)}, bf16[16,4096]{1,0:T(8,128)(2,1)S(1)}, u32[]{:S(2)}, u32[]{:S(2)}) %collective-permute-start.3) | collective-permute-done | bytes 131104 | tf_op jit(solution)/shard_map/ppermute | solution.py:815
  29.4 0.2 quads.1
  29.6 1.6 %collective-permute-start.4 = (bf16[16,4096]{1,0:T(8,128)(2,1)S(1)}, bf16[16,4096]{1,0:T(8,128)(2,1)S(1)}, u32[]{:S(2)}, u32[]{:S(2)}) collective-permute-start(bf16[16,4096]{1,0:T(8,128)(2,1)S(1)} %get-tuple-element.86.refs_10_), channel_id=1, source_target_pairs={{0,4},{1,5},{2,6},{3,7},{4,0},{5,1},{6,2},{7,3},{8,12},{9,13},{10,... | collective-permute-start | bytes 393224 | tf_op jit(solution)/shard_map/ppermute | solution.py:815
  31.2 5.1 %block_local_own0.1 = (f32[256,2048]{1,0:T(8,128)S(1)}, bf16[256,2048]{1,0:T(8,128)(2,1)S(1)}, bf16[256,2048]{1,0:T(8,128)(2,1)S(1)}, f32[8,128]{1,0:T(8,128)S(1)}) custom-call(s32[16]{0:T(128)S(1)} %get-tuple-element.61.refs_0_, bf16[256,4096]{1,0:T(8,128)(2,1)S(1)} %get-tuple-element.71.refs_1_, ...), custom_call_target="tpu_custom_call" | custom-call | flops 1073741824 | bytes 20971520 | tf_op jit(solution)/shard_map/block_local_own0/pallas_call | solution.py:650
  36.3 0.0 collective-permute-done.4.refs_3_
  36.3 0.2 round0.1
  36.5 1.6 %collective-permute-start.5 = (bf16[16,4096]{1,0:T(8,128)(2,1)S(1)}, bf16[16,4096]{1,0:T(8,128)(2,1)S(1)}, u32[]{:S(2)}, u32[]{:S(2)}) collective-permute-start(bf16[16,4096]{1,0:T(8,128)(2,1)S(1)} %get-tuple-element.92.refs_10_), channel_id=1, source_target_pairs={{0,8},{1,9},{2,10},{3,11},{4,12},{5,13},{6,14},{7,15},{8,0},{9,1},... | collective-permute-start | bytes 393224 | tf_op jit(solution)/shard_map/ppermute | solution.py:815
  38.2 5.1 %block_local_own2048.1 = (f32[256,2048]{1,0:T(8,128)S(1)}, bf16[256,2048]{1,0:T(8,128)(2,1)S(1)}, bf16[256,2048]{1,0:T(8,128)(2,1)S(1)}, f32[8,128]{1,0:T(8,128)S(1)}) custom-call(s32[16]{0:T(128)S(1)} %get-tuple-element.61.refs_0_, bf16[256,4096]{1,0:T(8,128)(2,1)S(1)} %get-tuple-element.71.refs_1_, ...), custom_call_target="tpu_custom_call" | custom-call | flops 1073741824 | bytes 20971520 | tf_op jit(solution)/shard_map/block_local_own2048/pallas_call | solution.py:650
  43.3 0.0 collective-permute-done.5.refs_3_
  43.3 0.3 round1.1
  43.6 2.7 %collective-permute-start.6 = (bf16[16,4096]{1,0:T(8,128)(2,1)S(1)}, bf16[16,4096]{1,0:T(8,128)(2,1)S(1)}, u32[]{:S(2)}, u32[]{:S(2)}) collective-permute-start(bf16[16,4096]{1,0:T(8,128)(2,1)S(1)} %get-tuple-element.103.refs_10_), channel_id=1, source_target_pairs={{0,16},{1,17},{2,18},{3,19},{4,20},{5,21},{6,22},{7,23},{8,24},{9,... | collective-permute-start | bytes 393224 | tf_op jit(solution)/shard_map/ppermute | solution.py:815
  46.2 6.4 %block_local_other0.1 = (f32[256,2560]{1,0:T(8,128)S(1)}, bf16[256,2560]{1,0:T(8,128)(2,1)S(1)}, bf16[256,2560]{1,0:T(8,128)(2,1)S(1)}, f32[8,128]{1,0:T(8,128)S(1)}) custom-call(s32[16]{0:T(128)S(1)} %get-tuple-element.61.refs_0_, bf16[256,4096]{1,0:T(8,128)(2,1)S(1)} %get-tuple-element.96.refs_1_, ...), custom_call_target="tpu_custom_call" | custom-call | flops 1342177280 | bytes 26214400 | tf_op jit(solution)/shard_map/block_local_other0/pallas_call | solution.py:650
  52.6 0.0 collective-permute-done.6.refs_3_
  52.6 0.4 round2.1
  53.0 0.1 collective-permute-start.7
  53.0 4.5 %block_local_other2560.1 = (f32[256,1536]{1,0:T(8,128)S(1)}, bf16[256,1536]{1,0:T(8,128)(2,1)S(1)}, bf16[256,1536]{1,0:T(8,128)(2,1)S(1)}, f32[8,128]{1,0:T(8,128)}) custom-call(s32[16]{0:T(128)S(1)} %get-tuple-element.61.refs_0_, bf16[256,4096]{1,0:T(8,128)(2,1)S(1)} %get-tuple-element.96.refs_1_, ...), custom_call_target="tpu_custom_call" | custom-call | flops 805306368 | bytes 15728640 | tf_op jit(solution)/shard_map/block_local_other2560/pallas_call | solution.py:650
  57.5 0.5 collective-permute-done.7.refs_14_
  58.1 4.0 %block_output.1 = bf16[256,8192]{1,0:T(8,128)(2,1)} custom-call(s32[16]{0:T(128)S(1)} %get-tuple-element.61.refs_0_, bf16[256,128]{1,0:T(8,128)(2,1)S(1)} %get-tuple-element.62.refs_1_, f32[256,2048]{1,0:T(8,128)S(1)} %get-tuple-element.87.refs_2_, bf16[256,2048]{1,0:T(8,128)(2,1)S(1)} %get-tuple-element.88.refs_3_, ...), custom_call_target="tpu_custom_call" | custom-call | flops 41943040 | bytes 16777216 | tf_op jit(solution)/shard_map/block_output/pallas_call | solution.py:672
Async XLA Ops:
  2.0 19.1 %collective-permute-start.1 = (f32[16,4096]{1,0:T(8,128)S(1)}, f32[16,4096]{1,0:T(8,128)S(1)}, u32[]{:S(2)}, u32[]{:S(2)}) collective-permute-start(f32[16,4096]{1,0:T(8,128)S(1)} %get-tuple-element.65.refs_2_.refs_6_.refs_4_), channel_id=1, source_target_pairs={{0,1},{1,0},{2,3},{3,2},{4,5},{5,4},{6,7},{7,6},{8,9},{9,8},{10,11... | collective-permute-start | bytes 786440 | tf_op jit(solution)/shard_map/ppermute | solution.py:859
  5.0 7.7 %collective-permute-start = (bf16[3,2,8192]{2,1,0:T(2,128)(2,1)S(1)}, bf16[3,2,8192]{2,1,0:T(2,128)(2,1)S(1)}, u32[]{:S(2)}, u32[]{:S(2)}) collective-permute-start(bf16[3,2,8192]{2,1,0:T(2,128)(2,1)S(1)} %get-tuple-element.67), channel_id=1, source_target_pairs={{0,1},{1,2},{2,3},{3,4},{4,5},{5,6},{6,7},{7,8},{8,9},{9,10},{10,1... | collective-permute-start | bytes 294920 | tf_op jit(solution)/shard_map/ppermute | solution.py:855
  18.6 9.2 %collective-permute-start.2 = (bf16[16,4096]{1,0:T(8,128)(2,1)S(1)}, bf16[16,4096]{1,0:T(8,128)(2,1)S(1)}, u32[]{:S(2)}, u32[]{:S(2)}) collective-permute-start(bf16[16,4096]{1,0:T(8,128)(2,1)S(1)} %get-tuple-element.82), channel_id=1, source_target_pairs={{0,1},{1,0},{2,3},{3,2},{4,5},{5,4},{6,7},{7,6},{8,9},{9,8},{10,11... | collective-permute-start | bytes 393224 | tf_op jit(solution)/shard_map/ppermute | solution.py:815
  28.0 1.4 %collective-permute-start.3 = (bf16[16,4096]{1,0:T(8,128)(2,1)S(1)}, bf16[16,4096]{1,0:T(8,128)(2,1)S(1)}, u32[]{:S(2)}, u32[]{:S(2)}) collective-permute-start(bf16[16,4096]{1,0:T(8,128)(2,1)S(1)} %get-tuple-element.85), channel_id=1, source_target_pairs={{0,2},{1,3},{2,0},{3,1},{4,6},{5,7},{6,4},{7,5},{8,10},{9,11},{10,... | collective-permute-start | bytes 393224 | tf_op jit(solution)/shard_map/ppermute | solution.py:815
  29.6 6.7 %collective-permute-start.4 = (bf16[16,4096]{1,0:T(8,128)(2,1)S(1)}, bf16[16,4096]{1,0:T(8,128)(2,1)S(1)}, u32[]{:S(2)}, u32[]{:S(2)}) collective-permute-start(bf16[16,4096]{1,0:T(8,128)(2,1)S(1)} %get-tuple-element.86.refs_10_), channel_id=1, source_target_pairs={{0,4},{1,5},{2,6},{3,7},{4,0},{5,1},{6,2},{7,3},{8,12},{9,13},{10,... | collective-permute-start | bytes 393224 | tf_op jit(solution)/shard_map/ppermute | solution.py:815
  36.5 6.8 %collective-permute-start.5 = (bf16[16,4096]{1,0:T(8,128)(2,1)S(1)}, bf16[16,4096]{1,0:T(8,128)(2,1)S(1)}, u32[]{:S(2)}, u32[]{:S(2)}) collective-permute-start(bf16[16,4096]{1,0:T(8,128)(2,1)S(1)} %get-tuple-element.92.refs_10_), channel_id=1, source_target_pairs={{0,8},{1,9},{2,10},{3,11},{4,12},{5,13},{6,14},{7,15},{8,0},{9,1},... | collective-permute-start | bytes 393224 | tf_op jit(solution)/shard_map/ppermute | solution.py:815
  43.6 9.0 %collective-permute-start.6 = (bf16[16,4096]{1,0:T(8,128)(2,1)S(1)}, bf16[16,4096]{1,0:T(8,128)(2,1)S(1)}, u32[]{:S(2)}, u32[]{:S(2)}) collective-permute-start(bf16[16,4096]{1,0:T(8,128)(2,1)S(1)} %get-tuple-element.103.refs_10_), channel_id=1, source_target_pairs={{0,16},{1,17},{2,18},{3,19},{4,20},{5,21},{6,22},{7,23},{8,24},{9,... | collective-permute-start | bytes 393224 | tf_op jit(solution)/shard_map/ppermute | solution.py:815
  53.0 5.1 %collective-permute-start.7 = (bf16[16,4096]{1,0:T(8,128)(2,1)S(1)}, bf16[16,4096]{1,0:T(8,128)(2,1)S(1)}, u32[]{:S(2)}, u32[]{:S(2)}) collective-permute-start(bf16[16,4096]{1,0:T(8,128)(2,1)S(1)} %get-tuple-element.112.refs_10_), channel_id=1, source_target_pairs={{0,1},{1,0},{2,3},{3,2},{4,5},{5,4},{6,7},{7,6},{8,9},{9,8},{10,11... | collective-permute-start | bytes 393224 | tf_op jit(solution)/shard_map/ppermute | solution.py:815
